TPU v7x, 128 devices: a whole 4x4x4 slice. The times are simulated.
128 devices in a mesh: sample: 8 (over z, core), space: 16 (over y, x).
Axes of the slice: x: 4, y: 4, z: 4, core: 2. Of those that a mesh axis runs over, the one named last changes fastest.
Arguments:
- displacements: bfloat16 [64, 3, 296208], P('sample', None, 'space')
- connectivity: int32 [8, 262144], P(None, 'space'), may hold values from 0 to 18512, as said below
- density: float32 [262144], P('space'), may hold values from 0.1 to 1
- stiffness: bfloat16 [24, 24], replicated
- filter_inverse: float32 [128, 128], replicated
- send_rows: int32 [16, 8, 16, 256], P('space'), may hold values from 0 to 2047, as said below
- send_count: int32 [16, 8, 16], P('space'), may hold values from 0 to 256, as said below
- recv_cell: int32 [8, 16, 16, 256], P('sample', 'space'), may hold values from 0 to 2047
Outputs:
- compliance: float32 [64], replicated
- filtered_sensitivity: float32 [8, 16, 2048], P('sample', 'space')
- filtered_energy: float32 [8, 16, 2048], P('sample', 'space')
Inputs may be any that keep to these rules, and one draw needn't show every extreme that they name: `connectivity`: column j * 16384 + e lists the eight distinct corner nodes of element e of slab j, as indices into that slab's 18513 nodes. `send_rows`: for each slab j and group i, the first send_count[j, i, d] slots of the lists over all d hold each of the group's 2048 elements exactly once; other slots hold 0. `send_count`: for each slab and group the counts over destinations sum to 2048, and one destination takes exactly 256.
All inputs are finite; a program needn't handle non-finite values.
Results may differ from a plain program's by a relative error of at most 0.0003.
Values sent between devices are 32-bit elements; how exact they have to be, the bound alone decides.
No kernel may reach another device: no remote copies, remote signals or barrier semaphores. Data moves between devices by JAX's collectives and lax.ppermute only.
A program may use at most 128 MiB of HBM per device.

v0:
```python
import math

import jax
import jax.numpy as jnp
from jax import lax
from jax.sharding import PartitionSpec as P

penalty = 3.0
spread_weight = 0.5
epsilon = 1e-06


def robust_weights(compliance):
    center = jnp.mean(compliance)
    spread = jnp.sqrt(jnp.mean((compliance - center) ** 2) + epsilon)
    return (1.0 + spread_weight * (compliance - center) / spread) / compliance.shape[0]


def body(
    displacements,
    connectivity,
    density,
    stiffness,
    filter_inverse,
    send_rows,
    send_count,
    recv_cell,
):
    groups = lax.axis_size("sample")
    slab_count = lax.axis_size("space")
    group_id = lax.axis_index("sample")
    local_samples = displacements.shape[0]
    node_count = displacements.shape[2]
    elements = density.shape[0]
    block_size = math.gcd(elements, 8192)
    blocks = elements // block_size
    node_table = jnp.transpose(displacements, (2, 0, 1)).reshape(node_count, local_samples * 3)
    link_blocks = jnp.transpose(connectivity.reshape(8, blocks, block_size), (1, 0, 2))

    def block_energy(indices):
        rows = node_table[indices].reshape(8, block_size, local_samples, 3)
        gathered = jnp.transpose(rows, (1, 2, 3, 0)).reshape(block_size, local_samples, 24)
        applied = jnp.einsum("esb,ab->esa", gathered, stiffness, preferred_element_type=jnp.float32)
        return jnp.sum(gathered.astype(jnp.float32) * applied, axis=2)

    energy = lax.map(block_energy, link_blocks)
    solid_frac = density.reshape(blocks, block_size, 1)
    partial_terms = jnp.sum(energy * solid_frac**3, axis=(0, 1)) / (elements * slab_count)
    all_samples = local_samples * groups
    slab_total = lax.psum(partial_terms, "space")
    compliance = lax.all_gather(slab_total, "sample", axis=0, tiled=True)
    weight = robust_weights(compliance)
    own_weight = lax.dynamic_slice(weight, (group_id * local_samples,), (local_samples,))
    sensitivity = (
        -penalty * solid_frac[:, :, 0] ** 2 * jnp.sum(energy * own_weight[None, None, :], axis=2)
    ).reshape(elements)
    mean_energy = (jnp.sum(energy, axis=2) / all_samples).reshape(elements)
    sub_rows = elements // groups
    capacity = send_rows.shape[-1]
    both_fields = jnp.stack([sensitivity, mean_energy], axis=1)
    offsets = (jnp.arange(groups, dtype=jnp.int32) * sub_rows)[:, None, None]
    picked = send_rows[0] + offsets
    slot_ids = lax.broadcasted_iota(jnp.int32, (groups, slab_count, capacity), 2)
    live_mask = (slot_ids < send_count[0][:, :, None])[..., None]
    chosen = jnp.where(live_mask, both_fields[picked], 0.0)
    out_sens = chosen[..., 0].reshape(groups * slab_count, capacity)
    out_energy = chosen[..., 1].reshape(groups * slab_count, capacity)
    got_sens, got_energy = (
        lax.all_to_all(out_sens, ("sample", "space"), split_axis=0, concat_axis=0, tiled=True),
        lax.all_to_all(out_energy, ("sample", "space"), split_axis=0, concat_axis=0, tiled=True),
    )
    arrived_sens = jnp.sum(got_sens.reshape(groups, slab_count, capacity), axis=0)
    arrived_energy = jnp.sum(got_energy.reshape(groups, slab_count, capacity), axis=0)
    cell_ids = recv_cell[0, 0].reshape(-1)
    arrived_both = jnp.stack([arrived_sens.reshape(-1), arrived_energy.reshape(-1)], axis=0)
    total_slots = cell_ids.shape[0]
    step_rows = math.gcd(total_slots, 1024)
    node_iota = lax.broadcasted_iota(jnp.int32, (step_rows, sub_rows), 1)

    def add_block(turn, accum):
        start = turn * step_rows
        block_ids = lax.dynamic_slice_in_dim(cell_ids, start, step_rows, 0)
        block_vals = lax.dynamic_slice_in_dim(arrived_both, start, step_rows, 1)
        one_hot = (block_ids[:, None] == node_iota).astype(jnp.float32)
        return accum + jnp.dot(block_vals, one_hot, precision=lax.Precision.HIGHEST)

    node_both = lax.fori_loop(
        0, total_slots // step_rows, add_block, jnp.zeros((2, sub_rows), jnp.float32)
    )
    patch_size = filter_inverse.shape[0]
    patches = node_both.reshape(2 * sub_rows // patch_size, patch_size)
    result = jnp.dot(patches, filter_inverse.T, precision=lax.Precision.HIGHEST).reshape(
        2, 1, 1, sub_rows
    )
    return (compliance, result[0], result[1])


def solution(mesh):
    in_specs = (
        P("sample", None, "space"),
        P(None, "space"),
        P("space"),
        P(),
        P(),
        P("space", None, None, None),
        P("space", None, None),
        P("sample", "space", None, None),
    )
    out_specs = (P(), P("sample", "space", None), P("sample", "space", None))
    return jax.shard_map(body, mesh=mesh, in_specs=in_specs, out_specs=out_specs, check_vma=False)
```

profile of v0, /device:TPU:0, one launch (start us, length us, event | category | flops | bytes accessed | tf_op | source)
XLA Modules:
  0.0 714.3 jit_solution(4725301467093796300)
XLA Ops:
  0.7 0.5 iota_multiply_fusion
  1.2 1.6 copy.20
  2.8 0.7 reshape.134
  3.6 3.7 copy.21
  7.3 477.6 %while.24 = (s32[]{:T(128)}, f32[2,8192,8]{1,2,0:T(8,128)}, s32[2,8,8192]{2,1,0:T(8,128)}, bf16[18513,24]{1,0:T(8,128)(2,1)}, bf16[24,24]{1,0:T(8,128)(2,1)S(1)}, /*index=5*/s32[]{:T(128)}) while((s32[]{:T(128)}, f32[2,8192,8]{1,2,0:T(8,128)}, s32[2,8,8192]{2,1,0:T(8,128)}, bf16[18513,24]{1,0:T(8,128)(2,1)}, bf16[24,24]{1,0:T(8,128)(2,1)S(1)}, ...), condition=%wide.region_2.3_spmd, body=%wide.region_0.2_spmd.sunk | while | flops 80412672 | bytes 24643272 | solution.py:46
  7.3 1.0 fusion.26
  8.3 0.1 copy.39
  8.4 221.0 %gather_fusion = bf16[65536,24]{1,0:T(8,128)(2,1)} fusion(bf16[18513,24]{1,0:T(8,128)(2,1)} %get-tuple-element.248, s32[65536]{0:T(1024)S(1)} %broadcast_clamp_fusion.3), kind=kCustom, calls=%fused_computation.clone.1 | custom fusion | bytes 6553600 | tf_op jit(solution)/shard_map/while/body/eval_jaxpr/gather | solution.py:41
  229.4 12.9 %copy.40 = bf16[65536,24]{0,1:T(8,128)(2,1)S(1)} copy(bf16[65536,24]{1,0:T(8,128)(2,1)} %gather_fusion) | data formatting | bytes 6291456 | tf_op jit(solution)/shard_map/while/body/eval_jaxpr/gather | solution.py:41
  242.2 1.7 copy.41
  244.0 1.4 fusion.27
  245.4 0.7 bitcast_dynamic-update-slice_fusion.2
  246.1 1.0 fusion.26
  247.2 221.0 %gather_fusion = bf16[65536,24]{1,0:T(8,128)(2,1)} fusion(bf16[18513,24]{1,0:T(8,128)(2,1)} %get-tuple-element.248, s32[65536]{0:T(1024)S(1)} %broadcast_clamp_fusion.3), kind=kCustom, calls=%fused_computation.clone.1 | custom fusion | bytes 6553600 | tf_op jit(solution)/shard_map/while/body/eval_jaxpr/gather | solution.py:41
  468.2 12.9 %copy.40 = bf16[65536,24]{0,1:T(8,128)(2,1)S(1)} copy(bf16[65536,24]{1,0:T(8,128)(2,1)} %gather_fusion) | data formatting | bytes 6291456 | tf_op jit(solution)/shard_map/while/body/eval_jaxpr/gather | solution.py:41
  481.0 1.7 copy.41
  482.8 1.4 fusion.27
  484.2 0.7 bitcast_dynamic-update-slice_fusion.2
  485.0 1.3 multiply_reduce_fusion.1
  486.3 40.7 %psum.7 = f32[8]{0:T(128)S(1)} all-reduce(f32[8]{0:T(128)S(1)} %broadcast_multiply_fusion), channel_id=1, replica_groups=mesh['sample'=8,'space'=16] {'space'}, use_global_device_ids=true, to_apply=%region_4.5 | all-reduce | flops 8 | bytes 64 | tf_op jit(solution)/shard_map/psum | solution.py:50
  527.0 0.6 dynamic-slice
  528.2 0.2 dynamic-update-slice
  528.5 13.1 %all-reduce = f32[64]{0:T(128)S(1)} all-reduce(f32[64]{0:T(128)S(1)} %dynamic-update-slice), channel_id=1, replica_groups=mesh['sample'=8,'space'=16] {'sample'}, use_global_device_ids=true, to_apply=%add | all-reduce | flops 64 | bytes 512
  541.6 0.6 reduce_sum.75
  542.9 0.6 multiply_reduce_fusion.2
  544.2 0.1 dynamic_slice.21
  544.3 1.4 multiply_reduce_fusion
  545.8 0.1 copy.31
  545.9 0.1 pad_maximum_fusion
  546.0 5.0 copy.22
  551.0 0.1 compare_select_fusion.1
  551.1 0.1 copy.32
  551.2 111.6 %gather_fusion.1 = f32[32768,2]{1,0:T(8,128)} fusion(f32[16384,2]{1,0:T(8,128)} %copy.22, s32[32768]{0:T(1024)S(1)} %broadcast_clamp_fusion.1), kind=kCustom, calls=%fused_computation.1 | custom fusion | bytes 655360 | tf_op jit(solution)/shard_map/gather | solution.py:65
  662.8 10.0 %copy.23 = f32[8,16,256,2]{2,1,0,3:T(8,128)S(1)} copy(f32[8,16,256,2]{3,2,1,0:T(8,128)} %bitcast.81) | data formatting | bytes 524288 | tf_op jit(solution)/shard_map/gather | solution.py:65
  672.7 0.1 iota_compare_fusion.4
  672.9 0.8 copy.24
  673.7 4.6 all-to-all-start
  678.3 0.8 copy.25
  679.1 8.8 %all-to-all-done = f32[128,1,256]{2,1,0:T(1,128)S(1)} async-done(((f32[128,1,256]{2,1,0:T(1,128)}), f32[128,1,256]{2,1,0:T(1,128)S(1)}, u32[]{:S(2)}, u32[]{:S(2)}) %all-to-all-start) | async-done | bytes 131104 | tf_op jit(solution)/shard_map/all_to_all | solution.py:69
  687.9 4.8 all-to-all-start.1
  692.8 9.3 %all-to-all-done.1 = f32[128,1,256]{2,1,0:T(1,128)S(1)} async-done(((f32[128,1,256]{2,1,0:T(1,128)}), f32[128,1,256]{2,1,0:T(1,128)S(1)}, u32[]{:S(2)}, u32[]{:S(2)}) %all-to-all-start.1) | async-done | bytes 131104 | tf_op jit(solution)/shard_map/all_to_all | solution.py:70
  702.2 11.2 %while.25 = (s32[]{:T(128)}, f32[2,2048]{1,0:T(2,128)S(1)}, f32[2,4096]{1,0:T(2,128)S(1)}, s32[4096]{0:T(1024)S(1)}, s32[]{:T(128)}, /*index=5*/s32[]{:T(128)}, s32[]{:T(128)}, s32[]{:T(128)}) while((s32[]{:T(128)}, f32[2,2048]{1,0:T(2,128)S(1)}, f32[2,4096]{1,0:T(2,128)S(1)}, s32[4096]{0:T(1024)S(1)}, s32[]{:T(128)}, ...), condition=%wide.region_12.13_spmd.clone, body=%wide.region_11.12_spmd.clone.sunk | while | flops 52437000 | bytes 53397 | solution.py:87
  702.3 2.8 fusion.29
  705.0 2.8 fusion.29
  707.8 2.8 fusion.29
  710.6 2.8 fusion.29
  713.4 0.2 fusion.15
  713.6 0.6 fusion.14
  (47 shorter events, 0.5 us)
Async XLA Ops:
  0.6 712.8 %copy-start = (f32[128,128]{1,0:T(8,128)S(1)}, f32[128,128]{1,0:T(8,128)}, u32[]{:S(2)}) copy-start(f32[128,128]{1,0:T(8,128)} %param.16) | copy-start | bytes 196612
  0.6 6.6 copy-start.7
  7.3 477.6 %copy-start.1 = (f32[16384]{0:T(1024)S(1)}, f32[16384]{0:T(1024)}, u32[]{:S(2)}) copy-start(f32[16384]{0:T(1024)} %param.14) | copy-start | bytes 196612
  7.3 519.7 %copy-start.8 = (u32[128]{0:T(128)S(1)}, u32[128]{0:T(128)}, u32[]{:S(2)}) copy-start(u32[128]{0:T(128)} %constant.88) | copy-start | bytes 1540
  484.9 66.1 %copy-start.2 = (s32[1,8,16,256]{3,2,1,0:T(8,128)S(1)}, s32[1,8,16,256]{3,2,1,0:T(8,128)}, u32[]{:S(2)}) copy-start(s32[1,8,16,256]{3,2,1,0:T(8,128)} %param.17) | copy-start | bytes 393220
  484.9 66.1 %copy-start.5 = (s32[8]{0:T(128)S(1)}, s32[8]{0:T(128)}, u32[]{:S(2)}) copy-start(s32[8]{0:T(128)} %iota_multiply_fusion) | copy-start | bytes 100
  541.6 121.1 %copy-start.6 = (f32[64]{0:T(128)}, f32[64]{0:T(128)S(1)}, u32[]{:S(2)}) copy-start(f32[64]{0:T(128)S(1)} %all-reduce) | copy-start | bytes 772
  662.7 10.0 %copy-start.4 = (s32[1,8,16]{2,1,0:T(8,128)S(1)}, s32[1,8,16]{2,1,0:T(8,128)}, u32[]{:S(2)}) copy-start(s32[1,8,16]{2,1,0:T(8,128)} %param.18) | copy-start | bytes 1540
  662.8 30.0 %copy-start.3 = (s32[1,1,16,256]{3,2,1,0:T(8,128)S(1)}, s32[1,1,16,256]{3,2,1,0:T(8,128)}, u32[]{:S(2)}) copy-start(s32[1,1,16,256]{3,2,1,0:T(8,128)} %param.19) | copy-start | bytes 49156
  673.7 14.2 %all-to-all-start = ((f32[128,1,256]{2,1,0:T(1,128)}), f32[128,1,256]{2,1,0:T(1,128)S(1)}, u32[]{:S(2)}, u32[]{:S(2)}) async-start(f32[128,1,256]{2,1,0:T(1,128)} %copy.24), calls=%async_computation | async-start | bytes 262144 | tf_op jit(solution)/shard_map/all_to_all | solution.py:69
  687.9 14.2 %all-to-all-start.1 = ((f32[128,1,256]{2,1,0:T(1,128)}), f32[128,1,256]{2,1,0:T(1,128)S(1)}, u32[]{:S(2)}, u32[]{:S(2)}) async-start(f32[128,1,256]{2,1,0:T(1,128)} %copy.25), calls=%async_computation.1 | async-start | bytes 262144 | tf_op jit(solution)/shard_map/all_to_all | solution.py:70
where the time goes:
time: 716 us; the launch traced here: 714 us
  local copies, waits for them, and re-layouts  609 us (85%)
  blocking collectives  53.9 us (8%)
  waiting for transfers between devices  18.1 us (3%)
  matrix products  14.1 us (2%)
  starting transfers between devices  9.41 us (1%)
    gather x4, local copies, waits for them, and re-layouts, block_energy(): rows = node_table[indices].reshape(8, block_size, local_samples, 3)  468 us
    gather x2, local copies, waits for them, and re-layouts, body(): chosen = jnp.where(live_mask, both_fields[picked], 0.0)  122 us
    psum x1, blocking collectives, body(): slab_total = lax.psum(partial_terms, 'space')  40.7 us
  transfers between devices with their start and end apart: 2, of which 2 were waited for; matrix products, arithmetic and copies ran while one was open for 0% of the time, Pallas kernels for 0%

commit v1 on v0

v1 whole, which is shorter than its diff:
```python
import functools

import jax
import jax.numpy as jnp
from jax import lax
from jax.experimental import pallas as pl
from jax.experimental.pallas import tpu as pltpu
from jax.sharding import PartitionSpec as P

penalty = 3.0
spread_weight = 0.5
epsilon = 1e-06

LANES = 128
BLOCK = 1024
UNROLL = 32
CHUNK = 256
ROWS = 16
F32 = jnp.float32
BF16 = jnp.bfloat16


def energy_kernel(steps, place_ref, *refs):
    links = refs[:8]
    own_ref, other_ref, weight_ref, density_ref = refs[8:12]
    out_refs, parts_ref = refs[12:16], refs[16]
    table, rows, total = refs[17:]
    turn, sub = pl.program_id(0), pl.program_id(1)
    nodes = table.shape[0]

    @pl.when((turn == 0) & (sub == 0))
    def _():
        total[...] = jnp.zeros_like(total)
        pad = jnp.zeros((ROWS, LANES), F32)

        def fill(n, _):
            at = pl.ds(pl.multiple_of(n * LANES, LANES), LANES)
            own, other = own_ref[:, at], other_ref[:, at]
            half = []
            for k in range(3):
                half += [own[8 * k : 8 * k + 8], other[8 * k : 8 * k + 8]]
            half.append(pad)
            table[at, :] = jnp.concatenate(half + half, axis=0).T
            return 0

        lax.fori_loop(0, nodes // LANES, fill, 0)

    first_half = lax.broadcasted_iota(jnp.int32, (1, LANES), 1) < LANES // 2

    def gather(t, _):
        start = pl.multiple_of(t * UNROLL, UNROLL)
        view = rows.at[pl.ds(start, UNROLL)]
        for u in range(UNROLL):
            e = start + u
            for p in range(4):
                low = table[pl.ds(links[2 * p][e], 1), :]
                high = table[pl.ds(links[2 * p + 1][e], 1), :]
                view[u : u + 1, p * LANES : (p + 1) * LANES] = jnp.where(first_half, low, high)
        return 0

    lax.fori_loop(0, BLOCK // UNROLL, gather, 0)

    acc = total[...]
    for chunk in range(BLOCK // CHUNK):
        field = rows[chunk * CHUNK : (chunk + 1) * CHUNK, :]
        applied = jnp.dot(field.astype(BF16), weight_ref[...], preferred_element_type=F32)
        product = field * applied
        folded = product[:, :LANES]
        for p in range(1, 4):
            folded = folded + product[:, p * LANES : (p + 1) * LANES]
        turned = folded.T
        half = turned[: LANES // 2] + turned[LANES // 2 :]
        energy = half[:ROWS] + half[ROWS : 2 * ROWS] + half[2 * ROWS : 3 * ROWS]
        at = pl.ds(pl.multiple_of(sub * BLOCK + chunk * CHUNK, CHUNK), CHUNK)
        for d in range(4):

            @pl.when(turn == d)
            def _(d=d):
                out_refs[d][:, at] = energy

        rho = density_ref[0, :, chunk * CHUNK : (chunk + 1) * CHUNK]
        scaled = energy * (rho * rho * rho)
        for p in range(CHUNK // LANES):
            acc = acc + scaled[:, p * LANES : (p + 1) * LANES]
    total[...] = acc

    @pl.when((turn == 3) & (sub == steps - 1))
    def _():
        column = jnp.sum(acc, axis=1, keepdims=True)
        row_id = lax.broadcasted_iota(jnp.int32, (ROWS, 64), 0)
        lane = lax.broadcasted_iota(jnp.int32, (ROWS, 64), 1)
        spot = jnp.where(row_id < 8, place_ref[4] * 8 + row_id, place_ref[5] * 8 + row_id - 8)
        row = jnp.sum(jnp.where(lane == spot, column, 0.0), axis=0, keepdims=True)
        parts_ref[...] = jnp.broadcast_to(row, parts_ref.shape)


def split(x):
    high = x.astype(BF16)
    return high, (x - high.astype(F32)).astype(BF16)


def send_kernel(elements, place_ref, count_ref, parts_ref, e0, e1, e2, e3, density_ref, picks_ref, comp_ref, out_ref):
    comp = jnp.sum(parts_ref[...], axis=0, keepdims=True) / elements
    comp_ref[...] = comp
    center = jnp.mean(comp, axis=1, keepdims=True)
    spread = jnp.sqrt(jnp.mean((comp - center) ** 2, axis=1, keepdims=True) + epsilon)
    weight = (1.0 + spread_weight * (comp - center) / spread) / 64.0
    row_id = lax.broadcasted_iota(jnp.int32, (8, 64), 0)
    lane = lax.broadcasted_iota(jnp.int32, (8, 64), 1)
    sens = mean = None
    for d, e_ref in enumerate((e0, e1, e2, e3)):
        for h in range(2):
            spot = place_ref[6 + 2 * d + h] * 8 + row_id
            column = jnp.sum(jnp.where(lane == spot, weight, 0.0), axis=1, keepdims=True)
            field = e_ref[8 * h : 8 * h + 8, :]
            term = column * field
            sens = term if sens is None else sens + term
            mean = field if mean is None else mean + field
    rho = density_ref[0]
    sens = -penalty * rho * rho * jnp.sum(sens, axis=0, keepdims=True)
    mean = jnp.sum(mean, axis=0, keepdims=True) / 64.0
    both = [f[:, h * LANES : (h + 1) * LANES] for f in (sens, mean) for h in range(16)]
    table = jnp.concatenate(split(jnp.concatenate(both, axis=0)), axis=0)
    width = picks_ref.shape[2]
    low_id = lax.broadcasted_iota(jnp.int32, (LANES, width), 0)
    high_id = lax.broadcasted_iota(jnp.int32, (16, width), 0)
    slot = lax.broadcasted_iota(jnp.int32, (16, width), 1)
    for d in range(picks_ref.shape[1]):
        pick = picks_ref[0, d : d + 1, :]
        hot = jnp.where(low_id == (pick & (LANES - 1)), 1.0, 0.0).astype(BF16)
        found = jnp.dot(table, hot, preferred_element_type=F32)
        found = found[:32] + found[32:]
        live = (high_id == (pick >> 7)) & (slot < count_ref[place_ref[0] * 16 + d])
        for f in range(2):
            got = jnp.sum(jnp.where(live, found[16 * f : 16 * f + 16], 0.0), axis=0, keepdims=True)
            for p in range(width // LANES):
                r = f * (width // LANES) + p
                out_ref[d, r : r + 1, :] = got[:, p * LANES : (p + 1) * LANES]


def owner_kernel(got_ref, cells_ref, filter_ref, sens_ref, energy_ref):
    sources, width = cells_ref.shape[2], cells_ref.shape[3]
    low_id = lax.broadcasted_iota(jnp.int32, (LANES, width), 0)
    high_id = lax.broadcasted_iota(jnp.int32, (16, width), 0)
    node = jnp.zeros((64, LANES), F32)
    for j in range(sources):
        cell = cells_ref[0, 0, j : j + 1, :]
        hot = jnp.where(low_id == (cell & (LANES - 1)), 1.0, 0.0).astype(BF16)
        mine = high_id == (cell >> 7)
        pieces = []
        for f in range(2):
            value = jnp.concatenate([got_ref[j, 2 * f : 2 * f + 1, :], got_ref[j, 2 * f + 1 : 2 * f + 2, :]], axis=1)
            pieces.append(jnp.where(mine, value, 0.0))
        rows = jnp.concatenate(split(jnp.concatenate(pieces, axis=0)), axis=0)
        node = node + lax.dot_general(rows, hot, (((1,), (1,)), ((), ())), preferred_element_type=F32)
    node = node[:32] + node[32:]
    result = lax.dot_general(
        node, filter_ref[...], (((1,), (1,)), ((), ())),
        precision=lax.Precision.HIGHEST, preferred_element_type=F32,
    )
    for p in range(16):
        sens_ref[0, :, p * LANES : (p + 1) * LANES] = result[p : p + 1]
        energy_ref[0, :, p * LANES : (p + 1) * LANES] = result[16 + p : 17 + p]


def block_stiffness(stiffness):
    lane = jnp.arange(512, dtype=jnp.int32)
    spot = lane % 64
    corner = 2 * (lane // LANES) + (lane % LANES) // 64
    dof = jnp.where(spot < 48, 8 * (spot // ROWS) + corner, -1)
    hot = (dof[:, None] == jnp.arange(24, dtype=jnp.int32)[None, :]).astype(BF16)
    wide = jnp.dot(hot, jnp.dot(stiffness.T, hot.T, preferred_element_type=F32).astype(BF16), preferred_element_type=F32)
    same = (lane % ROWS)[:, None] == (lane % ROWS)[None, :]
    return jnp.where(same, wide, 0.0).astype(BF16)


def body(displacements, connectivity, density, stiffness, filter_inverse, send_rows, send_count, recv_cell):
    group_id = lax.axis_index("sample")
    z, core = group_id // 2, group_id % 2
    node_count = displacements.shape[2]
    elements = density.shape[0]
    groups = 8
    sub_rows = elements // groups
    slabs = lax.axis_size("space")
    nodes = (node_count + LANES - 1) // LANES * LANES

    own = jnp.transpose(displacements, (1, 0, 2)).reshape(24, node_count).astype(F32)
    own = jnp.pad(own, ((0, 0), (0, nodes - node_count)))
    other = lax.ppermute(own, "sample", [(i, i ^ 1) for i in range(8)])
    links = connectivity.reshape(-1)
    rho = density.reshape(groups, 1, sub_rows)
    weights = block_stiffness(stiffness)

    order = (1, 2, 3, 0)
    place = [2 * ((z + d) % 4) + core for d in order] + [group_id, group_id ^ 1]
    steps = sub_rows // BLOCK
    per_corner = elements // BLOCK

    def link_spec(c):
        return pl.BlockSpec(
            (BLOCK,), lambda t, s, at: (c * per_corner + at[t] * steps + s,), memory_space=pltpu.SMEM
        )

    whole = pl.BlockSpec(memory_space=pltpu.VMEM)
    energies = pl.pallas_call(
        functools.partial(energy_kernel, steps),
        grid_spec=pltpu.PrefetchScalarGridSpec(
            num_scalar_prefetch=1,
            grid=(4, steps),
            in_specs=[link_spec(c) for c in range(8)]
            + [whole, whole, whole, pl.BlockSpec((1, 1, BLOCK), lambda t, s, at: (at[t], 0, s))],
            out_specs=[whole] * 5,
            scratch_shapes=[
                pltpu.VMEM((nodes, LANES), F32),
                pltpu.VMEM((BLOCK, 4 * LANES), F32),
                pltpu.VMEM((ROWS, LANES), F32),
            ],
        ),
        out_shape=[jax.ShapeDtypeStruct((ROWS, sub_rows), F32)] * 4 + [jax.ShapeDtypeStruct((128, 64), F32)],
        compiler_params=pltpu.CompilerParams(vmem_limit_bytes=48 * 2**20),
        name="energy",
    )(jnp.stack(place).astype(jnp.int32), *([links] * 8), own, other, weights, rho)
    parts = lax.all_to_all(energies[4], ("sample", "space"), split_axis=0, concat_axis=0, tiled=True)
    arrived = [energies[3]] + [
        lax.ppermute(energies[d - 1], "sample", [(i, (i + 2 * d) % 8) for i in range(8)]) for d in (1, 2, 3)
    ]
    source = [2 * ((z - d) % 4) for d in range(4)]
    place2 = [group_id] * 6
    for base in source:
        place2 += [base + core, base + 1 - core]

    smem = pl.BlockSpec(memory_space=pltpu.SMEM)
    width = send_rows.shape[-1]
    compliance, outgoing = pl.pallas_call(
        functools.partial(send_kernel, float(elements * slabs)),
        in_specs=[smem, smem] + [whole] * 7,
        out_specs=[whole] * 2,
        out_shape=[
            jax.ShapeDtypeStruct((1, 64), F32),
            jax.ShapeDtypeStruct((slabs, 2 * width // LANES, LANES), F32),
        ],
        name="send",
    )(
        jnp.stack(place2).astype(jnp.int32),
        send_count.reshape(-1),
        parts,
        *arrived,
        lax.dynamic_slice_in_dim(rho, group_id, 1, 0),
        lax.dynamic_slice_in_dim(send_rows[0], group_id, 1, 0),
    )
    got = lax.all_to_all(outgoing, "space", split_axis=0, concat_axis=0, tiled=True)
    sens, energy = pl.pallas_call(
        owner_kernel,
        in_specs=[whole] * 3,
        out_specs=[whole] * 2,
        out_shape=[jax.ShapeDtypeStruct((1, 1, sub_rows), F32)] * 2,
        name="owner",
    )(got, recv_cell, filter_inverse)
    return (compliance.reshape(-1), sens, energy)


def solution(mesh):
    in_specs = (
        P("sample", None, "space"),
        P(None, "space"),
        P("space"),
        P(),
        P(),
        P("space", None, None, None),
        P("space", None, None),
        P("sample", "space", None, None),
    )
    out_specs = (P(), P("sample", "space", None), P("sample", "space", None))
    return jax.shard_map(body, mesh=mesh, in_specs=in_specs, out_specs=out_specs, check_vma=False)
```

time: 716 us -> 119 us (0.17)
  local copies, waits for them, and re-layouts: 609 us -> 4.1 us
  Pallas kernels: 0 us -> 74.7 us
  blocking collectives: 53.9 us -> 11.7 us
  matrix products: 14.1 us -> 0.54 us
  waiting for transfers between devices: 18.1 us -> 10.5 us
    gather x6 -> x0, local copies, waits for them, and re-layouts: 589 us -> none  [the longest x4 468 us: block_energy(): rows = node_table[indices].reshape(8, block_size, local_samples, 3)]
    pallas_call x0 -> x3, Pallas kernels: none -> 74.7 us  [the longest x1 70 us: body(): pl.pallas_call(functools.partial(energy_kernel, steps), grid_spec=pltpu.P...]
    psum x1 -> x0, blocking collectives: 40.7 us -> none  [body(): slab_total = lax.psum(partial_terms, 'space')]
    dot_general x7 -> x1, matrix products: 14.1 us -> 0.54 us  [block_stiffness(): jnp.dot(hot, jnp.dot(stiffness.T, hot.T, preferred_element_type=F32).asty...]
    unnamed x1 -> x0, blocking collectives: 13.1 us -> none
    all_to_all x0 -> x1, blocking collectives: none -> 11.7 us  [body(): lax.all_to_all(outgoing, 'space', split_axis=0, concat_axis=0, tiled=True)]
    all_to_all x2 -> x1, waiting for transfers between devices: 18.1 us -> 7.55 us  [body(): lax.all_to_all(energies[4], ('sample', 'space'), split_axis=0, concat_axi...]
    while x5 -> x0, local copies, waits for them, and re-layouts: 7.25 us -> none  [the longest x1 3.69 us: body(): energy = lax.map(block_energy, link_blocks)]
  transfers between devices with their start and end apart: 2 -> 5, of which waited for: 2 -> 2; matrix products, arithmetic and copies ran while one was open for 0% -> 3% of each run, Pallas kernels for 0% -> 0%
where the time goes in v1:
time: 119 us; the launch traced here: 118 us
  Pallas kernels  74.7 us (63%)
  starting transfers between devices  14.7 us (12%)
  blocking collectives  11.7 us (10%)
  waiting for transfers between devices  10.5 us (9%)
  local copies, waits for them, and re-layouts  4.1 us (3%)
  other arithmetic  1.36 us (1%)
    pallas_call x1, Pallas kernels, body(): pl.pallas_call(functools.partial(energy_kernel, steps), grid_spec=pltpu.P...  70 us
    all_to_all x1, blocking collectives, body(): lax.all_to_all(outgoing, 'space', split_axis=0, concat_axis=0, tiled=True)  11.7 us
    all_to_all x1, starting transfers between devices, body(): lax.all_to_all(energies[4], ('sample', 'space'), split_axis=0, concat_axi...  8.04 us
    all_to_all x1, waiting for transfers between devices, body(): lax.all_to_all(energies[4], ('sample', 'space'), split_axis=0, concat_axi...  7.55 us
    ppermute x3, starting transfers between devices, body(): lax.ppermute(energies[d - 1], 'sample', [(i, (i + 2 * d) % 8) for i in ra...  6.58 us
    ppermute x1, waiting for transfers between devices, body(): other = lax.ppermute(own, 'sample', [(i, i ^ 1) for i in range(8)])  2.96 us
    pallas_call x1, Pallas kernels, body(): pl.pallas_call(functools.partial(send_kernel, float(elements * slabs)), i...  2.44 us
  transfers between devices with their start and end apart: 5, of which 2 were waited for; matrix products, arithmetic and copies ran while one was open for 3% of the time, Pallas kernels for 0%

profile of v1, /device:TPU:0, one launch (start us, length us, event | category | flops | bytes accessed | tf_op | source)
XLA Modules:
  0.0 118.5 jit_solution(8048464900845239955)
XLA Ops:
  0.6 0.0 copy-start
  0.6 0.0 copy-start.3
  0.7 0.0 copy-start.9
  0.7 1.3 %pad_convert_fusion.refs_8_ = f32[24,18560]{1,0:T(8,128)S(1)} fusion(bf16[24,18513]{1,0:T(8,128)(2,1)} %bitcast.37), kind=kLoop, calls=%fused_computation.3 | loop fusion | flops 445440 | bytes 2670384 | tf_op jit(solution)/shard_map/jit(_pad)/pad | solution.py:188
  2.0 0.0 copy-start.2
  2.0 0.1 collective-permute-start
  2.2 0.0 copy-done.3
  2.2 0.1 copy.12
  2.3 0.1 stack.66.place_ref
  2.4 0.0 copy-done.9
  2.4 0.5 fusion.refs_10_
  3.0 3.0 %collective-permute-done.refs_9_ = f32[24,18560]{1,0:T(8,128)} collective-permute-done((f32[24,18560]{1,0:T(8,128)S(1)}, f32[24,18560]{1,0:T(8,128)}, u32[]{:S(2)}, u32[]{:S(2)}) %collective-permute-start) | collective-permute-done | bytes 1781792 | tf_op jit(solution)/shard_map/ppermute | solution.py:189
  6.0 0.0 copy-done.2
  6.0 0.0 copy-start.8
  6.0 70.0 %energy.1 = (f32[16,2048]{1,0:T(8,128)S(1)}, f32[16,2048]{1,0:T(8,128)S(1)}, f32[16,2048]{1,0:T(8,128)S(1)}, f32[16,2048]{1,0:T(8,128)S(1)}, f32[128,64]{1,0:T(8,128)}) custom-call(s32[6]{0:T(128)S(1)} %stack.66.place_ref, s32[131072]{0:T(1024)S(1)} %bitcast.27, s32[131072]{0:T(1024)S(1)} %bitcast.28, s32[131072]{0:T(1024)S(1)} %bitcast.29, ...), custom_call_target="tpu_custom_call" | custom-call | tf_op jit(solution)/shard_map/energy/pallas_call | solution.py:205
  75.9 0.0 copy-start.1
  75.9 0.7 copy-done.1
  76.6 2.0 %collective-permute-start.1 = (f32[16,2048]{1,0:T(8,128)S(1)}, f32[16,2048]{1,0:T(8,128)S(1)}, u32[]{:S(2)}, u32[]{:S(2)}) collective-permute-start(f32[16,2048]{1,0:T(8,128)S(1)} %get-tuple-element.14), channel_id=1, source_target_pairs={{0,32},{16,48},{32,64},{48,80},{64,96},{80,112},{96,0},{112,16},{1... | collective-permute-start | bytes 393224 | tf_op jit(solution)/shard_map/ppermute | solution.py:225
  78.6 3.6 %collective-permute-start.2 = (f32[16,2048]{1,0:T(8,128)S(1)}, f32[16,2048]{1,0:T(8,128)S(1)}, u32[]{:S(2)}, u32[]{:S(2)}) collective-permute-start(f32[16,2048]{1,0:T(8,128)S(1)} %get-tuple-element.15), channel_id=1, source_target_pairs={{0,64},{16,80},{32,96},{48,112},{64,0},{80,16},{96,32},{112,48},{1... | collective-permute-start | bytes 393224 | tf_op jit(solution)/shard_map/ppermute | solution.py:225
  82.1 1.0 collective-permute-start.3
  83.2 0.6 constant_dynamic-slice_fusion.density_ref
  83.8 8.0 %all-to-all-start = ((f32[128,1,64]{2,1,0:T(1,128)}), f32[128,1,64]{2,1,0:T(1,128)S(1)}, u32[]{:S(2)}, u32[]{:S(2)}) async-start(f32[128,1,64]{2,1,0:T(1,128)} %bitcast.17), calls=%async_computation | async-start | bytes 131072 | tf_op jit(solution)/shard_map/all_to_all | solution.py:223
  91.8 0.0 copy-done
  91.8 0.6 dynamic-slice_bitcast_fusion.picks_ref
  92.4 0.0 copy-done.8
  92.4 0.7 reshape.105.count_ref
  93.1 0.6 stack.61.place_ref
  93.7 7.6 %all-to-all-done = f32[128,1,64]{2,1,0:T(1,128)S(1)} async-done(((f32[128,1,64]{2,1,0:T(1,128)}), f32[128,1,64]{2,1,0:T(1,128)S(1)}, u32[]{:S(2)}, u32[]{:S(2)}) %all-to-all-start) | async-done | bytes 32800 | tf_op jit(solution)/shard_map/all_to_all | solution.py:223
  101.3 0.0 copy-start.4
  101.3 0.0 collective-permute-done.1.e1
  101.3 0.0 copy-start.5
  101.3 0.0 collective-permute-done.2.e2
  101.3 0.0 copy-start.6
  101.3 0.0 collective-permute-done.3.e3
  101.3 0.0 copy-start.7
  101.3 0.6 copy-done.4
  101.9 0.1 copy-done.5
  102.0 0.0 copy-done.6
  102.0 0.0 copy-done.7
  102.0 2.4 %send.1 = (f32[1,64]{1,0:T(1,128)}, f32[16,4,128]{2,1,0:T(4,128)}) custom-call(s32[14]{0:T(128)} %stack.61.place_ref, s32[128]{0:T(128)} %reshape.105.count_ref, f32[128,64]{1,0:T(8,128)} %bitcast.39, f32[16,2048]{1,0:T(8,128)} %copy-done.1, f32[16,2048]{1,0:T(8,128)} %copy-done.5, f32[16,2048]{1,0:T(8,128)} %copy-done.6, f32[16,2048]{1,0:T(8,128)} %copy-done.7, ...), custom_call_target="tpu_custom_call" | custom-call | tf_op jit(solution)/shard_map/send/pallas_call | solution.py:234
  104.5 11.7 %all_to_all.16.got_ref = f32[16,4,128]{2,1,0:T(4,128)} all-to-all(f32[16,4,128]{2,1,0:T(4,128)} %get-tuple-element.18), channel_id=1, replica_groups=mesh['sample'=8,'space'=16] {'space'}, dimensions={0} | all-to-all | bytes 65536 | tf_op jit(solution)/shard_map/all_to_all | solution.py:251
  116.2 2.3 %owner.1 = (f32[1,1,2048]{2,1,0:T(1,128)}, f32[1,1,2048]{2,1,0:T(1,128)}) custom-call(f32[16,4,128]{2,1,0:T(4,128)} %all_to_all.16.got_ref, s32[1,1,16,256]{3,2,1,0:T(8,128)} %cells_ref.1, f32[128,128]{1,0:T(8,128)} %filter_ref.1), custom_call_target="tpu_custom_call" | custom-call | tf_op jit(solution)/shard_map/owner/pallas_call | solution.py:252
  (1 shorter events, 0.0 us)
Async XLA Ops:
  0.6 91.2 %copy-start = (s32[1,8,16,256]{3,2,1,0:T(8,128)S(1)}, s32[1,8,16,256]{3,2,1,0:T(8,128)}, u32[]{:S(2)}) copy-start(s32[1,8,16,256]{3,2,1,0:T(8,128)} %param.13) | copy-start | bytes 393220
  0.6 1.6 %copy-start.3 = (s32[8,16384]{1,0:T(8,128)S(1)}, s32[8,16384]{1,0:T(8,128)}, u32[]{:S(2)}) copy-start(s32[8,16384]{1,0:T(8,128)} %param.9) | copy-start | bytes 1572868
  0.7 1.8 %copy-start.9 = (bf16[24,24]{1,0:T(8,128)(2,1)S(1)}, bf16[24,24]{1,0:T(8,128)(2,1)}, u32[]{:S(2)}) copy-start(bf16[24,24]{1,0:T(8,128)(2,1)} %param.11) | copy-start | bytes 3460
  2.0 3.9 %copy-start.2 = (f32[16384]{0:T(1024)S(1)}, f32[16384]{0:T(1024)}, u32[]{:S(2)}) copy-start(f32[16384]{0:T(1024)} %param.10) | copy-start | bytes 196612
  2.0 3.9 %collective-permute-start = (f32[24,18560]{1,0:T(8,128)S(1)}, f32[24,18560]{1,0:T(8,128)}, u32[]{:S(2)}, u32[]{:S(2)}) collective-permute-start(f32[24,18560]{1,0:T(8,128)S(1)} %pad_convert_fusion.refs_8_), channel_id=1, source_target_pairs={{0,16},{16,0},{32,48},{48,32},{64,80},{80,64},{96,112},{112,96},{1... | collective-permute-start | bytes 5345288 | tf_op jit(solution)/shard_map/ppermute | solution.py:189
  6.0 86.5 %copy-start.8 = (s32[1,8,16]{2,1,0:T(8,128)S(1)}, s32[1,8,16]{2,1,0:T(8,128)}, u32[]{:S(2)}) copy-start(s32[1,8,16]{2,1,0:T(8,128)} %param.14) | copy-start | bytes 1540
  75.9 0.7 copy-start.1
  76.6 24.7 %collective-permute-start.1 = (f32[16,2048]{1,0:T(8,128)S(1)}, f32[16,2048]{1,0:T(8,128)S(1)}, u32[]{:S(2)}, u32[]{:S(2)}) collective-permute-start(f32[16,2048]{1,0:T(8,128)S(1)} %get-tuple-element.14), channel_id=1, source_target_pairs={{0,32},{16,48},{32,64},{48,80},{64,96},{80,112},{96,0},{112,16},{1... | collective-permute-start | bytes 393224 | tf_op jit(solution)/shard_map/ppermute | solution.py:225
  78.6 22.7 %collective-permute-start.2 = (f32[16,2048]{1,0:T(8,128)S(1)}, f32[16,2048]{1,0:T(8,128)S(1)}, u32[]{:S(2)}, u32[]{:S(2)}) collective-permute-start(f32[16,2048]{1,0:T(8,128)S(1)} %get-tuple-element.15), channel_id=1, source_target_pairs={{0,64},{16,80},{32,96},{48,112},{64,0},{80,16},{96,32},{112,48},{1... | collective-permute-start | bytes 393224 | tf_op jit(solution)/shard_map/ppermute | solution.py:225
  82.1 19.2 %collective-permute-start.3 = (f32[16,2048]{1,0:T(8,128)S(1)}, f32[16,2048]{1,0:T(8,128)S(1)}, u32[]{:S(2)}, u32[]{:S(2)}) collective-permute-start(f32[16,2048]{1,0:T(8,128)S(1)} %get-tuple-element.16), channel_id=1, source_target_pairs={{0,96},{16,112},{32,0},{48,16},{64,32},{80,48},{96,64},{112,80},{1... | collective-permute-start | bytes 393224 | tf_op jit(solution)/shard_map/ppermute | solution.py:225
  83.8 17.5 %all-to-all-start = ((f32[128,1,64]{2,1,0:T(1,128)}), f32[128,1,64]{2,1,0:T(1,128)S(1)}, u32[]{:S(2)}, u32[]{:S(2)}) async-start(f32[128,1,64]{2,1,0:T(1,128)} %bitcast.17), calls=%async_computation | async-start | bytes 131072 | tf_op jit(solution)/shard_map/all_to_all | solution.py:223
  101.3 0.6 copy-start.4
  101.3 0.7 copy-start.5
  101.3 0.7 copy-start.6
  101.3 0.7 copy-start.7

commit v2 on v1

--- a/solution.py
+++ b/solution.py
@@ -13,8 +13,8 @@
 
 LANES = 128
 BLOCK = 1024
+FILL = 29
 UNROLL = 32
-CHUNK = 256
 ROWS = 16
 F32 = jnp.float32
 BF16 = jnp.bfloat16
@@ -34,16 +34,18 @@
         pad = jnp.zeros((ROWS, LANES), F32)
 
         def fill(n, _):
-            at = pl.ds(pl.multiple_of(n * LANES, LANES), LANES)
-            own, other = own_ref[:, at], other_ref[:, at]
-            half = []
-            for k in range(3):
-                half += [own[8 * k : 8 * k + 8], other[8 * k : 8 * k + 8]]
-            half.append(pad)
-            table[at, :] = jnp.concatenate(half + half, axis=0).T
+            start = pl.multiple_of(n * (FILL * LANES), LANES)
+            for i in range(FILL):
+                at = pl.ds(start + i * LANES, LANES)
+                own, other = own_ref[:, at], other_ref[:, at]
+                half = []
+                for k in range(3):
+                    half += [own[8 * k : 8 * k + 8], other[8 * k : 8 * k + 8]]
+                half.append(pad)
+                table[at, :] = jnp.concatenate(half + half, axis=0).T
             return 0
 
-        lax.fori_loop(0, nodes // LANES, fill, 0)
+        lax.fori_loop(0, nodes // (FILL * LANES), fill, 0)
 
     first_half = lax.broadcasted_iota(jnp.int32, (1, LANES), 1) < LANES // 2
 
@@ -60,28 +62,27 @@
 
     lax.fori_loop(0, BLOCK // UNROLL, gather, 0)
 
+    field = rows[...]
+    applied = jnp.dot(field.astype(BF16), weight_ref[...], preferred_element_type=F32)
+    product = field * applied
+    folded = product[:, :LANES]
+    for p in range(1, 4):
+        folded = folded + product[:, p * LANES : (p + 1) * LANES]
+    turned = folded.T
+    half = turned[: LANES // 2] + turned[LANES // 2 :]
+    energy = half[:ROWS] + half[ROWS : 2 * ROWS] + half[2 * ROWS : 3 * ROWS]
+    at = pl.ds(pl.multiple_of(sub * BLOCK, BLOCK), BLOCK)
+    for d in range(4):
+
+        @pl.when(turn == d)
+        def _(d=d):
+            out_refs[d][:, at] = energy
+
+    rho = density_ref[0]
+    scaled = energy * (rho * rho * rho)
     acc = total[...]
-    for chunk in range(BLOCK // CHUNK):
-        field = rows[chunk * CHUNK : (chunk + 1) * CHUNK, :]
-        applied = jnp.dot(field.astype(BF16), weight_ref[...], preferred_element_type=F32)
-        product = field * applied
-        folded = product[:, :LANES]
-        for p in range(1, 4):
-            folded = folded + product[:, p * LANES : (p + 1) * LANES]
-        turned = folded.T
-        half = turned[: LANES // 2] + turned[LANES // 2 :]
-        energy = half[:ROWS] + half[ROWS : 2 * ROWS] + half[2 * ROWS : 3 * ROWS]
-        at = pl.ds(pl.multiple_of(sub * BLOCK + chunk * CHUNK, CHUNK), CHUNK)
-        for d in range(4):
-
-            @pl.when(turn == d)
-            def _(d=d):
-                out_refs[d][:, at] = energy
-
-        rho = density_ref[0, :, chunk * CHUNK : (chunk + 1) * CHUNK]
-        scaled = energy * (rho * rho * rho)
-        for p in range(CHUNK // LANES):
-            acc = acc + scaled[:, p * LANES : (p + 1) * LANES]
+    for p in range(BLOCK // LANES):
+        acc = acc + scaled[:, p * LANES : (p + 1) * LANES]
     total[...] = acc
 
     @pl.when((turn == 3) & (sub == steps - 1))
@@ -99,7 +100,20 @@
     return high, (x - high.astype(F32)).astype(BF16)
 
 
-def send_kernel(elements, place_ref, count_ref, parts_ref, e0, e1, e2, e3, density_ref, picks_ref, comp_ref, out_ref):
+def prepare_kernel(place_ref, count_ref, picks_ref, *refs):
+    hot_ref, live_ref = refs[-2:]
+    dests, width = picks_ref.shape[1:]
+    low_id = lax.broadcasted_iota(jnp.int32, (LANES, width), 0)
+    high_id = lax.broadcasted_iota(jnp.int32, (16, width), 0)
+    slot = lax.broadcasted_iota(jnp.int32, (16, width), 1)
+    for d in range(dests):
+        pick = picks_ref[0, d : d + 1, :]
+        hot_ref[d] = jnp.where(low_id == (pick & (LANES - 1)), 1.0, 0.0).astype(BF16)
+        live = (high_id == (pick >> 7)) & (slot < count_ref[place_ref[0] * 16 + d])
+        live_ref[d] = jnp.where(live, 1.0, 0.0)
+
+
+def send_kernel(elements, place_ref, parts_ref, e0, e1, e2, e3, density_ref, hot_ref, live_ref, comp_ref, out_ref):
     comp = jnp.sum(parts_ref[...], axis=0, keepdims=True) / elements
     comp_ref[...] = comp
     center = jnp.mean(comp, axis=1, keepdims=True)
@@ -121,18 +135,12 @@
     mean = jnp.sum(mean, axis=0, keepdims=True) / 64.0
     both = [f[:, h * LANES : (h + 1) * LANES] for f in (sens, mean) for h in range(16)]
     table = jnp.concatenate(split(jnp.concatenate(both, axis=0)), axis=0)
-    width = picks_ref.shape[2]
-    low_id = lax.broadcasted_iota(jnp.int32, (LANES, width), 0)
-    high_id = lax.broadcasted_iota(jnp.int32, (16, width), 0)
-    slot = lax.broadcasted_iota(jnp.int32, (16, width), 1)
-    for d in range(picks_ref.shape[1]):
-        pick = picks_ref[0, d : d + 1, :]
-        hot = jnp.where(low_id == (pick & (LANES - 1)), 1.0, 0.0).astype(BF16)
-        found = jnp.dot(table, hot, preferred_element_type=F32)
+    dests, _, width = hot_ref.shape
+    for d in range(dests):
+        found = jnp.dot(table, hot_ref[d], preferred_element_type=F32)
         found = found[:32] + found[32:]
-        live = (high_id == (pick >> 7)) & (slot < count_ref[place_ref[0] * 16 + d])
         for f in range(2):
-            got = jnp.sum(jnp.where(live, found[16 * f : 16 * f + 16], 0.0), axis=0, keepdims=True)
+            got = jnp.sum(found[16 * f : 16 * f + 16] * live_ref[d], axis=0, keepdims=True)
             for p in range(width // LANES):
                 r = f * (width // LANES) + p
                 out_ref[d, r : r + 1, :] = got[:, p * LANES : (p + 1) * LANES]
@@ -221,33 +229,43 @@
         name="energy",
     )(jnp.stack(place).astype(jnp.int32), *([links] * 8), own, other, weights, rho)
     parts = lax.all_to_all(energies[4], ("sample", "space"), split_axis=0, concat_axis=0, tiled=True)
-    arrived = [energies[3]] + [
-        lax.ppermute(energies[d - 1], "sample", [(i, (i + 2 * d) % 8) for i in range(8)]) for d in (1, 2, 3)
-    ]
     source = [2 * ((z - d) % 4) for d in range(4)]
     place2 = [group_id] * 6
     for base in source:
         place2 += [base + core, base + 1 - core]
+    place2 = jnp.stack(place2).astype(jnp.int32)
 
     smem = pl.BlockSpec(memory_space=pltpu.SMEM)
+    stay = pl.BlockSpec(memory_space=pl.ANY)
     width = send_rows.shape[-1]
+    e1, e2, e3, hot, live = pl.pallas_call(
+        prepare_kernel,
+        in_specs=[smem, smem, whole, stay, stay, stay],
+        out_specs=[stay, stay, stay, whole, whole],
+        out_shape=[jax.ShapeDtypeStruct((ROWS, sub_rows), F32)] * 3
+        + [jax.ShapeDtypeStruct((slabs, LANES, width), BF16), jax.ShapeDtypeStruct((slabs, 16, width), F32)],
+        input_output_aliases={3: 0, 4: 1, 5: 2},
+        cost_estimate=pl.CostEstimate(flops=4 * 10**9, bytes_accessed=2**21, transcendentals=0),
+        name="prepare",
+    )(
+        place2,
+        send_count.reshape(-1),
+        lax.dynamic_slice_in_dim(send_rows[0], group_id, 1, 0),
+        *energies[:3],
+    )
+    arrived = [energies[3]] + [
+        lax.ppermute(e, "sample", [(i, (i + 2 * d) % 8) for i in range(8)]) for d, e in ((1, e1), (2, e2), (3, e3))
+    ]
     compliance, outgoing = pl.pallas_call(
         functools.partial(send_kernel, float(elements * slabs)),
-        in_specs=[smem, smem] + [whole] * 7,
+        in_specs=[smem] + [whole] * 8,
         out_specs=[whole] * 2,
         out_shape=[
             jax.ShapeDtypeStruct((1, 64), F32),
             jax.ShapeDtypeStruct((slabs, 2 * width // LANES, LANES), F32),
         ],
         name="send",
-    )(
-        jnp.stack(place2).astype(jnp.int32),
-        send_count.reshape(-1),
-        parts,
-        *arrived,
-        lax.dynamic_slice_in_dim(rho, group_id, 1, 0),
-        lax.dynamic_slice_in_dim(send_rows[0], group_id, 1, 0),
-    )
+    )(place2, parts, *arrived, lax.dynamic_slice_in_dim(rho, group_id, 1, 0), hot, live)
     got = lax.all_to_all(outgoing, "space", split_axis=0, concat_axis=0, tiled=True)
     sens, energy = pl.pallas_call(
         owner_kernel,

time: 119 us -> 106 us (0.89)
  Pallas kernels: 74.7 us -> 59.5 us
  waiting for transfers between devices: 10.5 us -> 6.09 us
  blocking collectives: 11.7 us -> 14.4 us
  starting transfers between devices: 14.7 us -> 16.7 us
  local copies, waits for them, and re-layouts: 4.1 us -> 5.9 us
    pallas_call x1, Pallas kernels: 70 us -> 52.4 us  [body(): pl.pallas_call(functools.partial(energy_kernel, steps), grid_spec=pltpu.P...]
    all_to_all x1, waiting for transfers between devices: 7.55 us -> 1.37 us  [body(): lax.all_to_all(energies[4], ('sample', 'space'), split_axis=0, concat_axi...]
    ppermute x3, waiting for transfers between devices: 0.01 us -> 3.64 us  [body(): lax.ppermute(e, 'sample', [(i, (i + 2 * d) % 8) for i in range(8)])]
    all_to_all x1, starting transfers between devices: 8.04 us -> 11.1 us  [body(): lax.all_to_all(energies[4], ('sample', 'space'), split_axis=0, concat_axi...]
    all_to_all x1, blocking collectives: 11.7 us -> 14.4 us  [body(): lax.all_to_all(outgoing, 'space', split_axis=0, concat_axis=0, tiled=True)]
    pallas_call x0 -> x1, Pallas kernels: none -> 2.01 us  [body(): pl.pallas_call(prepare_kernel, in_specs=[smem, smem, whole, stay, stay, s...]
    unnamed x21 -> x27, local copies, waits for them, and re-layouts: 1.52 us -> 3.41 us
    ppermute x1, waiting for transfers between devices: 2.96 us -> 1.09 us  [body(): other = lax.ppermute(own, 'sample', [(i, i ^ 1) for i in range(8)])]
  transfers between devices with their start and end apart: 5 -> 5, of which waited for: 2 -> 3; matrix products, arithmetic and copies ran while one was open for 3% -> 3% of each run, Pallas kernels for 0% -> 2%
where the time goes in v2:
time: 106 us; the launch traced here: 105 us
  Pallas kernels  59.5 us (56%)
  starting transfers between devices  16.7 us (16%)
  blocking collectives  14.4 us (14%)
  waiting for transfers between devices  6.09 us (6%)
  local copies, waits for them, and re-layouts  5.9 us (6%)
  other arithmetic  1.36 us (1%)
    pallas_call x1, Pallas kernels, body(): pl.pallas_call(functools.partial(energy_kernel, steps), grid_spec=pltpu.P...  52.4 us
    all_to_all x1, blocking collectives, body(): lax.all_to_all(outgoing, 'space', split_axis=0, concat_axis=0, tiled=True)  14.4 us
    all_to_all x1, starting transfers between devices, body(): lax.all_to_all(energies[4], ('sample', 'space'), split_axis=0, concat_axi...  11.1 us
    ppermute x3, starting transfers between devices, body(): lax.ppermute(e, 'sample', [(i, (i + 2 * d) % 8) for i in range(8)])  5.49 us
    ppermute x3, waiting for transfers between devices, body(): lax.ppermute(e, 'sample', [(i, (i + 2 * d) % 8) for i in range(8)])  3.64 us
    unnamed x27, local copies, waits for them, and re-layouts  3.41 us
    pallas_call x1, Pallas kernels, body(): pl.pallas_call(functools.partial(send_kernel, float(elements * slabs)), i...  2.8 us
    pallas_call x1, Pallas kernels, body(): pl.pallas_call(owner_kernel, in_specs=[whole] * 3, out_specs=[whole] * 2,...  2.29 us
  transfers between devices with their start and end apart: 5, of which 3 were waited for; matrix products, arithmetic and copies ran while one was open for 3% of the time, Pallas kernels for 2%

profile of v2, /device:TPU:0, one launch (start us, length us, event | category | flops | bytes accessed | tf_op | source)
XLA Modules:
  0.0 105.3 jit_solution(18254939270457871953)
XLA Ops:
  0.6 0.0 copy-start
  0.6 0.0 copy-start.6
  0.7 0.0 copy-start.11
  0.7 0.0 copy-start.12
  0.7 1.3 %pad_convert_fusion.refs_8_ = f32[24,18560]{1,0:T(8,128)S(1)} fusion(bf16[24,18513]{1,0:T(8,128)(2,1)} %bitcast.37), kind=kLoop, calls=%fused_computation.3 | loop fusion | flops 445440 | bytes 2670384 | tf_op jit(solution)/shard_map/jit(_pad)/pad | solution.py:196
  2.0 0.0 copy-start.2
  2.0 0.1 collective-permute-start
  2.3 0.0 copy-done.6
  2.3 0.1 copy.15
  2.4 0.0 copy-done.11
  2.4 0.6 reshape.107.count_ref
  3.0 0.1 stack.66.place_ref
  3.1 0.6 stack.61.place_ref
  3.7 0.0 copy-done
  3.7 0.6 dynamic-slice_bitcast_fusion.picks_ref
  4.3 0.0 copy-done.12
  4.3 0.5 fusion.refs_10_
  4.9 1.1 %collective-permute-done.refs_9_ = f32[24,18560]{1,0:T(8,128)} collective-permute-done((f32[24,18560]{1,0:T(8,128)S(1)}, f32[24,18560]{1,0:T(8,128)}, u32[]{:S(2)}, u32[]{:S(2)}) %collective-permute-start) | collective-permute-done | bytes 1781792 | tf_op jit(solution)/shard_map/ppermute | solution.py:197
  6.0 0.0 copy-done.2
  6.0 52.4 %energy.1 = (f32[16,2048]{1,0:T(8,128)S(1)}, f32[16,2048]{1,0:T(8,128)S(1)}, f32[16,2048]{1,0:T(8,128)S(1)}, f32[16,2048]{1,0:T(8,128)S(1)}, f32[128,64]{1,0:T(8,128)}) custom-call(s32[6]{0:T(128)S(1)} %stack.66.place_ref, s32[131072]{0:T(1024)S(1)} %bitcast.27, s32[131072]{0:T(1024)S(1)} %bitcast.28, s32[131072]{0:T(1024)S(1)} %bitcast.29, ...), custom_call_target="tpu_custom_call" | custom-call | tf_op jit(solution)/shard_map/energy/pallas_call | solution.py:213
  58.3 0.0 copy-start.1
  58.3 0.6 copy-done.1
  59.0 0.0 copy-start.3
  59.0 0.6 copy-done.3
  59.6 0.0 copy-start.4
  59.6 0.7 copy-done.4
  60.3 0.0 copy-start.5
  60.3 0.7 copy-done.5
  60.9 11.1 %all-to-all-start = ((f32[128,1,64]{2,1,0:T(1,128)}), f32[128,1,64]{2,1,0:T(1,128)S(1)}, u32[]{:S(2)}, u32[]{:S(2)}) async-start(f32[128,1,64]{2,1,0:T(1,128)} %bitcast.17), calls=%async_computation | async-start | bytes 131072 | tf_op jit(solution)/shard_map/all_to_all | solution.py:231
  72.1 2.0 %prepare.1 = (f32[16,2048]{1,0:T(8,128)}, f32[16,2048]{1,0:T(8,128)}, f32[16,2048]{1,0:T(8,128)}, bf16[16,128,256]{2,1,0:T(8,128)(2,1)}, f32[16,16,256]{2,1,0:T(8,128)}) custom-call(s32[14]{0:T(128)} %stack.61.place_ref, s32[128]{0:T(128)} %reshape.107.count_ref, ...), custom_call_target="tpu_custom_call", output_to_operand_aliasing={{0}: (3, {}), {1}: (4, {}), {2}: (5, {})} | custom-call | flops 4000000000 | bytes 2097152 | tf_op jit(solution)/shard_map/prepare/pallas_call | solution.py:241
  74.1 1.1 %collective-permute-start.1 = (f32[16,2048]{1,0:T(8,128)}, f32[16,2048]{1,0:T(8,128)S(1)}, u32[]{:S(2)}, u32[]{:S(2)}) collective-permute-start(f32[16,2048]{1,0:T(8,128)} %get-tuple-element.22), channel_id=1, source_target_pairs={{0,32},{16,48},{32,64},{48,80},{64,96},{80,112},{96,0},{112,16},{1... | collective-permute-start | bytes 393224 | tf_op jit(solution)/shard_map/ppermute | solution.py:257
  75.2 3.2 %collective-permute-start.2 = (f32[16,2048]{1,0:T(8,128)}, f32[16,2048]{1,0:T(8,128)S(1)}, u32[]{:S(2)}, u32[]{:S(2)}) collective-permute-start(f32[16,2048]{1,0:T(8,128)} %get-tuple-element.23), channel_id=1, source_target_pairs={{0,64},{16,80},{32,96},{48,112},{64,0},{80,16},{96,32},{112,48},{1... | collective-permute-start | bytes 393224 | tf_op jit(solution)/shard_map/ppermute | solution.py:257
  78.4 1.2 %collective-permute-start.3 = (f32[16,2048]{1,0:T(8,128)}, f32[16,2048]{1,0:T(8,128)S(1)}, u32[]{:S(2)}, u32[]{:S(2)}) collective-permute-start(f32[16,2048]{1,0:T(8,128)} %get-tuple-element.24), channel_id=1, source_target_pairs={{0,96},{16,112},{32,0},{48,16},{64,32},{80,48},{96,64},{112,80},{1... | collective-permute-start | bytes 393224 | tf_op jit(solution)/shard_map/ppermute | solution.py:257
  79.6 0.6 constant_dynamic-slice_fusion.density_ref
  80.2 1.4 %all-to-all-done = f32[128,1,64]{2,1,0:T(1,128)S(1)} async-done(((f32[128,1,64]{2,1,0:T(1,128)}), f32[128,1,64]{2,1,0:T(1,128)S(1)}, u32[]{:S(2)}, u32[]{:S(2)}) %all-to-all-start) | async-done | bytes 32800 | tf_op jit(solution)/shard_map/all_to_all | solution.py:231
  81.5 0.0 copy-start.7
  81.5 0.0 collective-permute-done.1.e1
  81.5 0.0 copy-start.8
  81.5 3.6 %collective-permute-done.2.e2 = f32[16,2048]{1,0:T(8,128)S(1)} collective-permute-done((f32[16,2048]{1,0:T(8,128)}, f32[16,2048]{1,0:T(8,128)S(1)}, u32[]{:S(2)}, u32[]{:S(2)}) %collective-permute-start.2) | collective-permute-done | bytes 131104 | tf_op jit(solution)/shard_map/ppermute | solution.py:257
  85.2 0.0 copy-start.9
  85.2 0.0 collective-permute-done.3.e3
  85.2 0.0 copy-done.7
  85.2 0.0 copy-done.8
  85.2 0.6 copy-done.9
  85.8 0.0 copy-done.10
  85.9 2.8 %send.1 = (f32[1,64]{1,0:T(1,128)}, f32[16,4,128]{2,1,0:T(4,128)}) custom-call(s32[14]{0:T(128)} %stack.61.place_ref, f32[128,64]{1,0:T(8,128)} %bitcast.39, f32[16,2048]{1,0:T(8,128)} %copy-done.1, f32[16,2048]{1,0:T(8,128)} %copy-done.8, f32[16,2048]{1,0:T(8,128)} %copy-done.9, f32[16,2048]{1,0:T(8,128)} %copy-done.10, ...), custom_call_target="tpu_custom_call" | custom-call | tf_op jit(solution)/shard_map/send/pallas_call | solution.py:259
  88.7 14.4 %all_to_all.16.got_ref = f32[16,4,128]{2,1,0:T(4,128)} all-to-all(f32[16,4,128]{2,1,0:T(4,128)} %get-tuple-element.28), channel_id=1, replica_groups=mesh['sample'=8,'space'=16] {'space'}, dimensions={0} | all-to-all | bytes 65536 | tf_op jit(solution)/shard_map/all_to_all | solution.py:269
  103.0 2.3 %owner.1 = (f32[1,1,2048]{2,1,0:T(1,128)}, f32[1,1,2048]{2,1,0:T(1,128)}) custom-call(f32[16,4,128]{2,1,0:T(4,128)} %all_to_all.16.got_ref, s32[1,1,16,256]{3,2,1,0:T(8,128)} %cells_ref.1, f32[128,128]{1,0:T(8,128)} %filter_ref.1), custom_call_target="tpu_custom_call" | custom-call | tf_op jit(solution)/shard_map/owner/pallas_call | solution.py:270
  (2 shorter events, 0.0 us)
Async XLA Ops:
  0.6 3.1 %copy-start = (s32[1,8,16,256]{3,2,1,0:T(8,128)S(1)}, s32[1,8,16,256]{3,2,1,0:T(8,128)}, u32[]{:S(2)}) copy-start(s32[1,8,16,256]{3,2,1,0:T(8,128)} %param.13) | copy-start | bytes 393220
  0.6 1.6 %copy-start.6 = (s32[8,16384]{1,0:T(8,128)S(1)}, s32[8,16384]{1,0:T(8,128)}, u32[]{:S(2)}) copy-start(s32[8,16384]{1,0:T(8,128)} %param.9) | copy-start | bytes 1572868
  0.7 1.7 %copy-start.11 = (s32[1,8,16]{2,1,0:T(8,128)S(1)}, s32[1,8,16]{2,1,0:T(8,128)}, u32[]{:S(2)}) copy-start(s32[1,8,16]{2,1,0:T(8,128)} %param.14) | copy-start | bytes 1540
  0.7 3.7 %copy-start.12 = (bf16[24,24]{1,0:T(8,128)(2,1)S(1)}, bf16[24,24]{1,0:T(8,128)(2,1)}, u32[]{:S(2)}) copy-start(bf16[24,24]{1,0:T(8,128)(2,1)} %param.11) | copy-start | bytes 3460
  2.0 3.9 %copy-start.2 = (f32[16384]{0:T(1024)S(1)}, f32[16384]{0:T(1024)}, u32[]{:S(2)}) copy-start(f32[16384]{0:T(1024)} %param.10) | copy-start | bytes 196612
  2.0 3.9 %collective-permute-start = (f32[24,18560]{1,0:T(8,128)S(1)}, f32[24,18560]{1,0:T(8,128)}, u32[]{:S(2)}, u32[]{:S(2)}) collective-permute-start(f32[24,18560]{1,0:T(8,128)S(1)} %pad_convert_fusion.refs_8_), channel_id=1, source_target_pairs={{0,16},{16,0},{32,48},{48,32},{64,80},{80,64},{96,112},{112,96},{1... | collective-permute-start | bytes 5345288 | tf_op jit(solution)/shard_map/ppermute | solution.py:197
  58.3 0.6 copy-start.1
  59.0 0.6 copy-start.3
  59.6 0.7 copy-start.4
  60.3 0.7 copy-start.5
  60.9 20.6 %all-to-all-start = ((f32[128,1,64]{2,1,0:T(1,128)}), f32[128,1,64]{2,1,0:T(1,128)S(1)}, u32[]{:S(2)}, u32[]{:S(2)}) async-start(f32[128,1,64]{2,1,0:T(1,128)} %bitcast.17), calls=%async_computation | async-start | bytes 131072 | tf_op jit(solution)/shard_map/all_to_all | solution.py:231
  74.1 7.5 %collective-permute-start.1 = (f32[16,2048]{1,0:T(8,128)}, f32[16,2048]{1,0:T(8,128)S(1)}, u32[]{:S(2)}, u32[]{:S(2)}) collective-permute-start(f32[16,2048]{1,0:T(8,128)} %get-tuple-element.22), channel_id=1, source_target_pairs={{0,32},{16,48},{32,64},{48,80},{64,96},{80,112},{96,0},{112,16},{1... | collective-permute-start | bytes 393224 | tf_op jit(solution)/shard_map/ppermute | solution.py:257
  75.2 10.0 %collective-permute-start.2 = (f32[16,2048]{1,0:T(8,128)}, f32[16,2048]{1,0:T(8,128)S(1)}, u32[]{:S(2)}, u32[]{:S(2)}) collective-permute-start(f32[16,2048]{1,0:T(8,128)} %get-tuple-element.23), channel_id=1, source_target_pairs={{0,64},{16,80},{32,96},{48,112},{64,0},{80,16},{96,32},{112,48},{1... | collective-permute-start | bytes 393224 | tf_op jit(solution)/shard_map/ppermute | solution.py:257
  78.4 6.8 %collective-permute-start.3 = (f32[16,2048]{1,0:T(8,128)}, f32[16,2048]{1,0:T(8,128)S(1)}, u32[]{:S(2)}, u32[]{:S(2)}) collective-permute-start(f32[16,2048]{1,0:T(8,128)} %get-tuple-element.24), channel_id=1, source_target_pairs={{0,96},{16,112},{32,0},{48,16},{64,32},{80,48},{96,64},{112,80},{1... | collective-permute-start | bytes 393224 | tf_op jit(solution)/shard_map/ppermute | solution.py:257
  81.5 3.6 %copy-start.7 = (f32[128,1,64]{2,1,0:T(1,128)}, f32[128,1,64]{2,1,0:T(1,128)S(1)}, u32[]{:S(2)}) copy-start(f32[128,1,64]{2,1,0:T(1,128)S(1)} %all-to-all-done) | copy-start | bytes 98308
  81.5 3.6 %copy-start.8 = (f32[16,2048]{1,0:T(8,128)}, f32[16,2048]{1,0:T(8,128)S(1)}, u32[]{:S(2)}) copy-start(f32[16,2048]{1,0:T(8,128)S(1)} %collective-permute-done.1.e1) | copy-start | bytes 393220
  85.2 0.7 copy-start.9
  85.2 0.7 copy-start.10

commit v3 on v2

--- a/solution.py
+++ b/solution.py
@@ -23,8 +23,8 @@
 def energy_kernel(steps, place_ref, *refs):
     links = refs[:8]
     own_ref, other_ref, weight_ref, density_ref = refs[8:12]
-    out_refs, parts_ref = refs[12:16], refs[16]
-    table, rows, total = refs[17:]
+    out_ref, parts_ref = refs[12:14]
+    table, rows, total = refs[14:]
     turn, sub = pl.program_id(0), pl.program_id(1)
     nodes = table.shape[0]
 
@@ -71,13 +71,7 @@
     turned = folded.T
     half = turned[: LANES // 2] + turned[LANES // 2 :]
     energy = half[:ROWS] + half[ROWS : 2 * ROWS] + half[2 * ROWS : 3 * ROWS]
-    at = pl.ds(pl.multiple_of(sub * BLOCK, BLOCK), BLOCK)
-    for d in range(4):
-
-        @pl.when(turn == d)
-        def _(d=d):
-            out_refs[d][:, at] = energy
-
+    out_ref[0] = energy
     rho = density_ref[0]
     scaled = energy * (rho * rho * rho)
     acc = total[...]
@@ -100,50 +94,38 @@
     return high, (x - high.astype(F32)).astype(BF16)
 
 
-def prepare_kernel(place_ref, count_ref, picks_ref, *refs):
-    hot_ref, live_ref = refs[-2:]
-    dests, width = picks_ref.shape[1:]
-    low_id = lax.broadcasted_iota(jnp.int32, (LANES, width), 0)
-    high_id = lax.broadcasted_iota(jnp.int32, (16, width), 0)
-    slot = lax.broadcasted_iota(jnp.int32, (16, width), 1)
-    for d in range(dests):
-        pick = picks_ref[0, d : d + 1, :]
-        hot_ref[d] = jnp.where(low_id == (pick & (LANES - 1)), 1.0, 0.0).astype(BF16)
-        live = (high_id == (pick >> 7)) & (slot < count_ref[place_ref[0] * 16 + d])
-        live_ref[d] = jnp.where(live, 1.0, 0.0)
-
-
-def send_kernel(elements, place_ref, parts_ref, e0, e1, e2, e3, density_ref, hot_ref, live_ref, comp_ref, out_ref):
+def send_kernel(elements, place_ref, count_ref, parts_ref, energy_ref, density_ref, picks_ref, comp_ref, out_ref):
     comp = jnp.sum(parts_ref[...], axis=0, keepdims=True) / elements
     comp_ref[...] = comp
     center = jnp.mean(comp, axis=1, keepdims=True)
     spread = jnp.sqrt(jnp.mean((comp - center) ** 2, axis=1, keepdims=True) + epsilon)
     weight = (1.0 + spread_weight * (comp - center) / spread) / 64.0
-    row_id = lax.broadcasted_iota(jnp.int32, (8, 64), 0)
-    lane = lax.broadcasted_iota(jnp.int32, (8, 64), 1)
-    sens = mean = None
-    for d, e_ref in enumerate((e0, e1, e2, e3)):
-        for h in range(2):
-            spot = place_ref[6 + 2 * d + h] * 8 + row_id
-            column = jnp.sum(jnp.where(lane == spot, weight, 0.0), axis=1, keepdims=True)
-            field = e_ref[8 * h : 8 * h + 8, :]
-            term = column * field
-            sens = term if sens is None else sens + term
-            mean = field if mean is None else mean + field
-    rho = density_ref[0]
-    sens = -penalty * rho * rho * jnp.sum(sens, axis=0, keepdims=True)
-    mean = jnp.sum(mean, axis=0, keepdims=True) / 64.0
-    both = [f[:, h * LANES : (h + 1) * LANES] for f in (sens, mean) for h in range(16)]
-    table = jnp.concatenate(split(jnp.concatenate(both, axis=0)), axis=0)
-    dests, _, width = hot_ref.shape
-    for d in range(dests):
-        found = jnp.dot(table, hot_ref[d], preferred_element_type=F32)
-        found = found[:32] + found[32:]
-        for f in range(2):
-            got = jnp.sum(found[16 * f : 16 * f + 16] * live_ref[d], axis=0, keepdims=True)
-            for p in range(width // LANES):
-                r = f * (width // LANES) + p
-                out_ref[d, r : r + 1, :] = got[:, p * LANES : (p + 1) * LANES]
+    row_id = lax.broadcasted_iota(jnp.int32, (ROWS, 64), 0)
+    lane = lax.broadcasted_iota(jnp.int32, (ROWS, 64), 1)
+    spot = jnp.where(row_id < 8, place_ref[4] * 8 + row_id, place_ref[5] * 8 + row_id - 8)
+    column = jnp.sum(jnp.where(lane == spot, weight, 0.0), axis=1, keepdims=True)
+    _, dests, width = picks_ref.shape
+    low_id = lax.broadcasted_iota(jnp.int32, (LANES, width), 0)
+    high_id = lax.broadcasted_iota(jnp.int32, (16, width), 0)
+    slot = lax.broadcasted_iota(jnp.int32, (16, width), 1)
+    for q in range(4):
+        energy = energy_ref[q]
+        rho = density_ref[place_ref[q]]
+        sens = -penalty * rho * rho * jnp.sum(column * energy, axis=0, keepdims=True)
+        mean = jnp.sum(energy, axis=0, keepdims=True) / 64.0
+        both = [f[:, h * LANES : (h + 1) * LANES] for f in (sens, mean) for h in range(16)]
+        table = jnp.concatenate(split(jnp.concatenate(both, axis=0)), axis=0)
+        for d in range(dests):
+            pick = picks_ref[q, d : d + 1, :]
+            hot = jnp.where(low_id == (pick & (LANES - 1)), 1.0, 0.0).astype(BF16)
+            found = jnp.dot(table, hot, preferred_element_type=F32)
+            found = found[:32] + found[32:]
+            live = (high_id == (pick >> 7)) & (slot < count_ref[place_ref[q] * 16 + d])
+            for f in range(2):
+                got = jnp.sum(jnp.where(live, found[16 * f : 16 * f + 16], 0.0), axis=0, keepdims=True)
+                for p in range(width // LANES):
+                    r = f * (width // LANES) + p
+                    out_ref[q * dests + d, r : r + 1, :] = got[:, p * LANES : (p + 1) * LANES]
 
 
 def owner_kernel(got_ref, cells_ref, filter_ref, sens_ref, energy_ref):
@@ -156,8 +138,11 @@
         hot = jnp.where(low_id == (cell & (LANES - 1)), 1.0, 0.0).astype(BF16)
         mine = high_id == (cell >> 7)
         pieces = []
+        share = got_ref[j]
+        for q in range(1, 4):
+            share = share + got_ref[q * sources + j]
         for f in range(2):
-            value = jnp.concatenate([got_ref[j, 2 * f : 2 * f + 1, :], got_ref[j, 2 * f + 1 : 2 * f + 2, :]], axis=1)
+            value = jnp.concatenate([share[2 * f : 2 * f + 1], share[2 * f + 1 : 2 * f + 2]], axis=1)
             pieces.append(jnp.where(mine, value, 0.0))
         rows = jnp.concatenate(split(jnp.concatenate(pieces, axis=0)), axis=0)
         node = node + lax.dot_general(rows, hot, (((1,), (1,)), ((), ())), preferred_element_type=F32)
@@ -184,7 +169,7 @@
 
 def body(displacements, connectivity, density, stiffness, filter_inverse, send_rows, send_count, recv_cell):
     group_id = lax.axis_index("sample")
-    z, core = group_id // 2, group_id % 2
+    core = group_id % 2
     node_count = displacements.shape[2]
     elements = density.shape[0]
     groups = 8
@@ -199,8 +184,7 @@
     rho = density.reshape(groups, 1, sub_rows)
     weights = block_stiffness(stiffness)
 
-    order = (1, 2, 3, 0)
-    place = [2 * ((z + d) % 4) + core for d in order] + [group_id, group_id ^ 1]
+    place = jnp.stack([2 * q + core for q in range(4)] + [group_id, group_id ^ 1]).astype(jnp.int32)
     steps = sub_rows // BLOCK
     per_corner = elements // BLOCK
 
@@ -210,63 +194,42 @@
         )
 
     whole = pl.BlockSpec(memory_space=pltpu.VMEM)
-    energies = pl.pallas_call(
+    energies, mine = pl.pallas_call(
         functools.partial(energy_kernel, steps),
         grid_spec=pltpu.PrefetchScalarGridSpec(
             num_scalar_prefetch=1,
             grid=(4, steps),
             in_specs=[link_spec(c) for c in range(8)]
             + [whole, whole, whole, pl.BlockSpec((1, 1, BLOCK), lambda t, s, at: (at[t], 0, s))],
-            out_specs=[whole] * 5,
+            out_specs=[pl.BlockSpec((1, ROWS, BLOCK), lambda t, s, at: (t, 0, s)), whole],
             scratch_shapes=[
                 pltpu.VMEM((nodes, LANES), F32),
                 pltpu.VMEM((BLOCK, 4 * LANES), F32),
                 pltpu.VMEM((ROWS, LANES), F32),
             ],
         ),
-        out_shape=[jax.ShapeDtypeStruct((ROWS, sub_rows), F32)] * 4 + [jax.ShapeDtypeStruct((128, 64), F32)],
+        out_shape=[jax.ShapeDtypeStruct((4, ROWS, sub_rows), F32), jax.ShapeDtypeStruct((128, 64), F32)],
         compiler_params=pltpu.CompilerParams(vmem_limit_bytes=48 * 2**20),
         name="energy",
-    )(jnp.stack(place).astype(jnp.int32), *([links] * 8), own, other, weights, rho)
-    parts = lax.all_to_all(energies[4], ("sample", "space"), split_axis=0, concat_axis=0, tiled=True)
-    source = [2 * ((z - d) % 4) for d in range(4)]
-    place2 = [group_id] * 6
-    for base in source:
-        place2 += [base + core, base + 1 - core]
-    place2 = jnp.stack(place2).astype(jnp.int32)
-
+    )(place, *([links] * 8), own, other, weights, rho)
+    parts = lax.all_to_all(mine, ("sample", "space"), split_axis=0, concat_axis=0, tiled=True)
     smem = pl.BlockSpec(memory_space=pltpu.SMEM)
-    stay = pl.BlockSpec(memory_space=pl.ANY)
-    width = send_rows.shape[-1]
-    e1, e2, e3, hot, live = pl.pallas_call(
-        prepare_kernel,
-        in_specs=[smem, smem, whole, stay, stay, stay],
-        out_specs=[stay, stay, stay, whole, whole],
-        out_shape=[jax.ShapeDtypeStruct((ROWS, sub_rows), F32)] * 3
-        + [jax.ShapeDtypeStruct((slabs, LANES, width), BF16), jax.ShapeDtypeStruct((slabs, 16, width), F32)],
-        input_output_aliases={3: 0, 4: 1, 5: 2},
-        cost_estimate=pl.CostEstimate(flops=4 * 10**9, bytes_accessed=2**21, transcendentals=0),
-        name="prepare",
-    )(
-        place2,
-        send_count.reshape(-1),
-        lax.dynamic_slice_in_dim(send_rows[0], group_id, 1, 0),
-        *energies[:3],
-    )
-    arrived = [energies[3]] + [
-        lax.ppermute(e, "sample", [(i, (i + 2 * d) % 8) for i in range(8)]) for d, e in ((1, e1), (2, e2), (3, e3))
-    ]
+    dests, width = send_rows.shape[-2:]
+    picks = lax.dynamic_index_in_dim(send_rows.reshape(4, 2, dests, width), core, 1, keepdims=False)
     compliance, outgoing = pl.pallas_call(
         functools.partial(send_kernel, float(elements * slabs)),
-        in_specs=[smem] + [whole] * 8,
+        in_specs=[smem, smem] + [whole] * 4,
         out_specs=[whole] * 2,
         out_shape=[
             jax.ShapeDtypeStruct((1, 64), F32),
-            jax.ShapeDtypeStruct((slabs, 2 * width // LANES, LANES), F32),
+            jax.ShapeDtypeStruct((4 * dests, 2 * width // LANES, LANES), F32),
         ],
         name="send",
-    )(place2, parts, *arrived, lax.dynamic_slice_in_dim(rho, group_id, 1, 0), hot, live)
-    got = lax.all_to_all(outgoing, "space", split_axis=0, concat_axis=0, tiled=True)
+    )(place, send_count.reshape(-1), parts, energies, rho, picks)
+    peers = [[i * slabs + j for i in range(c, groups, 2) for j in range(slabs)] for c in range(2)]
+    got = lax.all_to_all(
+        outgoing, ("sample", "space"), split_axis=0, concat_axis=0, tiled=True, axis_index_groups=peers
+    )
     sens, energy = pl.pallas_call(
         owner_kernel,
         in_specs=[whole] * 3,

time: 106 us -> 102 us (0.962)
  starting transfers between devices: 16.7 us -> 11.2 us
  waiting for transfers between devices: 6.09 us -> 11.2 us
  local copies, waits for them, and re-layouts: 5.9 us -> 2.86 us
    all_to_all x1, waiting for transfers between devices: 1.37 us -> 8.15 us  [body(): lax.all_to_all(mine, ('sample', 'space'), split_axis=0, concat_axis=0, ti...]
    ppermute x3 -> x0, starting transfers between devices: 5.49 us -> none  [body(): lax.ppermute(e, 'sample', [(i, (i + 2 * d) % 8) for i in range(8)])]
    ppermute x3 -> x0, waiting for transfers between devices: 3.64 us -> none  [body(): lax.ppermute(e, 'sample', [(i, (i + 2 * d) % 8) for i in range(8)])]
    pallas_call x1 -> x0, Pallas kernels: 2.01 us -> none  [body(): pl.pallas_call(prepare_kernel, in_specs=[smem, smem, whole, stay, stay, s...]
    ppermute x1, waiting for transfers between devices: 1.09 us -> 3.03 us  [body(): other = lax.ppermute(own, 'sample', [(i, i ^ 1) for i in range(8)])]
    unnamed x27 -> x17, local copies, waits for them, and re-layouts: 3.41 us -> 1.55 us
    dynamic_slice x2 -> x0, local copies, waits for them, and re-layouts: 1.21 us -> none  [the longest x1 0.61 us: body(): lax.dynamic_slice_in_dim(send_rows[0], group_id, 1, 0)]
  transfers between devices with their start and end apart: 5 -> 2, of which waited for: 3 -> 2; matrix products, arithmetic and copies ran while one was open for 3% -> 2% of each run, Pallas kernels for 2% -> 0%
where the time goes in v3:
time: 102 us
  Pallas kernels  58.5 us (57%)
  blocking collectives  15.3 us (15%)
  starting transfers between devices  11.2 us (11%)
  waiting for transfers between devices  11.2 us (11%)
  local copies, waits for them, and re-layouts  2.86 us (3%)
  other arithmetic  1.36 us (1%)
    pallas_call x1, Pallas kernels, body(): pl.pallas_call(functools.partial(energy_kernel, steps), grid_spec=pltpu.P...  52.3 us
    all_to_all x1, blocking collectives, body(): lax.all_to_all(outgoing, ('sample', 'space'), split_axis=0, concat_axis=0...  15.3 us
    all_to_all x1, starting transfers between devices, body(): lax.all_to_all(mine, ('sample', 'space'), split_axis=0, concat_axis=0, ti...  11.1 us
    all_to_all x1, waiting for transfers between devices, body(): lax.all_to_all(mine, ('sample', 'space'), split_axis=0, concat_axis=0, ti...  8.15 us
    pallas_call x1, Pallas kernels, body(): pl.pallas_call(functools.partial(send_kernel, float(elements * slabs)), i...  3.86 us
    ppermute x1, waiting for transfers between devices, body(): other = lax.ppermute(own, 'sample', [(i, i ^ 1) for i in range(8)])  3.03 us
    pallas_call x1, Pallas kernels, body(): pl.pallas_call(owner_kernel, in_specs=[whole] * 3, out_specs=[whole] * 2,...  2.34 us
  transfers between devices with their start and end apart: 2, of which 2 were waited for; matrix products, arithmetic and copies ran while one was open for 2% of the time, Pallas kernels for 0%

profile of v3, /device:TPU:0, one launch (start us, length us, event | category | flops | bytes accessed | tf_op | source)
XLA Modules:
  0.0 101.7 jit_solution(6512436751714213268)
XLA Ops:
  0.6 0.0 copy-start
  0.6 0.0 copy-start.4
  0.7 0.0 copy-start.7
  0.7 0.0 copy-start.2
  0.7 1.4 %pad_convert_fusion.refs_8_ = f32[24,18560]{1,0:T(8,128)S(1)} fusion(bf16[24,18513]{1,0:T(8,128)(2,1)} %bitcast.34), kind=kLoop, calls=%fused_computation.3 | loop fusion | flops 445440 | bytes 2670384 | tf_op jit(solution)/shard_map/jit(_pad)/pad | solution.py:181
  2.0 0.1 collective-permute-start
  2.1 0.0 copy-done.4
  2.2 0.1 copy.15
  2.3 0.1 stack.27.place_ref
  2.4 0.0 copy-start.3
  2.4 0.0 copy-done.7
  2.4 0.5 fusion.refs_10_
  2.9 3.0 %collective-permute-done.refs_9_ = f32[24,18560]{1,0:T(8,128)} collective-permute-done((f32[24,18560]{1,0:T(8,128)S(1)}, f32[24,18560]{1,0:T(8,128)}, u32[]{:S(2)}, u32[]{:S(2)}) %collective-permute-start) | collective-permute-done | bytes 1781792 | tf_op jit(solution)/shard_map/ppermute | solution.py:182
  6.0 0.0 copy-done.2
  6.0 0.0 copy-start.6
  6.0 52.3 %energy.1 = (f32[4,16,2048]{2,1,0:T(8,128)S(1)}, f32[128,64]{1,0:T(8,128)}) custom-call(s32[6]{0:T(128)S(1)} %stack.27.place_ref, s32[131072]{0:T(1024)S(1)} %bitcast.24, s32[131072]{0:T(1024)S(1)} %bitcast.25, s32[131072]{0:T(1024)S(1)} %bitcast.26, s32[131072]{0:T(1024)S(1)} %bitcast.27, s32[131072]{0:T(1024)S(1)} %bitcast.28, s32[131072]{0:T(1024)S(1)} %bitcast.29, ...), custom_call_target="tpu_custom_call" | custom-call | tf_op jit(solution)/shard_map/energy/pallas_call | solution.py:197
  58.2 0.0 copy-done.3
  58.2 0.0 copy-start.1
  58.2 0.8 copy-done.1
  59.0 11.1 %all-to-all-start = ((f32[128,1,64]{2,1,0:T(1,128)}), f32[128,1,64]{2,1,0:T(1,128)S(1)}, u32[]{:S(2)}, u32[]{:S(2)}) async-start(f32[128,1,64]{2,1,0:T(1,128)} %bitcast.10), calls=%async_computation | async-start | bytes 131072 | tf_op jit(solution)/shard_map/all_to_all | solution.py:215
  70.2 0.0 copy-done
  70.2 0.6 dynamic-slice_bitcast_fusion.picks_ref
  70.8 0.0 copy-done.6
  70.8 0.6 reshape.107.count_ref
  71.4 8.1 %all-to-all-done = f32[128,1,64]{2,1,0:T(1,128)S(1)} async-done(((f32[128,1,64]{2,1,0:T(1,128)}), f32[128,1,64]{2,1,0:T(1,128)S(1)}, u32[]{:S(2)}, u32[]{:S(2)}) %all-to-all-start) | async-done | bytes 32800 | tf_op jit(solution)/shard_map/all_to_all | solution.py:215
  79.6 0.0 copy-start.5
  79.6 0.6 copy-done.5
  80.2 3.9 %send.1 = (f32[1,64]{1,0:T(1,128)}, f32[64,4,128]{2,1,0:T(4,128)}) custom-call(s32[6]{0:T(128)} %copy-done.3, s32[128]{0:T(128)} %reshape.107.count_ref, f32[128,64]{1,0:T(8,128)} %bitcast.36, f32[4,16,2048]{2,1,0:T(8,128)} %copy-done.1, f32[8,1,2048]{2,1,0:T(1,128)} %bitcast.32, s32[4,16,256]{2,1,0:T(8,128)} %dynamic-slice_bitcast_fusion.picks_ref), custom_call_target="tpu_custom_call" | custom-call | tf_op jit(solution)/shard_map/send/pallas_call | solution.py:219
  84.0 15.3 %all_to_all.16.got_ref = f32[64,4,128]{2,1,0:T(4,128)} all-to-all(f32[64,4,128]{2,1,0:T(4,128)} %get-tuple-element.12), channel_id=1, replica_groups={{0,1,2,3,4,5,6,7,8,9,10,11,12,13,14,15,32,33,34,35,36,37,38,39,40,41,42..., dimensions={0} | all-to-all | bytes 262144 | tf_op jit(solution)/shard_map/all_to_all | solution.py:230
  99.3 2.3 %owner.1 = (f32[1,1,2048]{2,1,0:T(1,128)}, f32[1,1,2048]{2,1,0:T(1,128)}) custom-call(f32[64,4,128]{2,1,0:T(4,128)} %all_to_all.16.got_ref, s32[1,1,16,256]{3,2,1,0:T(8,128)} %cells_ref.1, f32[128,128]{1,0:T(8,128)} %filter_ref.1), custom_call_target="tpu_custom_call" | custom-call | tf_op jit(solution)/shard_map/owner/pallas_call | solution.py:233
  (1 shorter events, 0.0 us)
Async XLA Ops:
  0.6 69.5 %copy-start = (s32[1,8,16,256]{3,2,1,0:T(8,128)S(1)}, s32[1,8,16,256]{3,2,1,0:T(8,128)}, u32[]{:S(2)}) copy-start(s32[1,8,16,256]{3,2,1,0:T(8,128)} %param.13) | copy-start | bytes 393220
  0.6 1.5 %copy-start.4 = (s32[8,16384]{1,0:T(8,128)S(1)}, s32[8,16384]{1,0:T(8,128)}, u32[]{:S(2)}) copy-start(s32[8,16384]{1,0:T(8,128)} %param.9) | copy-start | bytes 1572868
  0.7 1.7 %copy-start.7 = (bf16[24,24]{1,0:T(8,128)(2,1)S(1)}, bf16[24,24]{1,0:T(8,128)(2,1)}, u32[]{:S(2)}) copy-start(bf16[24,24]{1,0:T(8,128)(2,1)} %param.11) | copy-start | bytes 3460
  0.7 5.3 %copy-start.2 = (f32[16384]{0:T(1024)S(1)}, f32[16384]{0:T(1024)}, u32[]{:S(2)}) copy-start(f32[16384]{0:T(1024)} %param.10) | copy-start | bytes 196612
  2.0 3.9 %collective-permute-start = (f32[24,18560]{1,0:T(8,128)S(1)}, f32[24,18560]{1,0:T(8,128)}, u32[]{:S(2)}, u32[]{:S(2)}) collective-permute-start(f32[24,18560]{1,0:T(8,128)S(1)} %pad_convert_fusion.refs_8_), channel_id=1, source_target_pairs={{0,16},{16,0},{32,48},{48,32},{64,80},{80,64},{96,112},{112,96},{1... | collective-permute-start | bytes 5345288 | tf_op jit(solution)/shard_map/ppermute | solution.py:182
  2.4 55.9 %copy-start.3 = (s32[6]{0:T(128)}, s32[6]{0:T(128)S(1)}, u32[]{:S(2)}) copy-start(s32[6]{0:T(128)S(1)} %stack.27.place_ref) | copy-start | bytes 76
  6.0 64.9 %copy-start.6 = (s32[1,8,16]{2,1,0:T(8,128)S(1)}, s32[1,8,16]{2,1,0:T(8,128)}, u32[]{:S(2)}) copy-start(s32[1,8,16]{2,1,0:T(8,128)} %param.14) | copy-start | bytes 1540
  58.2 0.8 copy-start.1
  59.0 20.5 %all-to-all-start = ((f32[128,1,64]{2,1,0:T(1,128)}), f32[128,1,64]{2,1,0:T(1,128)S(1)}, u32[]{:S(2)}, u32[]{:S(2)}) async-start(f32[128,1,64]{2,1,0:T(1,128)} %bitcast.10), calls=%async_computation | async-start | bytes 131072 | tf_op jit(solution)/shard_map/all_to_all | solution.py:215
  79.6 0.6 copy-start.5

commit v4 on v3

--- a/solution.py
+++ b/solution.py
@@ -12,81 +12,85 @@
 epsilon = 1e-06
 
 LANES = 128
-BLOCK = 1024
+BLOCK = 2048
 FILL = 29
-UNROLL = 32
+UNROLL = 64
 ROWS = 16
 F32 = jnp.float32
 BF16 = jnp.bfloat16
 
 
-def energy_kernel(steps, place_ref, *refs):
-    links = refs[:8]
-    own_ref, other_ref, weight_ref, density_ref = refs[8:12]
-    out_ref, parts_ref = refs[12:14]
-    table, rows, total = refs[14:]
-    turn, sub = pl.program_id(0), pl.program_id(1)
-    nodes = table.shape[0]
-
-    @pl.when((turn == 0) & (sub == 0))
-    def _():
-        total[...] = jnp.zeros_like(total)
-        pad = jnp.zeros((ROWS, LANES), F32)
-
-        def fill(n, _):
-            start = pl.multiple_of(n * (FILL * LANES), LANES)
-            for i in range(FILL):
-                at = pl.ds(start + i * LANES, LANES)
-                own, other = own_ref[:, at], other_ref[:, at]
-                half = []
-                for k in range(3):
-                    half += [own[8 * k : 8 * k + 8], other[8 * k : 8 * k + 8]]
-                half.append(pad)
-                table[at, :] = jnp.concatenate(half + half, axis=0).T
+def energy_kernel(place_ref, links_ref, own_ref, other_ref, weight_ref, density_ref, out_ref, parts_ref, table, rows, *rest):
+    links, sem = rest[:8], rest[8]
+    elements = links_ref.shape[0] // 8
+    copies = []
+    for c in range(8):
+        for q in range(4):
+            start = pl.multiple_of(c * elements + place_ref[q] * BLOCK, BLOCK)
+            copies.append(
+                pltpu.make_async_copy(
+                    links_ref.at[pl.ds(start, BLOCK)], links[c].at[pl.ds(q * BLOCK, BLOCK)], sem.at[c, q]
+                )
+            )
+            copies[-1].start()
+
+    pad = jnp.zeros((ROWS, LANES), F32)
+
+    def fill(n, _):
+        start = pl.multiple_of(n * (FILL * LANES), LANES)
+        for i in range(FILL):
+            at = pl.ds(start + i * LANES, LANES)
+            own, other = own_ref[:, at], other_ref[:, at]
+            half = []
+            for k in range(3):
+                half += [own[8 * k : 8 * k + 8], other[8 * k : 8 * k + 8]]
+            half.append(pad)
+            table[at, :] = jnp.concatenate(half + half, axis=0).T
+        return 0
+
+    lax.fori_loop(0, table.shape[0] // (FILL * LANES), fill, 0)
+    for copy in copies:
+        copy.wait()
+
+    first_half = lax.broadcasted_iota(jnp.int32, (1, LANES), 1) < LANES // 2
+    reach = 4 * BLOCK - UNROLL
+
+    def group(q, acc):
+        def gather(t, _):
+            start = pl.multiple_of(t * UNROLL, UNROLL)
+            view = rows.at[pl.ds(start, UNROLL)]
+            e = q * BLOCK + start
+            for u in range(UNROLL):
+                for p in range(4):
+                    low = table[pl.ds(links[2 * p].at[pl.ds(u, reach)][e], 1), :]
+                    high = table[pl.ds(links[2 * p + 1].at[pl.ds(u, reach)][e], 1), :]
+                    view[u : u + 1, p * LANES : (p + 1) * LANES] = jnp.where(first_half, low, high)
             return 0
 
-        lax.fori_loop(0, nodes // (FILL * LANES), fill, 0)
-
-    first_half = lax.broadcasted_iota(jnp.int32, (1, LANES), 1) < LANES // 2
-
-    def gather(t, _):
-        start = pl.multiple_of(t * UNROLL, UNROLL)
-        view = rows.at[pl.ds(start, UNROLL)]
-        for u in range(UNROLL):
-            e = start + u
-            for p in range(4):
-                low = table[pl.ds(links[2 * p][e], 1), :]
-                high = table[pl.ds(links[2 * p + 1][e], 1), :]
-                view[u : u + 1, p * LANES : (p + 1) * LANES] = jnp.where(first_half, low, high)
-        return 0
-
-    lax.fori_loop(0, BLOCK // UNROLL, gather, 0)
-
-    field = rows[...]
-    applied = jnp.dot(field.astype(BF16), weight_ref[...], preferred_element_type=F32)
-    product = field * applied
-    folded = product[:, :LANES]
-    for p in range(1, 4):
-        folded = folded + product[:, p * LANES : (p + 1) * LANES]
-    turned = folded.T
-    half = turned[: LANES // 2] + turned[LANES // 2 :]
-    energy = half[:ROWS] + half[ROWS : 2 * ROWS] + half[2 * ROWS : 3 * ROWS]
-    out_ref[0] = energy
-    rho = density_ref[0]
-    scaled = energy * (rho * rho * rho)
-    acc = total[...]
-    for p in range(BLOCK // LANES):
-        acc = acc + scaled[:, p * LANES : (p + 1) * LANES]
-    total[...] = acc
-
-    @pl.when((turn == 3) & (sub == steps - 1))
-    def _():
-        column = jnp.sum(acc, axis=1, keepdims=True)
-        row_id = lax.broadcasted_iota(jnp.int32, (ROWS, 64), 0)
-        lane = lax.broadcasted_iota(jnp.int32, (ROWS, 64), 1)
-        spot = jnp.where(row_id < 8, place_ref[4] * 8 + row_id, place_ref[5] * 8 + row_id - 8)
-        row = jnp.sum(jnp.where(lane == spot, column, 0.0), axis=0, keepdims=True)
-        parts_ref[...] = jnp.broadcast_to(row, parts_ref.shape)
+        lax.fori_loop(0, BLOCK // UNROLL, gather, 0)
+        field = rows[...]
+        applied = jnp.dot(field.astype(BF16), weight_ref[...], preferred_element_type=F32)
+        product = field * applied
+        folded = product[:, :LANES]
+        for p in range(1, 4):
+            folded = folded + product[:, p * LANES : (p + 1) * LANES]
+        turned = folded.T
+        half = turned[: LANES // 2] + turned[LANES // 2 :]
+        energy = half[:ROWS] + half[ROWS : 2 * ROWS] + half[2 * ROWS : 3 * ROWS]
+        out_ref[q] = energy
+        rho = density_ref[place_ref[q]]
+        scaled = energy * (rho * rho * rho)
+        for p in range(BLOCK // LANES):
+            acc = acc + scaled[:, p * LANES : (p + 1) * LANES]
+        return acc
+
+    acc = lax.fori_loop(0, 4, group, jnp.zeros((ROWS, LANES), F32))
+    column = jnp.sum(acc, axis=1, keepdims=True)
+    row_id = lax.broadcasted_iota(jnp.int32, (ROWS, 64), 0)
+    lane = lax.broadcasted_iota(jnp.int32, (ROWS, 64), 1)
+    spot = jnp.where(row_id < 8, place_ref[4] * 8 + row_id, place_ref[5] * 8 + row_id - 8)
+    row = jnp.sum(jnp.where(lane == spot, column, 0.0), axis=0, keepdims=True)
+    parts_ref[...] = jnp.broadcast_to(row, parts_ref.shape)
 
 
 def split(x):
@@ -185,35 +189,20 @@
     weights = block_stiffness(stiffness)
 
     place = jnp.stack([2 * q + core for q in range(4)] + [group_id, group_id ^ 1]).astype(jnp.int32)
-    steps = sub_rows // BLOCK
-    per_corner = elements // BLOCK
-
-    def link_spec(c):
-        return pl.BlockSpec(
-            (BLOCK,), lambda t, s, at: (c * per_corner + at[t] * steps + s,), memory_space=pltpu.SMEM
-        )
-
     whole = pl.BlockSpec(memory_space=pltpu.VMEM)
+    smem = pl.BlockSpec(memory_space=pltpu.SMEM)
     energies, mine = pl.pallas_call(
-        functools.partial(energy_kernel, steps),
-        grid_spec=pltpu.PrefetchScalarGridSpec(
-            num_scalar_prefetch=1,
-            grid=(4, steps),
-            in_specs=[link_spec(c) for c in range(8)]
-            + [whole, whole, whole, pl.BlockSpec((1, 1, BLOCK), lambda t, s, at: (at[t], 0, s))],
-            out_specs=[pl.BlockSpec((1, ROWS, BLOCK), lambda t, s, at: (t, 0, s)), whole],
-            scratch_shapes=[
-                pltpu.VMEM((nodes, LANES), F32),
-                pltpu.VMEM((BLOCK, 4 * LANES), F32),
-                pltpu.VMEM((ROWS, LANES), F32),
-            ],
-        ),
+        energy_kernel,
+        in_specs=[smem, pl.BlockSpec(memory_space=pl.ANY)] + [whole] * 4,
+        out_specs=[whole] * 2,
         out_shape=[jax.ShapeDtypeStruct((4, ROWS, sub_rows), F32), jax.ShapeDtypeStruct((128, 64), F32)],
-        compiler_params=pltpu.CompilerParams(vmem_limit_bytes=48 * 2**20),
+        scratch_shapes=[pltpu.VMEM((nodes, LANES), F32), pltpu.VMEM((BLOCK, 4 * LANES), F32)]
+        + [pltpu.SMEM((4 * BLOCK,), jnp.int32)] * 8
+        + [pltpu.SemaphoreType.DMA((8, 4))],
+        compiler_params=pltpu.CompilerParams(vmem_limit_bytes=30 * 2**20),
         name="energy",
-    )(place, *([links] * 8), own, other, weights, rho)
+    )(place, links, own, other, weights, rho)
     parts = lax.all_to_all(mine, ("sample", "space"), split_axis=0, concat_axis=0, tiled=True)
-    smem = pl.BlockSpec(memory_space=pltpu.SMEM)
     dests, width = send_rows.shape[-2:]
     picks = lax.dynamic_index_in_dim(send_rows.reshape(4, 2, dests, width), core, 1, keepdims=False)
     compliance, outgoing = pl.pallas_call(
@@ -224,6 +213,7 @@
             jax.ShapeDtypeStruct((1, 64), F32),
             jax.ShapeDtypeStruct((4 * dests, 2 * width // LANES, LANES), F32),
         ],
+        compiler_params=pltpu.CompilerParams(vmem_limit_bytes=8 * 2**20),
         name="send",
     )(place, send_count.reshape(-1), parts, energies, rho, picks)
     peers = [[i * slabs + j for i in range(c, groups, 2) for j in range(slabs)] for c in range(2)]
@@ -235,6 +225,7 @@
         in_specs=[whole] * 3,
         out_specs=[whole] * 2,
         out_shape=[jax.ShapeDtypeStruct((1, 1, sub_rows), F32)] * 2,
+        compiler_params=pltpu.CompilerParams(vmem_limit_bytes=8 * 2**20),
         name="owner",
     )(got, recv_cell, filter_inverse)
     return (compliance.reshape(-1), sens, energy)

time: 102 us -> 95.6 us (0.937)
  Pallas kernels: 58.5 us -> 51.8 us
    pallas_call x1, Pallas kernels: 52.3 us -> 47.2 us  [body(): pl.pallas_call(energy_kernel, in_specs=[smem, pl.BlockSpec(memory_space=p...]
    unnamed x17 -> x13, local copies, waits for them, and re-layouts: 1.55 us -> 2.3 us
where the time goes in v4:
time: 95.6 us; the launch traced here: 95.2 us
  Pallas kernels  51.8 us (54%)
  blocking collectives  14.6 us (15%)
  starting transfers between devices  11.2 us (12%)
  waiting for transfers between devices  11 us (12%)
  local copies, waits for them, and re-layouts  3.17 us (3%)
  other arithmetic  1.36 us (1%)
  matrix products  1.23 us (1%)
    pallas_call x1, Pallas kernels, body(): pl.pallas_call(energy_kernel, in_specs=[smem, pl.BlockSpec(memory_space=p...  47.2 us
    all_to_all x1, blocking collectives, body(): lax.all_to_all(outgoing, ('sample', 'space'), split_axis=0, concat_axis=0...  14.6 us
    all_to_all x1, starting transfers between devices, body(): lax.all_to_all(mine, ('sample', 'space'), split_axis=0, concat_axis=0, ti...  11.1 us
    all_to_all x1, waiting for transfers between devices, body(): lax.all_to_all(mine, ('sample', 'space'), split_axis=0, concat_axis=0, ti...  8.68 us
    pallas_call x1, Pallas kernels, body(): pl.pallas_call(functools.partial(send_kernel, float(elements * slabs)), i...  3.15 us
    ppermute x1, waiting for transfers between devices, body(): other = lax.ppermute(own, 'sample', [(i, i ^ 1) for i in range(8)])  2.35 us
    unnamed x13, local copies, waits for them, and re-layouts  2.3 us
  transfers between devices with their start and end apart: 2, of which 2 were waited for; matrix products, arithmetic and copies ran while one was open for 2% of the time, Pallas kernels for 0%

profile of v4, /device:TPU:0, one launch (start us, length us, event | category | flops | bytes accessed | tf_op | source)
XLA Modules:
  0.0 95.2 jit_solution(14528840015460920196)
XLA Ops:
  0.6 0.0 copy-start
  0.6 0.0 copy-start.5
  0.7 0.0 copy-start.1
  0.7 1.4 %pad_convert_fusion.own_ref = f32[24,18560]{1,0:T(8,128)S(1)} fusion(bf16[24,18513]{1,0:T(8,128)(2,1)} %bitcast.29), kind=kLoop, calls=%fused_computation.3 | loop fusion | flops 445440 | bytes 2670384 | tf_op jit(solution)/shard_map/jit(_pad)/pad | solution.py:185
  2.0 0.1 collective-permute-start
  2.1 0.0 copy-done.5
  2.1 0.1 copy.15
  2.3 0.1 stack.27.place_ref
  2.4 1.2 %fusion.weight_ref = bf16[512,512]{1,0:T(8,128)(2,1)S(1)} fusion(bf16[24,24]{1,0:T(8,128)(2,1)} %param.11, s32[512]{0:T(512)S(1)} %get-tuple-element.15, s32[512]{0:T(512)S(1)} %get-tuple-element.16), kind=kOutput, calls=%fused_computation.1 | convolution fusion | flops 13996032 | bytes 529536 | tf_op jit(solution)/shard_map/dot_general | solution.py:169
  3.6 2.3 %collective-permute-done.other_ref = f32[24,18560]{1,0:T(8,128)} collective-permute-done((f32[24,18560]{1,0:T(8,128)S(1)}, f32[24,18560]{1,0:T(8,128)}, u32[]{:S(2)}, u32[]{:S(2)}) %collective-permute-start) | collective-permute-done | bytes 1781792 | tf_op jit(solution)/shard_map/ppermute | solution.py:186
  5.9 0.0 copy-done.1
  5.9 47.2 %energy.1 = (f32[4,16,2048]{2,1,0:T(8,128)S(1)}, f32[128,64]{1,0:T(8,128)S(1)}) custom-call(s32[6]{0:T(128)S(1)} %stack.27.place_ref, s32[131072]{0:T(1024)S(1)} %bitcast.24, f32[24,18560]{1,0:T(8,128)S(1)} %pad_convert_fusion.own_ref, f32[24,18560]{1,0:T(8,128)} %collective-permute-done.other_ref, bf16[512,512]{1,0:T(8,128)(2,1)S(1)} %fusion.weight_ref, ...), custom_call_target="tpu_custom_call" | custom-call | tf_op jit(solution)/shard_map/energy/pallas_call | solution.py:194
  53.1 0.0 copy-start.3
  53.1 0.6 copy-done.3
  53.8 11.1 %all-to-all-start = ((f32[128,1,64]{2,1,0:T(1,128)}), f32[128,1,64]{2,1,0:T(1,128)S(1)}, u32[]{:S(2)}, u32[]{:S(2)}) async-start(f32[128,1,64]{2,1,0:T(1,128)} %bitcast.28), calls=%async_computation | async-start | bytes 131072 | tf_op jit(solution)/shard_map/all_to_all | solution.py:205
  64.9 0.0 copy-done
  65.0 0.8 reshape.107.count_ref
  65.7 8.7 %all-to-all-done = f32[128,1,64]{2,1,0:T(1,128)S(1)} async-done(((f32[128,1,64]{2,1,0:T(1,128)}), f32[128,1,64]{2,1,0:T(1,128)S(1)}, u32[]{:S(2)}, u32[]{:S(2)}) %all-to-all-start) | async-done | bytes 32800 | tf_op jit(solution)/shard_map/all_to_all | solution.py:205
  74.4 3.2 %send.1 = (f32[1,64]{1,0:T(1,128)}, f32[64,4,128]{2,1,0:T(4,128)S(1)}) custom-call(s32[6]{0:T(128)S(1)} %stack.27.place_ref, s32[128]{0:T(128)S(1)} %reshape.107.count_ref, f32[128,64]{1,0:T(8,128)S(1)} %bitcast.27, f32[4,16,2048]{2,1,0:T(8,128)S(1)} %get-tuple-element.10.energy_ref, f32[8,1,2048]{2,1,0:T(1,128)S(1)} %bitcast.26, ...), custom_call_target="tpu_custom_call" | custom-call | tf_op jit(solution)/shard_map/send/pallas_call | solution.py:208
  77.6 14.6 %all_to_all.16.got_ref = f32[64,4,128]{2,1,0:T(4,128)S(1)} all-to-all(f32[64,4,128]{2,1,0:T(4,128)S(1)} %get-tuple-element.12), channel_id=1, replica_groups={{0,1,2,3,4,5,6,7,8,9,10,11,12,13,14,15,32,33,34,35,36,37,38,39,40,41,42..., dimensions={0} | all-to-all | bytes 262144 | tf_op jit(solution)/shard_map/all_to_all | solution.py:220
  92.2 0.0 copy-start.2
  92.2 0.8 copy-done.2
  93.0 0.0 copy-start.4
  93.0 0.7 copy-done.4
  93.8 1.4 %owner.1 = (f32[1,1,2048]{2,1,0:T(1,128)}, f32[1,1,2048]{2,1,0:T(1,128)}) custom-call(f32[64,4,128]{2,1,0:T(4,128)S(1)} %all_to_all.16.got_ref, s32[1,1,16,256]{3,2,1,0:T(8,128)S(1)} %copy-done.4, f32[128,128]{1,0:T(8,128)S(1)} %copy-done.2), custom_call_target="tpu_custom_call" | custom-call | tf_op jit(solution)/shard_map/owner/pallas_call | solution.py:223
  (2 shorter events, 0.0 us)
Async XLA Ops:
  0.6 64.3 %copy-start = (s32[1,8,16,256]{3,2,1,0:T(8,128)S(1)}, s32[1,8,16,256]{3,2,1,0:T(8,128)}, u32[]{:S(2)}) copy-start(s32[1,8,16,256]{3,2,1,0:T(8,128)} %param.13) | copy-start | bytes 393220
  0.6 1.5 %copy-start.5 = (s32[8,16384]{1,0:T(8,128)S(1)}, s32[8,16384]{1,0:T(8,128)}, u32[]{:S(2)}) copy-start(s32[8,16384]{1,0:T(8,128)} %param.9) | copy-start | bytes 1572868
  0.7 5.3 %copy-start.1 = (f32[16384]{0:T(1024)S(1)}, f32[16384]{0:T(1024)}, u32[]{:S(2)}) copy-start(f32[16384]{0:T(1024)} %param.10) | copy-start | bytes 196612
  2.0 3.9 %collective-permute-start = (f32[24,18560]{1,0:T(8,128)S(1)}, f32[24,18560]{1,0:T(8,128)}, u32[]{:S(2)}, u32[]{:S(2)}) collective-permute-start(f32[24,18560]{1,0:T(8,128)S(1)} %pad_convert_fusion.own_ref), channel_id=1, source_target_pairs={{0,16},{16,0},{32,48},{48,32},{64,80},{80,64},{96,112},{112,96},{1... | collective-permute-start | bytes 5345288 | tf_op jit(solution)/shard_map/ppermute | solution.py:186
  53.1 0.6 copy-start.3
  53.8 20.6 %all-to-all-start = ((f32[128,1,64]{2,1,0:T(1,128)}), f32[128,1,64]{2,1,0:T(1,128)S(1)}, u32[]{:S(2)}, u32[]{:S(2)}) async-start(f32[128,1,64]{2,1,0:T(1,128)} %bitcast.28), calls=%async_computation | async-start | bytes 131072 | tf_op jit(solution)/shard_map/all_to_all | solution.py:205
  92.2 0.8 copy-start.2
  93.0 0.7 copy-start.4

commit v5 on v4

--- a/solution.py
+++ b/solution.py
@@ -14,7 +14,7 @@
 LANES = 128
 BLOCK = 2048
 FILL = 29
-UNROLL = 64
+UNROLL = 128
 ROWS = 16
 F32 = jnp.float32
 BF16 = jnp.bfloat16
@@ -23,39 +23,39 @@
 def energy_kernel(place_ref, links_ref, own_ref, other_ref, weight_ref, density_ref, out_ref, parts_ref, table, rows, *rest):
     links, sem = rest[:8], rest[8]
     elements = links_ref.shape[0] // 8
-    copies = []
-    for c in range(8):
-        for q in range(4):
-            start = pl.multiple_of(c * elements + place_ref[q] * BLOCK, BLOCK)
-            copies.append(
-                pltpu.make_async_copy(
-                    links_ref.at[pl.ds(start, BLOCK)], links[c].at[pl.ds(q * BLOCK, BLOCK)], sem.at[c, q]
-                )
-            )
-            copies[-1].start()
-
-    pad = jnp.zeros((ROWS, LANES), F32)
+
+    def link_copy(c, q):
+        start = pl.multiple_of(c * elements + place_ref[q] * BLOCK, BLOCK)
+        there = links[c].at[pl.ds(pl.multiple_of(q * BLOCK, BLOCK), BLOCK)]
+        return pltpu.make_async_copy(links_ref.at[pl.ds(start, BLOCK)], there, sem.at[c, q])
+
+    for q in range(4):
+        for c in range(8):
+            link_copy(c, q).start()
+
+    row = lax.broadcasted_iota(jnp.int32, (LANES // 2, LANES), 0)
+    lane = lax.broadcasted_iota(jnp.int32, (LANES // 2, LANES), 1)
+    twice = jnp.where(row == lane % (LANES // 2), 1.0, 0.0).astype(BF16)
 
     def fill(n, _):
-        start = pl.multiple_of(n * (FILL * LANES), LANES)
-        for i in range(FILL):
-            at = pl.ds(start + i * LANES, LANES)
-            own, other = own_ref[:, at], other_ref[:, at]
-            half = []
-            for k in range(3):
-                half += [own[8 * k : 8 * k + 8], other[8 * k : 8 * k + 8]]
-            half.append(pad)
-            table[at, :] = jnp.concatenate(half + half, axis=0).T
+        at = pl.ds(pl.multiple_of(n * (FILL * LANES), LANES), FILL * LANES)
+        own, other = own_ref[:, at], other_ref[:, at]
+        half = []
+        for k in range(3):
+            half += [own[8 * k : 8 * k + 8], other[8 * k : 8 * k + 8]]
+        half = jnp.concatenate(half + [jnp.zeros((ROWS, FILL * LANES), F32)], axis=0).astype(BF16)
+        table[at, :] = lax.dot_general(half, twice, (((0,), (0,)), ((), ())), preferred_element_type=F32)
         return 0
 
     lax.fori_loop(0, table.shape[0] // (FILL * LANES), fill, 0)
-    for copy in copies:
-        copy.wait()
 
     first_half = lax.broadcasted_iota(jnp.int32, (1, LANES), 1) < LANES // 2
     reach = 4 * BLOCK - UNROLL
 
     def group(q, acc):
+        for c in range(8):
+            link_copy(c, q).wait()
+
         def gather(t, _):
             start = pl.multiple_of(t * UNROLL, UNROLL)
             view = rows.at[pl.ds(start, UNROLL)]
@@ -96,6 +96,17 @@
 def split(x):
     high = x.astype(BF16)
     return high, (x - high.astype(F32)).astype(BF16)
+
+
+def prepare_kernel(cells_ref, filter_in, _, hot_ref, mine_ref, filter_ref):
+    filter_ref[...] = filter_in[...]
+    sources, width = cells_ref.shape[2:]
+    low_id = lax.broadcasted_iota(jnp.int32, (LANES, width), 0)
+    high_id = lax.broadcasted_iota(jnp.int32, (16, width), 0)
+    for j in range(sources):
+        cell = cells_ref[0, 0, j : j + 1, :]
+        hot_ref[j] = jnp.where(low_id == (cell & (LANES - 1)), 1.0, 0.0).astype(BF16)
+        mine_ref[j] = jnp.where(high_id == (cell >> 7), 1.0, 0.0)
 
 
 def send_kernel(elements, place_ref, count_ref, parts_ref, energy_ref, density_ref, picks_ref, comp_ref, out_ref):
@@ -132,24 +143,19 @@
                     out_ref[q * dests + d, r : r + 1, :] = got[:, p * LANES : (p + 1) * LANES]
 
 
-def owner_kernel(got_ref, cells_ref, filter_ref, sens_ref, energy_ref):
-    sources, width = cells_ref.shape[2], cells_ref.shape[3]
-    low_id = lax.broadcasted_iota(jnp.int32, (LANES, width), 0)
-    high_id = lax.broadcasted_iota(jnp.int32, (16, width), 0)
+def owner_kernel(got_ref, hot_ref, mine_ref, filter_ref, sens_ref, energy_ref):
+    sources = hot_ref.shape[0]
     node = jnp.zeros((64, LANES), F32)
     for j in range(sources):
-        cell = cells_ref[0, 0, j : j + 1, :]
-        hot = jnp.where(low_id == (cell & (LANES - 1)), 1.0, 0.0).astype(BF16)
-        mine = high_id == (cell >> 7)
         pieces = []
         share = got_ref[j]
         for q in range(1, 4):
             share = share + got_ref[q * sources + j]
         for f in range(2):
             value = jnp.concatenate([share[2 * f : 2 * f + 1], share[2 * f + 1 : 2 * f + 2]], axis=1)
-            pieces.append(jnp.where(mine, value, 0.0))
+            pieces.append(mine_ref[j] * value)
         rows = jnp.concatenate(split(jnp.concatenate(pieces, axis=0)), axis=0)
-        node = node + lax.dot_general(rows, hot, (((1,), (1,)), ((), ())), preferred_element_type=F32)
+        node = node + lax.dot_general(rows, hot_ref[j], (((1,), (1,)), ((), ())), preferred_element_type=F32)
     node = node[:32] + node[32:]
     result = lax.dot_general(
         node, filter_ref[...], (((1,), (1,)), ((), ())),
@@ -205,6 +211,20 @@
     parts = lax.all_to_all(mine, ("sample", "space"), split_axis=0, concat_axis=0, tiled=True)
     dests, width = send_rows.shape[-2:]
     picks = lax.dynamic_index_in_dim(send_rows.reshape(4, 2, dests, width), core, 1, keepdims=False)
+    small = pltpu.CompilerParams(vmem_limit_bytes=8 * 2**20)
+    cell_hot, cell_mine, near_filter = pl.pallas_call(
+        prepare_kernel,
+        in_specs=[whole, whole, pl.BlockSpec(memory_space=pl.ANY)],
+        out_specs=[whole] * 3,
+        out_shape=[
+            jax.ShapeDtypeStruct((dests, LANES, width), BF16),
+            jax.ShapeDtypeStruct((dests, 16, width), F32),
+            jax.ShapeDtypeStruct(filter_inverse.shape, F32),
+        ],
+        compiler_params=small,
+        cost_estimate=pl.CostEstimate(flops=4 * 10**9, bytes_accessed=2**21, transcendentals=0),
+        name="prepare",
+    )(recv_cell, filter_inverse, energies)
     compliance, outgoing = pl.pallas_call(
         functools.partial(send_kernel, float(elements * slabs)),
         in_specs=[smem, smem] + [whole] * 4,
@@ -213,7 +233,7 @@
             jax.ShapeDtypeStruct((1, 64), F32),
             jax.ShapeDtypeStruct((4 * dests, 2 * width // LANES, LANES), F32),
         ],
-        compiler_params=pltpu.CompilerParams(vmem_limit_bytes=8 * 2**20),
+        compiler_params=small,
         name="send",
     )(place, send_count.reshape(-1), parts, energies, rho, picks)
     peers = [[i * slabs + j for i in range(c, groups, 2) for j in range(slabs)] for c in range(2)]
@@ -222,12 +242,12 @@
     )
     sens, energy = pl.pallas_call(
         owner_kernel,
-        in_specs=[whole] * 3,
+        in_specs=[whole] * 4,
         out_specs=[whole] * 2,
         out_shape=[jax.ShapeDtypeStruct((1, 1, sub_rows), F32)] * 2,
-        compiler_params=pltpu.CompilerParams(vmem_limit_bytes=8 * 2**20),
+        compiler_params=small,
         name="owner",
-    )(got, recv_cell, filter_inverse)
+    )(got, cell_hot, cell_mine, near_filter)
     return (compliance.reshape(-1), sens, energy)
 
 

time: 95.6 us -> 91.9 us (0.961)
  blocking collectives: 14.6 us -> 0 us
  waiting for transfers between devices: 11 us -> 19.2 us
  starting transfers between devices: 11.2 us -> 16.2 us
  Pallas kernels: 51.8 us -> 49.7 us
    all_to_all x1 -> x0, blocking collectives: 14.6 us -> none  [body(): lax.all_to_all(outgoing, ('sample', 'space'), split_axis=0, concat_axis=0...]
    all_to_all x0 -> x1, waiting for transfers between devices: none -> 8.15 us  [body(): lax.all_to_all(outgoing, ('sample', 'space'), split_axis=0, concat_axis=0...]
    all_to_all x0 -> x1, starting transfers between devices: none -> 4.94 us  [body(): lax.all_to_all(outgoing, ('sample', 'space'), split_axis=0, concat_axis=0...]
    pallas_call x1, Pallas kernels: 47.2 us -> 44.6 us  [body(): pl.pallas_call(energy_kernel, in_specs=[smem, pl.BlockSpec(memory_space=p...]
  transfers between devices with their start and end apart: 2 -> 3, of which waited for: 2 -> 3; matrix products, arithmetic and copies ran while one was open for 2% -> 2% of each run, Pallas kernels for 0% -> 0%
where the time goes in v5:
time: 91.9 us; the launch traced here: 91.5 us
  Pallas kernels  49.7 us (54%)
  waiting for transfers between devices  19.2 us (21%)
  starting transfers between devices  16.2 us (18%)
  local copies, waits for them, and re-layouts  3.15 us (3%)
  other arithmetic  1.36 us (1%)
  matrix products  1.23 us (1%)
    pallas_call x1, Pallas kernels, body(): pl.pallas_call(energy_kernel, in_specs=[smem, pl.BlockSpec(memory_space=p...  44.6 us
    all_to_all x1, starting transfers between devices, body(): lax.all_to_all(mine, ('sample', 'space'), split_axis=0, concat_axis=0, ti...  11.1 us
    all_to_all x1, waiting for transfers between devices, body(): lax.all_to_all(mine, ('sample', 'space'), split_axis=0, concat_axis=0, ti...  8.67 us
    all_to_all x1, waiting for transfers between devices, body(): lax.all_to_all(outgoing, ('sample', 'space'), split_axis=0, concat_axis=0...  8.15 us
    all_to_all x1, starting transfers between devices, body(): lax.all_to_all(outgoing, ('sample', 'space'), split_axis=0, concat_axis=0...  4.94 us
    pallas_call x1, Pallas kernels, body(): pl.pallas_call(functools.partial(send_kernel, float(elements * slabs)), i...  3.38 us
    ppermute x1, waiting for transfers between devices, body(): other = lax.ppermute(own, 'sample', [(i, i ^ 1) for i in range(8)])  2.35 us
    unnamed x13, local copies, waits for them, and re-layouts  2.28 us
  transfers between devices with their start and end apart: 3, of which 3 were waited for; matrix products, arithmetic and copies ran while one was open for 2% of the time, Pallas kernels for 0%

profile of v5, /device:TPU:0, one launch (start us, length us, event | category | flops | bytes accessed | tf_op | source)
XLA Modules:
  0.0 91.5 jit_solution(8207323229607189975)
XLA Ops:
  0.6 0.0 copy-start
  0.6 0.0 copy-start.5
  0.7 0.0 copy-start.1
  0.7 1.4 %pad_convert_fusion.own_ref = f32[24,18560]{1,0:T(8,128)S(1)} fusion(bf16[24,18513]{1,0:T(8,128)(2,1)} %bitcast.29), kind=kLoop, calls=%fused_computation.3 | loop fusion | flops 445440 | bytes 2670384 | tf_op jit(solution)/shard_map/jit(_pad)/pad | solution.py:191
  2.0 0.1 collective-permute-start
  2.1 0.0 copy-done.5
  2.1 0.1 copy.15
  2.3 0.1 stack.27.place_ref
  2.4 1.2 %fusion.weight_ref = bf16[512,512]{1,0:T(8,128)(2,1)S(1)} fusion(bf16[24,24]{1,0:T(8,128)(2,1)} %param.11, s32[512]{0:T(512)S(1)} %get-tuple-element.21, s32[512]{0:T(512)S(1)} %get-tuple-element.22), kind=kOutput, calls=%fused_computation.1 | convolution fusion | flops 13996032 | bytes 529536 | tf_op jit(solution)/shard_map/dot_general | solution.py:175
  3.6 2.3 %collective-permute-done.other_ref = f32[24,18560]{1,0:T(8,128)} collective-permute-done((f32[24,18560]{1,0:T(8,128)S(1)}, f32[24,18560]{1,0:T(8,128)}, u32[]{:S(2)}, u32[]{:S(2)}) %collective-permute-start) | collective-permute-done | bytes 1781792 | tf_op jit(solution)/shard_map/ppermute | solution.py:192
  5.9 0.0 copy-done.1
  5.9 44.6 %energy.1 = (f32[4,16,2048]{2,1,0:T(8,128)S(1)}, f32[128,64]{1,0:T(8,128)S(1)}) custom-call(s32[6]{0:T(128)S(1)} %stack.27.place_ref, s32[131072]{0:T(1024)S(1)} %bitcast.24, f32[24,18560]{1,0:T(8,128)S(1)} %pad_convert_fusion.own_ref, f32[24,18560]{1,0:T(8,128)} %collective-permute-done.other_ref, bf16[512,512]{1,0:T(8,128)(2,1)S(1)} %fusion.weight_ref, ...), custom_call_target="tpu_custom_call" | custom-call | tf_op jit(solution)/shard_map/energy/pallas_call | solution.py:200
  50.6 0.0 copy-start.2
  50.6 0.6 copy-done.2
  51.2 11.1 %all-to-all-start = ((f32[128,1,64]{2,1,0:T(1,128)}), f32[128,1,64]{2,1,0:T(1,128)S(1)}, u32[]{:S(2)}, u32[]{:S(2)}) async-start(f32[128,1,64]{2,1,0:T(1,128)} %bitcast.28), calls=%async_computation | async-start | bytes 131072 | tf_op jit(solution)/shard_map/all_to_all | solution.py:211
  62.4 0.0 copy-done
  62.4 0.8 reshape.107.count_ref
  63.2 8.7 %all-to-all-done = f32[128,1,64]{2,1,0:T(1,128)S(1)} async-done(((f32[128,1,64]{2,1,0:T(1,128)}), f32[128,1,64]{2,1,0:T(1,128)S(1)}, u32[]{:S(2)}, u32[]{:S(2)}) %all-to-all-start) | async-done | bytes 32800 | tf_op jit(solution)/shard_map/all_to_all | solution.py:211
  71.8 3.4 %send.1 = (f32[1,64]{1,0:T(1,128)}, f32[64,4,128]{2,1,0:T(4,128)}) custom-call(s32[6]{0:T(128)S(1)} %stack.27.place_ref, s32[128]{0:T(128)S(1)} %reshape.107.count_ref, f32[128,64]{1,0:T(8,128)S(1)} %bitcast.27, f32[4,16,2048]{2,1,0:T(8,128)S(1)} %get-tuple-element.13.energy_ref._, f32[8,1,2048]{2,1,0:T(1,128)S(1)} %bitcast.26, ...), custom_call_target="tpu_custom_call" | custom-call | tf_op jit(solution)/shard_map/send/pallas_call | solution.py:228
  75.2 4.9 %all-to-all-start.1 = ((f32[64,4,128]{2,1,0:T(4,128)}), f32[64,4,128]{2,1,0:T(4,128)S(1)}, u32[]{:S(2)}, u32[]{:S(2)}) async-start(f32[64,4,128]{2,1,0:T(4,128)} %get-tuple-element.15), calls=%async_computation.1 | async-start | bytes 262144 | tf_op jit(solution)/shard_map/all_to_all | solution.py:240
  80.2 0.0 copy-start.3
  80.2 0.8 copy-done.3
  81.0 0.0 copy-start.4
  81.0 0.7 copy-done.4
  81.7 0.2 prepare.1
  81.9 8.2 %all-to-all-done.1.got_ref = f32[64,4,128]{2,1,0:T(4,128)S(1)} async-done(((f32[64,4,128]{2,1,0:T(4,128)}), f32[64,4,128]{2,1,0:T(4,128)S(1)}, u32[]{:S(2)}, u32[]{:S(2)}) %all-to-all-start.1) | async-done | bytes 131104 | tf_op jit(solution)/shard_map/all_to_all | solution.py:240
  90.1 1.4 %owner.1 = (f32[1,1,2048]{2,1,0:T(1,128)}, f32[1,1,2048]{2,1,0:T(1,128)}) custom-call(f32[64,4,128]{2,1,0:T(4,128)S(1)} %all-to-all-done.1.got_ref, bf16[16,128,256]{2,1,0:T(8,128)(2,1)S(1)} %get-tuple-element.16.hot_ref, f32[16,16,256]{2,1,0:T(8,128)S(1)} %get-tuple-element.17.mine_ref, f32[128,128]{1,0:T(8,128)S(1)} %get-tuple-element.18.filter_ref), custom_call_target="tpu_custom_call" | custom-call | tf_op jit(solution)/shard_map/owner/pallas_call | solution.py:243
  (2 shorter events, 0.0 us)
Async XLA Ops:
  0.6 61.7 %copy-start = (s32[1,8,16,256]{3,2,1,0:T(8,128)S(1)}, s32[1,8,16,256]{3,2,1,0:T(8,128)}, u32[]{:S(2)}) copy-start(s32[1,8,16,256]{3,2,1,0:T(8,128)} %param.13) | copy-start | bytes 393220
  0.6 1.5 %copy-start.5 = (s32[8,16384]{1,0:T(8,128)S(1)}, s32[8,16384]{1,0:T(8,128)}, u32[]{:S(2)}) copy-start(s32[8,16384]{1,0:T(8,128)} %param.9) | copy-start | bytes 1572868
  0.7 5.3 %copy-start.1 = (f32[16384]{0:T(1024)S(1)}, f32[16384]{0:T(1024)}, u32[]{:S(2)}) copy-start(f32[16384]{0:T(1024)} %param.10) | copy-start | bytes 196612
  2.0 3.9 %collective-permute-start = (f32[24,18560]{1,0:T(8,128)S(1)}, f32[24,18560]{1,0:T(8,128)}, u32[]{:S(2)}, u32[]{:S(2)}) collective-permute-start(f32[24,18560]{1,0:T(8,128)S(1)} %pad_convert_fusion.own_ref), channel_id=1, source_target_pairs={{0,16},{16,0},{32,48},{48,32},{64,80},{80,64},{96,112},{112,96},{1... | collective-permute-start | bytes 5345288 | tf_op jit(solution)/shard_map/ppermute | solution.py:192
  50.6 0.6 copy-start.2
  51.2 20.6 %all-to-all-start = ((f32[128,1,64]{2,1,0:T(1,128)}), f32[128,1,64]{2,1,0:T(1,128)S(1)}, u32[]{:S(2)}, u32[]{:S(2)}) async-start(f32[128,1,64]{2,1,0:T(1,128)} %bitcast.28), calls=%async_computation | async-start | bytes 131072 | tf_op jit(solution)/shard_map/all_to_all | solution.py:211
  75.2 14.9 %all-to-all-start.1 = ((f32[64,4,128]{2,1,0:T(4,128)}), f32[64,4,128]{2,1,0:T(4,128)S(1)}, u32[]{:S(2)}, u32[]{:S(2)}) async-start(f32[64,4,128]{2,1,0:T(4,128)} %get-tuple-element.15), calls=%async_computation.1 | async-start | bytes 262144 | tf_op jit(solution)/shard_map/all_to_all | solution.py:240
  80.2 0.8 copy-start.3
  81.0 0.7 copy-start.4

commit v6 on v5

--- a/solution.py
+++ b/solution.py
@@ -120,7 +120,8 @@
     spot = jnp.where(row_id < 8, place_ref[4] * 8 + row_id, place_ref[5] * 8 + row_id - 8)
     column = jnp.sum(jnp.where(lane == spot, weight, 0.0), axis=1, keepdims=True)
     _, dests, width = picks_ref.shape
-    low_id = lax.broadcasted_iota(jnp.int32, (LANES, width), 0)
+    low_id = lax.broadcasted_iota(jnp.int32, (LANES, width), 0).astype(jnp.int16)
+    one, zero = jnp.ones((LANES, width), BF16), jnp.zeros((LANES, width), BF16)
     high_id = lax.broadcasted_iota(jnp.int32, (16, width), 0)
     slot = lax.broadcasted_iota(jnp.int32, (16, width), 1)
     for q in range(4):
@@ -132,7 +133,7 @@
         table = jnp.concatenate(split(jnp.concatenate(both, axis=0)), axis=0)
         for d in range(dests):
             pick = picks_ref[q, d : d + 1, :]
-            hot = jnp.where(low_id == (pick & (LANES - 1)), 1.0, 0.0).astype(BF16)
+            hot = jnp.where(low_id == (pick & (LANES - 1)).astype(jnp.int16), one, zero)
             found = jnp.dot(table, hot, preferred_element_type=F32)
             found = found[:32] + found[32:]
             live = (high_id == (pick >> 7)) & (slot < count_ref[place_ref[q] * 16 + d])

time: 91.9 us -> 91.1 us (level)
  no operation moved by 1% of the time
where the time goes in v6:
time: 91.1 us; the launch traced here: 90.7 us
  Pallas kernels  48.8 us (54%)
  waiting for transfers between devices  19.2 us (21%)
  starting transfers between devices  16.2 us (18%)
  local copies, waits for them, and re-layouts  3.15 us (3%)
  other arithmetic  1.36 us (1%)
  matrix products  1.23 us (1%)
    pallas_call x1, Pallas kernels, body(): pl.pallas_call(energy_kernel, in_specs=[smem, pl.BlockSpec(memory_space=p...  44.6 us
    all_to_all x1, starting transfers between devices, body(): lax.all_to_all(mine, ('sample', 'space'), split_axis=0, concat_axis=0, ti...  11.1 us
    all_to_all x1, waiting for transfers between devices, body(): lax.all_to_all(mine, ('sample', 'space'), split_axis=0, concat_axis=0, ti...  8.67 us
    all_to_all x1, waiting for transfers between devices, body(): lax.all_to_all(outgoing, ('sample', 'space'), split_axis=0, concat_axis=0...  8.15 us
    all_to_all x1, starting transfers between devices, body(): lax.all_to_all(outgoing, ('sample', 'space'), split_axis=0, concat_axis=0...  4.95 us
    pallas_call x1, Pallas kernels, body(): pl.pallas_call(functools.partial(send_kernel, float(elements * slabs)), i...  2.5 us
    ppermute x1, waiting for transfers between devices, body(): other = lax.ppermute(own, 'sample', [(i, i ^ 1) for i in range(8)])  2.35 us
    unnamed x13, local copies, waits for them, and re-layouts  2.28 us
  transfers between devices with their start and end apart: 3, of which 3 were waited for; matrix products, arithmetic and copies ran while one was open for 2% of the time, Pallas kernels for 0%

profile of v6, /device:TPU:0, one launch (start us, length us, event | category | flops | bytes accessed | tf_op | source)
XLA Modules:
  0.0 90.7 jit_solution(16896391140417245340)
XLA Ops:
  0.6 0.0 copy-start
  0.6 0.0 copy-start.5
  0.7 0.0 copy-start.1
  0.7 1.4 %pad_convert_fusion.own_ref = f32[24,18560]{1,0:T(8,128)S(1)} fusion(bf16[24,18513]{1,0:T(8,128)(2,1)} %bitcast.29), kind=kLoop, calls=%fused_computation.3 | loop fusion | flops 445440 | bytes 2670384 | tf_op jit(solution)/shard_map/jit(_pad)/pad | solution.py:192
  2.0 0.1 collective-permute-start
  2.1 0.0 copy-done.5
  2.1 0.1 copy.15
  2.3 0.1 stack.27.place_ref
  2.4 1.2 %fusion.weight_ref = bf16[512,512]{1,0:T(8,128)(2,1)S(1)} fusion(bf16[24,24]{1,0:T(8,128)(2,1)} %param.11, s32[512]{0:T(512)S(1)} %get-tuple-element.21, s32[512]{0:T(512)S(1)} %get-tuple-element.22), kind=kOutput, calls=%fused_computation.1 | convolution fusion | flops 13996032 | bytes 529536 | tf_op jit(solution)/shard_map/dot_general | solution.py:176
  3.6 2.3 %collective-permute-done.other_ref = f32[24,18560]{1,0:T(8,128)} collective-permute-done((f32[24,18560]{1,0:T(8,128)S(1)}, f32[24,18560]{1,0:T(8,128)}, u32[]{:S(2)}, u32[]{:S(2)}) %collective-permute-start) | collective-permute-done | bytes 1781792 | tf_op jit(solution)/shard_map/ppermute | solution.py:193
  5.9 0.0 copy-done.1
  5.9 44.6 %energy.1 = (f32[4,16,2048]{2,1,0:T(8,128)S(1)}, f32[128,64]{1,0:T(8,128)S(1)}) custom-call(s32[6]{0:T(128)S(1)} %stack.27.place_ref, s32[131072]{0:T(1024)S(1)} %bitcast.24, f32[24,18560]{1,0:T(8,128)S(1)} %pad_convert_fusion.own_ref, f32[24,18560]{1,0:T(8,128)} %collective-permute-done.other_ref, bf16[512,512]{1,0:T(8,128)(2,1)S(1)} %fusion.weight_ref, ...), custom_call_target="tpu_custom_call" | custom-call | tf_op jit(solution)/shard_map/energy/pallas_call | solution.py:201
  50.6 0.0 copy-start.2
  50.6 0.6 copy-done.2
  51.2 11.1 %all-to-all-start = ((f32[128,1,64]{2,1,0:T(1,128)}), f32[128,1,64]{2,1,0:T(1,128)S(1)}, u32[]{:S(2)}, u32[]{:S(2)}) async-start(f32[128,1,64]{2,1,0:T(1,128)} %bitcast.28), calls=%async_computation | async-start | bytes 131072 | tf_op jit(solution)/shard_map/all_to_all | solution.py:212
  62.4 0.0 copy-done
  62.4 0.8 reshape.107.count_ref
  63.2 8.7 %all-to-all-done = f32[128,1,64]{2,1,0:T(1,128)S(1)} async-done(((f32[128,1,64]{2,1,0:T(1,128)}), f32[128,1,64]{2,1,0:T(1,128)S(1)}, u32[]{:S(2)}, u32[]{:S(2)}) %all-to-all-start) | async-done | bytes 32800 | tf_op jit(solution)/shard_map/all_to_all | solution.py:212
  71.8 2.5 %send.1 = (f32[1,64]{1,0:T(1,128)}, f32[64,4,128]{2,1,0:T(4,128)}) custom-call(s32[6]{0:T(128)S(1)} %stack.27.place_ref, s32[128]{0:T(128)S(1)} %reshape.107.count_ref, f32[128,64]{1,0:T(8,128)S(1)} %bitcast.27, f32[4,16,2048]{2,1,0:T(8,128)S(1)} %get-tuple-element.13.energy_ref._, f32[8,1,2048]{2,1,0:T(1,128)S(1)} %bitcast.26, ...), custom_call_target="tpu_custom_call" | custom-call | tf_op jit(solution)/shard_map/send/pallas_call | solution.py:229
  74.3 5.0 %all-to-all-start.1 = ((f32[64,4,128]{2,1,0:T(4,128)}), f32[64,4,128]{2,1,0:T(4,128)S(1)}, u32[]{:S(2)}, u32[]{:S(2)}) async-start(f32[64,4,128]{2,1,0:T(4,128)} %get-tuple-element.15), calls=%async_computation.1 | async-start | bytes 262144 | tf_op jit(solution)/shard_map/all_to_all | solution.py:241
  79.3 0.0 copy-start.3
  79.3 0.8 copy-done.3
  80.1 0.0 copy-start.4
  80.1 0.7 copy-done.4
  80.9 0.2 prepare.1
  81.1 8.2 %all-to-all-done.1.got_ref = f32[64,4,128]{2,1,0:T(4,128)S(1)} async-done(((f32[64,4,128]{2,1,0:T(4,128)}), f32[64,4,128]{2,1,0:T(4,128)S(1)}, u32[]{:S(2)}, u32[]{:S(2)}) %all-to-all-start.1) | async-done | bytes 131104 | tf_op jit(solution)/shard_map/all_to_all | solution.py:241
  89.2 1.4 %owner.1 = (f32[1,1,2048]{2,1,0:T(1,128)}, f32[1,1,2048]{2,1,0:T(1,128)}) custom-call(f32[64,4,128]{2,1,0:T(4,128)S(1)} %all-to-all-done.1.got_ref, bf16[16,128,256]{2,1,0:T(8,128)(2,1)S(1)} %get-tuple-element.16.hot_ref, f32[16,16,256]{2,1,0:T(8,128)S(1)} %get-tuple-element.17.mine_ref, f32[128,128]{1,0:T(8,128)S(1)} %get-tuple-element.18.filter_ref), custom_call_target="tpu_custom_call" | custom-call | tf_op jit(solution)/shard_map/owner/pallas_call | solution.py:244
  (2 shorter events, 0.0 us)
Async XLA Ops:
  0.6 61.7 %copy-start = (s32[1,8,16,256]{3,2,1,0:T(8,128)S(1)}, s32[1,8,16,256]{3,2,1,0:T(8,128)}, u32[]{:S(2)}) copy-start(s32[1,8,16,256]{3,2,1,0:T(8,128)} %param.13) | copy-start | bytes 393220
  0.6 1.5 %copy-start.5 = (s32[8,16384]{1,0:T(8,128)S(1)}, s32[8,16384]{1,0:T(8,128)}, u32[]{:S(2)}) copy-start(s32[8,16384]{1,0:T(8,128)} %param.9) | copy-start | bytes 1572868
  0.7 5.3 %copy-start.1 = (f32[16384]{0:T(1024)S(1)}, f32[16384]{0:T(1024)}, u32[]{:S(2)}) copy-start(f32[16384]{0:T(1024)} %param.10) | copy-start | bytes 196612
  2.0 3.9 %collective-permute-start = (f32[24,18560]{1,0:T(8,128)S(1)}, f32[24,18560]{1,0:T(8,128)}, u32[]{:S(2)}, u32[]{:S(2)}) collective-permute-start(f32[24,18560]{1,0:T(8,128)S(1)} %pad_convert_fusion.own_ref), channel_id=1, source_target_pairs={{0,16},{16,0},{32,48},{48,32},{64,80},{80,64},{96,112},{112,96},{1... | collective-permute-start | bytes 5345288 | tf_op jit(solution)/shard_map/ppermute | solution.py:193
  50.6 0.6 copy-start.2
  51.2 20.6 %all-to-all-start = ((f32[128,1,64]{2,1,0:T(1,128)}), f32[128,1,64]{2,1,0:T(1,128)S(1)}, u32[]{:S(2)}, u32[]{:S(2)}) async-start(f32[128,1,64]{2,1,0:T(1,128)} %bitcast.28), calls=%async_computation | async-start | bytes 131072 | tf_op jit(solution)/shard_map/all_to_all | solution.py:212
  74.3 14.9 %all-to-all-start.1 = ((f32[64,4,128]{2,1,0:T(4,128)}), f32[64,4,128]{2,1,0:T(4,128)S(1)}, u32[]{:S(2)}, u32[]{:S(2)}) async-start(f32[64,4,128]{2,1,0:T(4,128)} %get-tuple-element.15), calls=%async_computation.1 | async-start | bytes 262144 | tf_op jit(solution)/shard_map/all_to_all | solution.py:241
  79.3 0.8 copy-start.3
  80.1 0.7 copy-start.4

commit v7 on v6

--- a/solution.py
+++ b/solution.py
@@ -109,16 +109,20 @@
         mine_ref[j] = jnp.where(high_id == (cell >> 7), 1.0, 0.0)
 
 
-def send_kernel(elements, place_ref, count_ref, parts_ref, energy_ref, density_ref, picks_ref, comp_ref, out_ref):
+def send_kernel(elements, place_ref, count_ref, parts_ref, energy_ref, density_ref, picks_ref, out_ref):
     comp = jnp.sum(parts_ref[...], axis=0, keepdims=True) / elements
-    comp_ref[...] = comp
-    center = jnp.mean(comp, axis=1, keepdims=True)
-    spread = jnp.sqrt(jnp.mean((comp - center) ** 2, axis=1, keepdims=True) + epsilon)
-    weight = (1.0 + spread_weight * (comp - center) / spread) / 64.0
+    lane = lax.broadcasted_iota(jnp.int32, (1, 64), 1)
+    near = jnp.sum(comp, axis=1, keepdims=True) / ROWS
+    away = jnp.where((lane >> 4) == (place_ref[4] >> 1), comp - near, 0.0)
+    scale = jnp.max(jnp.abs(away), axis=1, keepdims=True)
+    away = away / jnp.maximum(scale, 1e-30)
     row_id = lax.broadcasted_iota(jnp.int32, (ROWS, 64), 0)
-    lane = lax.broadcasted_iota(jnp.int32, (ROWS, 64), 1)
+    lanes = lax.broadcasted_iota(jnp.int32, (ROWS, 64), 1)
     spot = jnp.where(row_id < 8, place_ref[4] * 8 + row_id, place_ref[5] * 8 + row_id - 8)
-    column = jnp.sum(jnp.where(lane == spot, weight, 0.0), axis=1, keepdims=True)
+    column = jnp.sum(jnp.where(lanes == spot, away, 0.0), axis=1, keepdims=True)
+    comp = jnp.concatenate([comp, jnp.zeros_like(comp)], axis=1)
+    wide = lax.broadcasted_iota(jnp.int32, (1, LANES), 1)
+    facts = jnp.concatenate([comp, jnp.where(wide < 64, near, scale)], axis=0)
     _, dests, width = picks_ref.shape
     low_id = lax.broadcasted_iota(jnp.int32, (LANES, width), 0).astype(jnp.int16)
     one, zero = jnp.ones((LANES, width), BF16), jnp.zeros((LANES, width), BF16)
@@ -127,33 +131,46 @@
     for q in range(4):
         energy = energy_ref[q]
         rho = density_ref[place_ref[q]]
-        sens = -penalty * rho * rho * jnp.sum(column * energy, axis=0, keepdims=True)
-        mean = jnp.sum(energy, axis=0, keepdims=True) / 64.0
-        both = [f[:, h * LANES : (h + 1) * LANES] for f in (sens, mean) for h in range(16)]
+        total = jnp.sum(energy, axis=0, keepdims=True) / 64.0
+        tilted = jnp.sum(column * energy, axis=0, keepdims=True) / 64.0
+        slope = -penalty * rho * rho
+        both = [f[:, h * LANES : (h + 1) * LANES] for f in (slope * total, slope * tilted, total) for h in range(16)]
         table = jnp.concatenate(split(jnp.concatenate(both, axis=0)), axis=0)
         for d in range(dests):
             pick = picks_ref[q, d : d + 1, :]
             hot = jnp.where(low_id == (pick & (LANES - 1)).astype(jnp.int16), one, zero)
             found = jnp.dot(table, hot, preferred_element_type=F32)
-            found = found[:32] + found[32:]
+            found = found[:48] + found[48:]
             live = (high_id == (pick >> 7)) & (slot < count_ref[place_ref[q] * 16 + d])
-            for f in range(2):
+            for f in range(3):
                 got = jnp.sum(jnp.where(live, found[16 * f : 16 * f + 16], 0.0), axis=0, keepdims=True)
                 for p in range(width // LANES):
                     r = f * (width // LANES) + p
                     out_ref[q * dests + d, r : r + 1, :] = got[:, p * LANES : (p + 1) * LANES]
-
-
-def owner_kernel(got_ref, hot_ref, mine_ref, filter_ref, sens_ref, energy_ref):
+            out_ref[q * dests + d, 6:8, :] = facts
+
+
+def owner_kernel(got_ref, hot_ref, mine_ref, filter_ref, comp_ref, sens_ref, energy_ref):
     sources = hot_ref.shape[0]
+    facts = [got_ref[q * sources, 6:8, :] for q in range(4)]
+    comp = (facts[0] + facts[1] + facts[2] + facts[3])[:1, :64]
+    comp_ref[...] = comp
+    center = jnp.mean(comp, axis=1, keepdims=True)
+    spread = jnp.sqrt(jnp.mean((comp - center) ** 2, axis=1, keepdims=True) + epsilon)
+    row_id = lax.broadcasted_iota(jnp.int32, (8, LANES), 0)
+    factors = []
+    for q in range(4):
+        near, scale = facts[q][1:2, :1], facts[q][1:2, 64:65]
+        plain = 1.0 + spread_weight * (near - center) / spread
+        factors.append(jnp.where(row_id < 2, plain, jnp.where(row_id < 4, spread_weight * (scale / spread), 1.0)))
     node = jnp.zeros((64, LANES), F32)
     for j in range(sources):
+        share = factors[0] * got_ref[j]
+        for q in range(1, 4):
+            share = share + factors[q] * got_ref[q * sources + j]
         pieces = []
-        share = got_ref[j]
-        for q in range(1, 4):
-            share = share + got_ref[q * sources + j]
-        for f in range(2):
-            value = jnp.concatenate([share[2 * f : 2 * f + 1], share[2 * f + 1 : 2 * f + 2]], axis=1)
+        for value in (share[0:2] + share[2:4], share[4:6]):
+            value = jnp.concatenate([value[0:1], value[1:2]], axis=1)
             pieces.append(mine_ref[j] * value)
         rows = jnp.concatenate(split(jnp.concatenate(pieces, axis=0)), axis=0)
         node = node + lax.dot_general(rows, hot_ref[j], (((1,), (1,)), ((), ())), preferred_element_type=F32)
@@ -202,14 +219,15 @@
         energy_kernel,
         in_specs=[smem, pl.BlockSpec(memory_space=pl.ANY)] + [whole] * 4,
         out_specs=[whole] * 2,
-        out_shape=[jax.ShapeDtypeStruct((4, ROWS, sub_rows), F32), jax.ShapeDtypeStruct((128, 64), F32)],
+        out_shape=[jax.ShapeDtypeStruct((4, ROWS, sub_rows), F32), jax.ShapeDtypeStruct((2 * slabs, 64), F32)],
         scratch_shapes=[pltpu.VMEM((nodes, LANES), F32), pltpu.VMEM((BLOCK, 4 * LANES), F32)]
         + [pltpu.SMEM((4 * BLOCK,), jnp.int32)] * 8
         + [pltpu.SemaphoreType.DMA((8, 4))],
         compiler_params=pltpu.CompilerParams(vmem_limit_bytes=30 * 2**20),
         name="energy",
     )(place, links, own, other, weights, rho)
-    parts = lax.all_to_all(mine, ("sample", "space"), split_axis=0, concat_axis=0, tiled=True)
+    chips = [[i * slabs + j for i in (c, c + 1) for j in range(slabs)] for c in range(0, groups, 2)]
+    parts = lax.all_to_all(mine, ("sample", "space"), split_axis=0, concat_axis=0, tiled=True, axis_index_groups=chips)
     dests, width = send_rows.shape[-2:]
     picks = lax.dynamic_index_in_dim(send_rows.reshape(4, 2, dests, width), core, 1, keepdims=False)
     small = pltpu.CompilerParams(vmem_limit_bytes=8 * 2**20)
@@ -226,14 +244,11 @@
         cost_estimate=pl.CostEstimate(flops=4 * 10**9, bytes_accessed=2**21, transcendentals=0),
         name="prepare",
     )(recv_cell, filter_inverse, energies)
-    compliance, outgoing = pl.pallas_call(
+    outgoing = pl.pallas_call(
         functools.partial(send_kernel, float(elements * slabs)),
         in_specs=[smem, smem] + [whole] * 4,
-        out_specs=[whole] * 2,
-        out_shape=[
-            jax.ShapeDtypeStruct((1, 64), F32),
-            jax.ShapeDtypeStruct((4 * dests, 2 * width // LANES, LANES), F32),
-        ],
+        out_specs=whole,
+        out_shape=jax.ShapeDtypeStruct((4 * dests, 8, LANES), F32),
         compiler_params=small,
         name="send",
     )(place, send_count.reshape(-1), parts, energies, rho, picks)
@@ -241,11 +256,11 @@
     got = lax.all_to_all(
         outgoing, ("sample", "space"), split_axis=0, concat_axis=0, tiled=True, axis_index_groups=peers
     )
-    sens, energy = pl.pallas_call(
+    compliance, sens, energy = pl.pallas_call(
         owner_kernel,
         in_specs=[whole] * 4,
-        out_specs=[whole] * 2,
-        out_shape=[jax.ShapeDtypeStruct((1, 1, sub_rows), F32)] * 2,
+        out_specs=[whole] * 3,
+        out_shape=[jax.ShapeDtypeStruct((1, 64), F32)] + [jax.ShapeDtypeStruct((1, 1, sub_rows), F32)] * 2,
         compiler_params=small,
         name="owner",
     )(got, cell_hot, cell_mine, near_filter)

time: 91.1 us -> 89.1 us (0.978)
  waiting for transfers between devices: 19.2 us -> 17.7 us
  starting transfers between devices: 16.2 us -> 15 us
    all_to_all x1, starting transfers between devices: 11.1 us -> 7.4 us  [body(): lax.all_to_all(mine, ('sample', 'space'), split_axis=0, concat_axis=0, ti...]
    all_to_all x1, starting transfers between devices: 4.95 us -> 7.54 us  [body(): lax.all_to_all(outgoing, ('sample', 'space'), split_axis=0, concat_axis=0...]
    all_to_all x1, waiting for transfers between devices: 8.67 us -> 6.54 us  [body(): lax.all_to_all(mine, ('sample', 'space'), split_axis=0, concat_axis=0, ti...]
where the time goes in v7:
time: 89.1 us; the launch traced here: 88.6 us
  Pallas kernels  49.3 us (55%)
  waiting for transfers between devices  17.7 us (20%)
  starting transfers between devices  15 us (17%)
  local copies, waits for them, and re-layouts  3.13 us (4%)
  other arithmetic  1.36 us (2%)
  matrix products  1.23 us (1%)
    pallas_call x1, Pallas kernels, body(): pl.pallas_call(energy_kernel, in_specs=[smem, pl.BlockSpec(memory_space=p...  44.7 us
    all_to_all x1, waiting for transfers between devices, body(): lax.all_to_all(outgoing, ('sample', 'space'), split_axis=0, concat_axis=0...  8.85 us
    all_to_all x1, starting transfers between devices, body(): lax.all_to_all(outgoing, ('sample', 'space'), split_axis=0, concat_axis=0...  7.54 us
    all_to_all x1, starting transfers between devices, body(): lax.all_to_all(mine, ('sample', 'space'), split_axis=0, concat_axis=0, ti...  7.4 us
    all_to_all x1, waiting for transfers between devices, body(): lax.all_to_all(mine, ('sample', 'space'), split_axis=0, concat_axis=0, ti...  6.54 us
    pallas_call x1, Pallas kernels, body(): pl.pallas_call(functools.partial(send_kernel, float(elements * slabs)), i...  2.75 us
    ppermute x1, waiting for transfers between devices, body(): other = lax.ppermute(own, 'sample', [(i, i ^ 1) for i in range(8)])  2.35 us
    unnamed x13, local copies, waits for them, and re-layouts  2.26 us
  transfers between devices with their start and end apart: 3, of which 3 were waited for; matrix products, arithmetic and copies ran while one was open for 2% of the time, Pallas kernels for 0%

profile of v7, /device:TPU:0, one launch (start us, length us, event | category | flops | bytes accessed | tf_op | source)
XLA Modules:
  0.0 88.6 jit_solution(11907420881766536512)
XLA Ops:
  0.6 0.0 copy-start
  0.6 0.0 copy-start.5
  0.7 0.0 copy-start.1
  0.7 1.4 %pad_convert_fusion.own_ref = f32[24,18560]{1,0:T(8,128)S(1)} fusion(bf16[24,18513]{1,0:T(8,128)(2,1)} %bitcast.29), kind=kLoop, calls=%fused_computation.3 | loop fusion | flops 445440 | bytes 2670384 | tf_op jit(solution)/shard_map/jit(_pad)/pad | solution.py:209
  2.0 0.1 collective-permute-start
  2.1 0.0 copy-done.5
  2.1 0.1 copy.15
  2.3 0.1 stack.27.place_ref
  2.4 1.2 %fusion.weight_ref = bf16[512,512]{1,0:T(8,128)(2,1)S(1)} fusion(bf16[24,24]{1,0:T(8,128)(2,1)} %param.11, s32[512]{0:T(512)S(1)} %get-tuple-element.19, s32[512]{0:T(512)S(1)} %get-tuple-element.20), kind=kOutput, calls=%fused_computation.1 | convolution fusion | flops 13996032 | bytes 529536 | tf_op jit(solution)/shard_map/dot_general | solution.py:193
  3.6 2.3 %collective-permute-done.other_ref = f32[24,18560]{1,0:T(8,128)} collective-permute-done((f32[24,18560]{1,0:T(8,128)S(1)}, f32[24,18560]{1,0:T(8,128)}, u32[]{:S(2)}, u32[]{:S(2)}) %collective-permute-start) | collective-permute-done | bytes 1781792 | tf_op jit(solution)/shard_map/ppermute | solution.py:210
  5.9 0.0 copy-done.1
  5.9 44.7 %energy.1 = (f32[4,16,2048]{2,1,0:T(8,128)S(1)}, f32[32,64]{1,0:T(8,128)S(1)}) custom-call(s32[6]{0:T(128)S(1)} %stack.27.place_ref, s32[131072]{0:T(1024)S(1)} %bitcast.24, f32[24,18560]{1,0:T(8,128)S(1)} %pad_convert_fusion.own_ref, f32[24,18560]{1,0:T(8,128)} %collective-permute-done.other_ref, bf16[512,512]{1,0:T(8,128)(2,1)S(1)} %fusion.weight_ref, ...), custom_call_target="tpu_custom_call" | custom-call | tf_op jit(solution)/shard_map/energy/pallas_call | solution.py:218
  50.6 0.0 copy-start.2
  50.6 0.6 copy-done.2
  51.2 7.4 %all-to-all-start = ((f32[32,1,64]{2,1,0:T(1,128)}), f32[32,1,64]{2,1,0:T(1,128)S(1)}, u32[]{:S(2)}, u32[]{:S(2)}) async-start(f32[32,1,64]{2,1,0:T(1,128)} %bitcast.28), calls=%async_computation | async-start | bytes 32768 | tf_op jit(solution)/shard_map/all_to_all | solution.py:230
  58.6 0.0 copy-done
  58.7 0.8 reshape.107.count_ref
  59.4 6.5 %all-to-all-done = f32[32,1,64]{2,1,0:T(1,128)S(1)} async-done(((f32[32,1,64]{2,1,0:T(1,128)}), f32[32,1,64]{2,1,0:T(1,128)S(1)}, u32[]{:S(2)}, u32[]{:S(2)}) %all-to-all-start) | async-done | bytes 8224 | tf_op jit(solution)/shard_map/all_to_all | solution.py:230
  66.0 2.8 %send.1 = f32[64,8,128]{2,1,0:T(8,128)} custom-call(s32[6]{0:T(128)S(1)} %stack.27.place_ref, s32[128]{0:T(128)S(1)} %reshape.107.count_ref, f32[32,64]{1,0:T(8,128)S(1)} %bitcast.27, f32[4,16,2048]{2,1,0:T(8,128)S(1)} %get-tuple-element.12.energy_ref._, f32[8,1,2048]{2,1,0:T(1,128)S(1)} %bitcast.26, s32[4,16,256]{2,1,0:T(8,128)S(1)} %dynamic-slice_bitcast_fusion.picks_ref), custom_call_target="tpu_custom_call" | custom-call | tf_op jit(solution)/shard_map/send/pallas_call | solution.py:247
  68.7 7.5 %all-to-all-start.1 = ((f32[64,8,128]{2,1,0:T(8,128)}), f32[64,8,128]{2,1,0:T(8,128)S(1)}, u32[]{:S(2)}, u32[]{:S(2)}) async-start(f32[64,8,128]{2,1,0:T(8,128)} %send.1), calls=%async_computation.1 | async-start | bytes 524288 | tf_op jit(solution)/shard_map/all_to_all | solution.py:256
  76.3 0.0 copy-start.3
  76.3 0.8 copy-done.3
  77.1 0.0 copy-start.4
  77.1 0.7 copy-done.4
  77.8 0.2 prepare.1
  78.0 8.9 %all-to-all-done.1.got_ref = f32[64,8,128]{2,1,0:T(8,128)S(1)} async-done(((f32[64,8,128]{2,1,0:T(8,128)}), f32[64,8,128]{2,1,0:T(8,128)S(1)}, u32[]{:S(2)}, u32[]{:S(2)}) %all-to-all-start.1) | async-done | bytes 262176 | tf_op jit(solution)/shard_map/all_to_all | solution.py:256
  86.9 1.7 %owner.1 = (f32[1,64]{1,0:T(1,128)}, f32[1,1,2048]{2,1,0:T(1,128)}, f32[1,1,2048]{2,1,0:T(1,128)}) custom-call(f32[64,8,128]{2,1,0:T(8,128)S(1)} %all-to-all-done.1.got_ref, bf16[16,128,256]{2,1,0:T(8,128)(2,1)S(1)} %get-tuple-element.13.hot_ref, f32[16,16,256]{2,1,0:T(8,128)S(1)} %get-tuple-element.14.mine_ref, f32[128,128]{1,0:T(8,128)S(1)} %get-tuple-element.15.filter_ref), custom_call_target="tpu_custom_call" | custom-call | tf_op jit(solution)/shard_map/owner/pallas_call | solution.py:259
  (2 shorter events, 0.0 us)
Async XLA Ops:
  0.6 58.0 %copy-start = (s32[1,8,16,256]{3,2,1,0:T(8,128)S(1)}, s32[1,8,16,256]{3,2,1,0:T(8,128)}, u32[]{:S(2)}) copy-start(s32[1,8,16,256]{3,2,1,0:T(8,128)} %param.13) | copy-start | bytes 393220
  0.6 1.5 %copy-start.5 = (s32[8,16384]{1,0:T(8,128)S(1)}, s32[8,16384]{1,0:T(8,128)}, u32[]{:S(2)}) copy-start(s32[8,16384]{1,0:T(8,128)} %param.9) | copy-start | bytes 1572868
  0.7 5.3 %copy-start.1 = (f32[16384]{0:T(1024)S(1)}, f32[16384]{0:T(1024)}, u32[]{:S(2)}) copy-start(f32[16384]{0:T(1024)} %param.10) | copy-start | bytes 196612
  2.0 3.9 %collective-permute-start = (f32[24,18560]{1,0:T(8,128)S(1)}, f32[24,18560]{1,0:T(8,128)}, u32[]{:S(2)}, u32[]{:S(2)}) collective-permute-start(f32[24,18560]{1,0:T(8,128)S(1)} %pad_convert_fusion.own_ref), channel_id=1, source_target_pairs={{0,16},{16,0},{32,48},{48,32},{64,80},{80,64},{96,112},{112,96},{1... | collective-permute-start | bytes 5345288 | tf_op jit(solution)/shard_map/ppermute | solution.py:210
  50.6 0.6 copy-start.2
  51.2 14.8 %all-to-all-start = ((f32[32,1,64]{2,1,0:T(1,128)}), f32[32,1,64]{2,1,0:T(1,128)S(1)}, u32[]{:S(2)}, u32[]{:S(2)}) async-start(f32[32,1,64]{2,1,0:T(1,128)} %bitcast.28), calls=%async_computation | async-start | bytes 32768 | tf_op jit(solution)/shard_map/all_to_all | solution.py:230
  68.7 18.2 %all-to-all-start.1 = ((f32[64,8,128]{2,1,0:T(8,128)}), f32[64,8,128]{2,1,0:T(8,128)S(1)}, u32[]{:S(2)}, u32[]{:S(2)}) async-start(f32[64,8,128]{2,1,0:T(8,128)} %send.1), calls=%async_computation.1 | async-start | bytes 524288 | tf_op jit(solution)/shard_map/all_to_all | solution.py:256
  76.3 0.8 copy-start.3
  77.1 0.7 copy-start.4

commit v8 on v7

--- a/solution.py
+++ b/solution.py
@@ -50,7 +50,7 @@
     lax.fori_loop(0, table.shape[0] // (FILL * LANES), fill, 0)
 
     first_half = lax.broadcasted_iota(jnp.int32, (1, LANES), 1) < LANES // 2
-    reach = 4 * BLOCK - UNROLL
+    reach = 4 * BLOCK - UNROLL + 1
 
     def group(q, acc):
         for c in range(8):
@@ -99,14 +99,16 @@
 
 
 def prepare_kernel(cells_ref, filter_in, _, hot_ref, mine_ref, filter_ref):
-    filter_ref[...] = filter_in[...]
+    high, low = split(filter_in[...])
+    filter_ref[...] = jnp.concatenate([high, low, high], axis=1)
     sources, width = cells_ref.shape[2:]
     low_id = lax.broadcasted_iota(jnp.int32, (LANES, width), 0)
     high_id = lax.broadcasted_iota(jnp.int32, (16, width), 0)
     for j in range(sources):
         cell = cells_ref[0, 0, j : j + 1, :]
-        hot_ref[j] = jnp.where(low_id == (cell & (LANES - 1)), 1.0, 0.0).astype(BF16)
-        mine_ref[j] = jnp.where(high_id == (cell >> 7), 1.0, 0.0)
+        at = slice(j * width, (j + 1) * width)
+        hot_ref[:, at] = jnp.where(low_id == (cell & (LANES - 1)), 1.0, 0.0).astype(BF16)
+        mine_ref[:, at] = jnp.where(high_id == (cell >> 7), 1.0, 0.0)
 
 
 def send_kernel(elements, place_ref, count_ref, parts_ref, energy_ref, density_ref, picks_ref, out_ref):
@@ -151,7 +153,7 @@
 
 
 def owner_kernel(got_ref, hot_ref, mine_ref, filter_ref, comp_ref, sens_ref, energy_ref):
-    sources = hot_ref.shape[0]
+    sources = got_ref.shape[0] // 4
     facts = [got_ref[q * sources, 6:8, :] for q in range(4)]
     comp = (facts[0] + facts[1] + facts[2] + facts[3])[:1, :64]
     comp_ref[...] = comp
@@ -163,21 +165,23 @@
         near, scale = facts[q][1:2, :1], facts[q][1:2, 64:65]
         plain = 1.0 + spread_weight * (near - center) / spread
         factors.append(jnp.where(row_id < 2, plain, jnp.where(row_id < 4, spread_weight * (scale / spread), 1.0)))
-    node = jnp.zeros((64, LANES), F32)
+    sens, energy = [], []
     for j in range(sources):
         share = factors[0] * got_ref[j]
         for q in range(1, 4):
             share = share + factors[q] * got_ref[q * sources + j]
-        pieces = []
-        for value in (share[0:2] + share[2:4], share[4:6]):
-            value = jnp.concatenate([value[0:1], value[1:2]], axis=1)
-            pieces.append(mine_ref[j] * value)
-        rows = jnp.concatenate(split(jnp.concatenate(pieces, axis=0)), axis=0)
-        node = node + lax.dot_general(rows, hot_ref[j], (((1,), (1,)), ((), ())), preferred_element_type=F32)
+        value = share[0:2] + share[2:4]
+        sens += [value[0:1], value[1:2]]
+        energy += [share[4:5], share[5:6]]
+    mine = mine_ref[...]
+    rows = jnp.concatenate([mine * jnp.concatenate(field, axis=1) for field in (sens, energy)], axis=0)
+    rows = jnp.concatenate(split(rows), axis=0)
+    node = lax.dot_general(rows, hot_ref[...], (((1,), (1,)), ((), ())), preferred_element_type=F32)
     node = node[:32] + node[32:]
+    high, low = split(node)
     result = lax.dot_general(
-        node, filter_ref[...], (((1,), (1,)), ((), ())),
-        precision=lax.Precision.HIGHEST, preferred_element_type=F32,
+        jnp.concatenate([high, high, low], axis=1), filter_ref[...], (((1,), (1,)), ((), ())),
+        preferred_element_type=F32,
     )
     for p in range(16):
         sens_ref[0, :, p * LANES : (p + 1) * LANES] = result[p : p + 1]
@@ -236,9 +240,9 @@
         in_specs=[whole, whole, pl.BlockSpec(memory_space=pl.ANY)],
         out_specs=[whole] * 3,
         out_shape=[
-            jax.ShapeDtypeStruct((dests, LANES, width), BF16),
-            jax.ShapeDtypeStruct((dests, 16, width), F32),
-            jax.ShapeDtypeStruct(filter_inverse.shape, F32),
+            jax.ShapeDtypeStruct((LANES, dests * width), BF16),
+            jax.ShapeDtypeStruct((16, dests * width), F32),
+            jax.ShapeDtypeStruct((LANES, 3 * LANES), BF16),
         ],
         compiler_params=small,
         cost_estimate=pl.CostEstimate(flops=4 * 10**9, bytes_accessed=2**21, transcendentals=0),

time: 89.1 us -> 88.9 us (level)
  transfers between devices with their start and end apart: 3 -> 3, of which waited for: 3 -> 3; matrix products, arithmetic and copies ran while one was open for 2% -> 3% of each run, Pallas kernels for 0% -> 0%
where the time goes in v8:
time: 88.9 us; the launch traced here: 88.4 us
  Pallas kernels  49.2 us (55%)
  waiting for transfers between devices  17.7 us (20%)
  starting transfers between devices  15 us (17%)
  local copies, waits for them, and re-layouts  3.13 us (4%)
  other arithmetic  1.36 us (2%)
  matrix products  1.23 us (1%)
    pallas_call x1, Pallas kernels, body(): pl.pallas_call(energy_kernel, in_specs=[smem, pl.BlockSpec(memory_space=p...  44.7 us
    all_to_all x1, waiting for transfers between devices, body(): lax.all_to_all(outgoing, ('sample', 'space'), split_axis=0, concat_axis=0...  8.84 us
    all_to_all x1, starting transfers between devices, body(): lax.all_to_all(outgoing, ('sample', 'space'), split_axis=0, concat_axis=0...  7.54 us
    all_to_all x1, starting transfers between devices, body(): lax.all_to_all(mine, ('sample', 'space'), split_axis=0, concat_axis=0, ti...  7.41 us
    all_to_all x1, waiting for transfers between devices, body(): lax.all_to_all(mine, ('sample', 'space'), split_axis=0, concat_axis=0, ti...  6.54 us
    pallas_call x1, Pallas kernels, body(): pl.pallas_call(functools.partial(send_kernel, float(elements * slabs)), i...  2.75 us
    ppermute x1, waiting for transfers between devices, body(): other = lax.ppermute(own, 'sample', [(i, i ^ 1) for i in range(8)])  2.35 us
    unnamed x13, local copies, waits for them, and re-layouts  2.26 us
  transfers between devices with their start and end apart: 3, of which 3 were waited for; matrix products, arithmetic and copies ran while one was open for 3% of the time, Pallas kernels for 0%

profile of v8, /device:TPU:0, one launch (start us, length us, event | category | flops | bytes accessed | tf_op | source)
XLA Modules:
  0.0 88.4 jit_solution(8756401067509595989)
XLA Ops:
  0.6 0.0 copy-start
  0.6 0.0 copy-start.5
  0.7 0.0 copy-start.1
  0.7 1.4 %pad_convert_fusion.own_ref = f32[24,18560]{1,0:T(8,128)S(1)} fusion(bf16[24,18513]{1,0:T(8,128)(2,1)} %bitcast.29), kind=kLoop, calls=%fused_computation.3 | loop fusion | flops 445440 | bytes 2670384 | tf_op jit(solution)/shard_map/jit(_pad)/pad | solution.py:213
  2.0 0.1 collective-permute-start
  2.1 0.0 copy-done.5
  2.1 0.1 copy.15
  2.3 0.1 stack.27.place_ref
  2.4 1.2 %fusion.weight_ref = bf16[512,512]{1,0:T(8,128)(2,1)S(1)} fusion(bf16[24,24]{1,0:T(8,128)(2,1)} %param.11, s32[512]{0:T(512)S(1)} %get-tuple-element.19, s32[512]{0:T(512)S(1)} %get-tuple-element.20), kind=kOutput, calls=%fused_computation.1 | convolution fusion | flops 13996032 | bytes 529536 | tf_op jit(solution)/shard_map/dot_general | solution.py:197
  3.6 2.3 %collective-permute-done.other_ref = f32[24,18560]{1,0:T(8,128)} collective-permute-done((f32[24,18560]{1,0:T(8,128)S(1)}, f32[24,18560]{1,0:T(8,128)}, u32[]{:S(2)}, u32[]{:S(2)}) %collective-permute-start) | collective-permute-done | bytes 1781792 | tf_op jit(solution)/shard_map/ppermute | solution.py:214
  5.9 0.0 copy-done.1
  5.9 44.7 %energy.1 = (f32[4,16,2048]{2,1,0:T(8,128)S(1)}, f32[32,64]{1,0:T(8,128)S(1)}) custom-call(s32[6]{0:T(128)S(1)} %stack.27.place_ref, s32[131072]{0:T(1024)S(1)} %bitcast.24, f32[24,18560]{1,0:T(8,128)S(1)} %pad_convert_fusion.own_ref, f32[24,18560]{1,0:T(8,128)} %collective-permute-done.other_ref, bf16[512,512]{1,0:T(8,128)(2,1)S(1)} %fusion.weight_ref, ...), custom_call_target="tpu_custom_call" | custom-call | tf_op jit(solution)/shard_map/energy/pallas_call | solution.py:222
  50.6 0.0 copy-start.2
  50.6 0.6 copy-done.2
  51.2 7.4 %all-to-all-start = ((f32[32,1,64]{2,1,0:T(1,128)}), f32[32,1,64]{2,1,0:T(1,128)S(1)}, u32[]{:S(2)}, u32[]{:S(2)}) async-start(f32[32,1,64]{2,1,0:T(1,128)} %bitcast.28), calls=%async_computation | async-start | bytes 32768 | tf_op jit(solution)/shard_map/all_to_all | solution.py:234
  58.6 0.0 copy-done
  58.7 0.8 reshape.107.count_ref
  59.4 6.5 %all-to-all-done = f32[32,1,64]{2,1,0:T(1,128)S(1)} async-done(((f32[32,1,64]{2,1,0:T(1,128)}), f32[32,1,64]{2,1,0:T(1,128)S(1)}, u32[]{:S(2)}, u32[]{:S(2)}) %all-to-all-start) | async-done | bytes 8224 | tf_op jit(solution)/shard_map/all_to_all | solution.py:234
  66.0 2.8 %send.1 = f32[64,8,128]{2,1,0:T(8,128)} custom-call(s32[6]{0:T(128)S(1)} %stack.27.place_ref, s32[128]{0:T(128)S(1)} %reshape.107.count_ref, f32[32,64]{1,0:T(8,128)S(1)} %bitcast.27, f32[4,16,2048]{2,1,0:T(8,128)S(1)} %get-tuple-element.12.energy_ref._, f32[8,1,2048]{2,1,0:T(1,128)S(1)} %bitcast.26, s32[4,16,256]{2,1,0:T(8,128)S(1)} %dynamic-slice_bitcast_fusion.picks_ref), custom_call_target="tpu_custom_call" | custom-call | tf_op jit(solution)/shard_map/send/pallas_call | solution.py:251
  68.7 7.5 %all-to-all-start.1 = ((f32[64,8,128]{2,1,0:T(8,128)}), f32[64,8,128]{2,1,0:T(8,128)S(1)}, u32[]{:S(2)}, u32[]{:S(2)}) async-start(f32[64,8,128]{2,1,0:T(8,128)} %send.1), calls=%async_computation.1 | async-start | bytes 524288 | tf_op jit(solution)/shard_map/all_to_all | solution.py:260
  76.3 0.0 copy-start.3
  76.3 0.8 copy-done.3
  77.1 0.0 copy-start.4
  77.1 0.7 copy-done.4
  77.8 0.2 prepare.1
  78.1 8.8 %all-to-all-done.1.got_ref = f32[64,8,128]{2,1,0:T(8,128)S(1)} async-done(((f32[64,8,128]{2,1,0:T(8,128)}), f32[64,8,128]{2,1,0:T(8,128)S(1)}, u32[]{:S(2)}, u32[]{:S(2)}) %all-to-all-start.1) | async-done | bytes 262176 | tf_op jit(solution)/shard_map/all_to_all | solution.py:260
  86.9 1.5 %owner.1 = (f32[1,64]{1,0:T(1,128)}, f32[1,1,2048]{2,1,0:T(1,128)}, f32[1,1,2048]{2,1,0:T(1,128)}) custom-call(f32[64,8,128]{2,1,0:T(8,128)S(1)} %all-to-all-done.1.got_ref, bf16[128,4096]{1,0:T(8,128)(2,1)S(1)} %get-tuple-element.13.hot_ref, f32[16,4096]{1,0:T(8,128)S(1)} %get-tuple-element.14.mine_ref, bf16[128,384]{1,0:T(8,128)(2,1)S(1)} %get-tuple-element.15.filter_ref), custom_call_target="tpu_custom_call" | custom-call | tf_op jit(solution)/shard_map/owner/pallas_call | solution.py:263
  (2 shorter events, 0.0 us)
Async XLA Ops:
  0.6 58.0 %copy-start = (s32[1,8,16,256]{3,2,1,0:T(8,128)S(1)}, s32[1,8,16,256]{3,2,1,0:T(8,128)}, u32[]{:S(2)}) copy-start(s32[1,8,16,256]{3,2,1,0:T(8,128)} %param.13) | copy-start | bytes 393220
  0.6 1.5 %copy-start.5 = (s32[8,16384]{1,0:T(8,128)S(1)}, s32[8,16384]{1,0:T(8,128)}, u32[]{:S(2)}) copy-start(s32[8,16384]{1,0:T(8,128)} %param.9) | copy-start | bytes 1572868
  0.7 5.3 %copy-start.1 = (f32[16384]{0:T(1024)S(1)}, f32[16384]{0:T(1024)}, u32[]{:S(2)}) copy-start(f32[16384]{0:T(1024)} %param.10) | copy-start | bytes 196612
  2.0 3.9 %collective-permute-start = (f32[24,18560]{1,0:T(8,128)S(1)}, f32[24,18560]{1,0:T(8,128)}, u32[]{:S(2)}, u32[]{:S(2)}) collective-permute-start(f32[24,18560]{1,0:T(8,128)S(1)} %pad_convert_fusion.own_ref), channel_id=1, source_target_pairs={{0,16},{16,0},{32,48},{48,32},{64,80},{80,64},{96,112},{112,96},{1... | collective-permute-start | bytes 5345288 | tf_op jit(solution)/shard_map/ppermute | solution.py:214
  50.6 0.6 copy-start.2
  51.2 14.8 %all-to-all-start = ((f32[32,1,64]{2,1,0:T(1,128)}), f32[32,1,64]{2,1,0:T(1,128)S(1)}, u32[]{:S(2)}, u32[]{:S(2)}) async-start(f32[32,1,64]{2,1,0:T(1,128)} %bitcast.28), calls=%async_computation | async-start | bytes 32768 | tf_op jit(solution)/shard_map/all_to_all | solution.py:234
  68.7 18.2 %all-to-all-start.1 = ((f32[64,8,128]{2,1,0:T(8,128)}), f32[64,8,128]{2,1,0:T(8,128)S(1)}, u32[]{:S(2)}, u32[]{:S(2)}) async-start(f32[64,8,128]{2,1,0:T(8,128)} %send.1), calls=%async_computation.1 | async-start | bytes 524288 | tf_op jit(solution)/shard_map/all_to_all | solution.py:260
  76.3 0.8 copy-start.3
  77.1 0.7 copy-start.4

commit v9 on v8

--- a/solution.py
+++ b/solution.py
@@ -14,7 +14,7 @@
 LANES = 128
 BLOCK = 2048
 FILL = 29
-UNROLL = 128
+UNROLL = 256
 ROWS = 16
 F32 = jnp.float32
 BF16 = jnp.bfloat16
@@ -136,7 +136,7 @@
         total = jnp.sum(energy, axis=0, keepdims=True) / 64.0
         tilted = jnp.sum(column * energy, axis=0, keepdims=True) / 64.0
         slope = -penalty * rho * rho
-        both = [f[:, h * LANES : (h + 1) * LANES] for f in (slope * total, slope * tilted, total) for h in range(16)]
+        both = [f.reshape(16, LANES) for f in (slope * total, slope * tilted, total)]
         table = jnp.concatenate(split(jnp.concatenate(both, axis=0)), axis=0)
         for d in range(dests):
             pick = picks_ref[q, d : d + 1, :]

time: 88.9 us -> 88.6 us (level)
  no operation moved by 1% of the time
where the time goes in v9:
time: 88.6 us; the launch traced here: 88.2 us
  Pallas kernels  48.9 us (55%)
  waiting for transfers between devices  17.7 us (20%)
  starting transfers between devices  15 us (17%)
  local copies, waits for them, and re-layouts  3.13 us (4%)
  other arithmetic  1.36 us (2%)
  matrix products  1.23 us (1%)
    pallas_call x1, Pallas kernels, body(): pl.pallas_call(energy_kernel, in_specs=[smem, pl.BlockSpec(memory_space=p...  44.5 us
    all_to_all x1, waiting for transfers between devices, body(): lax.all_to_all(outgoing, ('sample', 'space'), split_axis=0, concat_axis=0...  8.83 us
    all_to_all x1, starting transfers between devices, body(): lax.all_to_all(outgoing, ('sample', 'space'), split_axis=0, concat_axis=0...  7.54 us
    all_to_all x1, starting transfers between devices, body(): lax.all_to_all(mine, ('sample', 'space'), split_axis=0, concat_axis=0, ti...  7.4 us
    all_to_all x1, waiting for transfers between devices, body(): lax.all_to_all(mine, ('sample', 'space'), split_axis=0, concat_axis=0, ti...  6.54 us
    pallas_call x1, Pallas kernels, body(): pl.pallas_call(functools.partial(send_kernel, float(elements * slabs)), i...  2.72 us
    ppermute x1, waiting for transfers between devices, body(): other = lax.ppermute(own, 'sample', [(i, i ^ 1) for i in range(8)])  2.35 us
    unnamed x13, local copies, waits for them, and re-layouts  2.26 us
  transfers between devices with their start and end apart: 3, of which 3 were waited for; matrix products, arithmetic and copies ran while one was open for 3% of the time, Pallas kernels for 0%

profile of v9, /device:TPU:0, one launch (start us, length us, event | category | flops | bytes accessed | tf_op | source)
XLA Modules:
  0.0 88.2 jit_solution(8232484687215214598)
XLA Ops:
  0.6 0.0 copy-start
  0.6 0.0 copy-start.5
  0.7 0.0 copy-start.1
  0.7 1.4 %pad_convert_fusion.own_ref = f32[24,18560]{1,0:T(8,128)S(1)} fusion(bf16[24,18513]{1,0:T(8,128)(2,1)} %bitcast.29), kind=kLoop, calls=%fused_computation.3 | loop fusion | flops 445440 | bytes 2670384 | tf_op jit(solution)/shard_map/jit(_pad)/pad | solution.py:213
  2.0 0.1 collective-permute-start
  2.1 0.0 copy-done.5
  2.1 0.1 copy.15
  2.3 0.1 stack.27.place_ref
  2.4 1.2 %fusion.weight_ref = bf16[512,512]{1,0:T(8,128)(2,1)S(1)} fusion(bf16[24,24]{1,0:T(8,128)(2,1)} %param.11, s32[512]{0:T(512)S(1)} %get-tuple-element.19, s32[512]{0:T(512)S(1)} %get-tuple-element.20), kind=kOutput, calls=%fused_computation.1 | convolution fusion | flops 13996032 | bytes 529536 | tf_op jit(solution)/shard_map/dot_general | solution.py:197
  3.6 2.3 %collective-permute-done.other_ref = f32[24,18560]{1,0:T(8,128)} collective-permute-done((f32[24,18560]{1,0:T(8,128)S(1)}, f32[24,18560]{1,0:T(8,128)}, u32[]{:S(2)}, u32[]{:S(2)}) %collective-permute-start) | collective-permute-done | bytes 1781792 | tf_op jit(solution)/shard_map/ppermute | solution.py:214
  5.9 0.0 copy-done.1
  5.9 44.5 %energy.1 = (f32[4,16,2048]{2,1,0:T(8,128)S(1)}, f32[32,64]{1,0:T(8,128)S(1)}) custom-call(s32[6]{0:T(128)S(1)} %stack.27.place_ref, s32[131072]{0:T(1024)S(1)} %bitcast.24, f32[24,18560]{1,0:T(8,128)S(1)} %pad_convert_fusion.own_ref, f32[24,18560]{1,0:T(8,128)} %collective-permute-done.other_ref, bf16[512,512]{1,0:T(8,128)(2,1)S(1)} %fusion.weight_ref, ...), custom_call_target="tpu_custom_call" | custom-call | tf_op jit(solution)/shard_map/energy/pallas_call | solution.py:222
  50.4 0.0 copy-start.2
  50.4 0.6 copy-done.2
  51.0 7.4 %all-to-all-start = ((f32[32,1,64]{2,1,0:T(1,128)}), f32[32,1,64]{2,1,0:T(1,128)S(1)}, u32[]{:S(2)}, u32[]{:S(2)}) async-start(f32[32,1,64]{2,1,0:T(1,128)} %bitcast.28), calls=%async_computation | async-start | bytes 32768 | tf_op jit(solution)/shard_map/all_to_all | solution.py:234
  58.4 0.0 copy-done
  58.5 0.8 reshape.107.count_ref
  59.2 6.5 %all-to-all-done = f32[32,1,64]{2,1,0:T(1,128)S(1)} async-done(((f32[32,1,64]{2,1,0:T(1,128)}), f32[32,1,64]{2,1,0:T(1,128)S(1)}, u32[]{:S(2)}, u32[]{:S(2)}) %all-to-all-start) | async-done | bytes 8224 | tf_op jit(solution)/shard_map/all_to_all | solution.py:234
  65.8 2.7 %send.1 = f32[64,8,128]{2,1,0:T(8,128)} custom-call(s32[6]{0:T(128)S(1)} %stack.27.place_ref, s32[128]{0:T(128)S(1)} %reshape.107.count_ref, f32[32,64]{1,0:T(8,128)S(1)} %bitcast.27, f32[4,16,2048]{2,1,0:T(8,128)S(1)} %get-tuple-element.12.energy_ref._, f32[8,1,2048]{2,1,0:T(1,128)S(1)} %bitcast.26, s32[4,16,256]{2,1,0:T(8,128)S(1)} %dynamic-slice_bitcast_fusion.picks_ref), custom_call_target="tpu_custom_call" | custom-call | tf_op jit(solution)/shard_map/send/pallas_call | solution.py:251
  68.5 7.5 %all-to-all-start.1 = ((f32[64,8,128]{2,1,0:T(8,128)}), f32[64,8,128]{2,1,0:T(8,128)S(1)}, u32[]{:S(2)}, u32[]{:S(2)}) async-start(f32[64,8,128]{2,1,0:T(8,128)} %send.1), calls=%async_computation.1 | async-start | bytes 524288 | tf_op jit(solution)/shard_map/all_to_all | solution.py:260
  76.1 0.0 copy-start.3
  76.1 0.8 copy-done.3
  76.9 0.0 copy-start.4
  76.9 0.7 copy-done.4
  77.6 0.2 prepare.1
  77.8 8.8 %all-to-all-done.1.got_ref = f32[64,8,128]{2,1,0:T(8,128)S(1)} async-done(((f32[64,8,128]{2,1,0:T(8,128)}), f32[64,8,128]{2,1,0:T(8,128)S(1)}, u32[]{:S(2)}, u32[]{:S(2)}) %all-to-all-start.1) | async-done | bytes 262176 | tf_op jit(solution)/shard_map/all_to_all | solution.py:260
  86.7 1.5 %owner.1 = (f32[1,64]{1,0:T(1,128)}, f32[1,1,2048]{2,1,0:T(1,128)}, f32[1,1,2048]{2,1,0:T(1,128)}) custom-call(f32[64,8,128]{2,1,0:T(8,128)S(1)} %all-to-all-done.1.got_ref, bf16[128,4096]{1,0:T(8,128)(2,1)S(1)} %get-tuple-element.13.hot_ref, f32[16,4096]{1,0:T(8,128)S(1)} %get-tuple-element.14.mine_ref, bf16[128,384]{1,0:T(8,128)(2,1)S(1)} %get-tuple-element.15.filter_ref), custom_call_target="tpu_custom_call" | custom-call | tf_op jit(solution)/shard_map/owner/pallas_call | solution.py:263
  (2 shorter events, 0.0 us)
Async XLA Ops:
  0.6 57.8 %copy-start = (s32[1,8,16,256]{3,2,1,0:T(8,128)S(1)}, s32[1,8,16,256]{3,2,1,0:T(8,128)}, u32[]{:S(2)}) copy-start(s32[1,8,16,256]{3,2,1,0:T(8,128)} %param.13) | copy-start | bytes 393220
  0.6 1.5 %copy-start.5 = (s32[8,16384]{1,0:T(8,128)S(1)}, s32[8,16384]{1,0:T(8,128)}, u32[]{:S(2)}) copy-start(s32[8,16384]{1,0:T(8,128)} %param.9) | copy-start | bytes 1572868
  0.7 5.3 %copy-start.1 = (f32[16384]{0:T(1024)S(1)}, f32[16384]{0:T(1024)}, u32[]{:S(2)}) copy-start(f32[16384]{0:T(1024)} %param.10) | copy-start | bytes 196612
  2.0 3.9 %collective-permute-start = (f32[24,18560]{1,0:T(8,128)S(1)}, f32[24,18560]{1,0:T(8,128)}, u32[]{:S(2)}, u32[]{:S(2)}) collective-permute-start(f32[24,18560]{1,0:T(8,128)S(1)} %pad_convert_fusion.own_ref), channel_id=1, source_target_pairs={{0,16},{16,0},{32,48},{48,32},{64,80},{80,64},{96,112},{112,96},{1... | collective-permute-start | bytes 5345288 | tf_op jit(solution)/shard_map/ppermute | solution.py:214
  50.4 0.6 copy-start.2
  51.0 14.8 %all-to-all-start = ((f32[32,1,64]{2,1,0:T(1,128)}), f32[32,1,64]{2,1,0:T(1,128)S(1)}, u32[]{:S(2)}, u32[]{:S(2)}) async-start(f32[32,1,64]{2,1,0:T(1,128)} %bitcast.28), calls=%async_computation | async-start | bytes 32768 | tf_op jit(solution)/shard_map/all_to_all | solution.py:234
  68.5 18.2 %all-to-all-start.1 = ((f32[64,8,128]{2,1,0:T(8,128)}), f32[64,8,128]{2,1,0:T(8,128)S(1)}, u32[]{:S(2)}, u32[]{:S(2)}) async-start(f32[64,8,128]{2,1,0:T(8,128)} %send.1), calls=%async_computation.1 | async-start | bytes 524288 | tf_op jit(solution)/shard_map/all_to_all | solution.py:260
  76.1 0.8 copy-start.3
  76.9 0.7 copy-start.4

commit v10 on v9

--- a/solution.py
+++ b/solution.py
@@ -111,7 +111,7 @@
         mine_ref[:, at] = jnp.where(high_id == (cell >> 7), 1.0, 0.0)
 
 
-def send_kernel(elements, place_ref, count_ref, parts_ref, energy_ref, density_ref, picks_ref, out_ref):
+def send_kernel(elements, place_ref, count_ref, parts_ref, energy_ref, density_ref, picks_ref, out_hbm, out_ref, sem):
     comp = jnp.sum(parts_ref[...], axis=0, keepdims=True) / elements
     lane = lax.broadcasted_iota(jnp.int32, (1, 64), 1)
     near = jnp.sum(comp, axis=1, keepdims=True) / ROWS
@@ -130,6 +130,7 @@
     one, zero = jnp.ones((LANES, width), BF16), jnp.zeros((LANES, width), BF16)
     high_id = lax.broadcasted_iota(jnp.int32, (16, width), 0)
     slot = lax.broadcasted_iota(jnp.int32, (16, width), 1)
+    copies = []
     for q in range(4):
         energy = energy_ref[q]
         rho = density_ref[place_ref[q]]
@@ -150,6 +151,11 @@
                     r = f * (width // LANES) + p
                     out_ref[q * dests + d, r : r + 1, :] = got[:, p * LANES : (p + 1) * LANES]
             out_ref[q * dests + d, 6:8, :] = facts
+        span = pl.ds(q * dests, dests)
+        copies.append(pltpu.make_async_copy(out_ref.at[span], out_hbm.at[span], sem.at[q]))
+        copies[-1].start()
+    for copy in copies:
+        copy.wait()
 
 
 def owner_kernel(got_ref, hot_ref, mine_ref, filter_ref, comp_ref, sens_ref, energy_ref):
@@ -251,8 +257,9 @@
     outgoing = pl.pallas_call(
         functools.partial(send_kernel, float(elements * slabs)),
         in_specs=[smem, smem] + [whole] * 4,
-        out_specs=whole,
+        out_specs=pl.BlockSpec(memory_space=pltpu.HBM),
         out_shape=jax.ShapeDtypeStruct((4 * dests, 8, LANES), F32),
+        scratch_shapes=[pltpu.VMEM((4 * dests, 8, LANES), F32), pltpu.SemaphoreType.DMA((4,))],
         compiler_params=small,
         name="send",
     )(place, send_count.reshape(-1), parts, energies, rho, picks)

time: 88.6 us -> 88.6 us (level)
  no operation moved by 1% of the time
where the time goes in v10:
time: 88.6 us; the launch traced here: 88.2 us
  Pallas kernels  48.9 us (55%)
  waiting for transfers between devices  17.7 us (20%)
  starting transfers between devices  15 us (17%)
  local copies, waits for them, and re-layouts  3.13 us (4%)
  other arithmetic  1.36 us (2%)
  matrix products  1.23 us (1%)
    pallas_call x1, Pallas kernels, body(): pl.pallas_call(energy_kernel, in_specs=[smem, pl.BlockSpec(memory_space=p...  44.5 us
    all_to_all x1, waiting for transfers between devices, body(): lax.all_to_all(outgoing, ('sample', 'space'), split_axis=0, concat_axis=0...  8.84 us
    all_to_all x1, starting transfers between devices, body(): lax.all_to_all(outgoing, ('sample', 'space'), split_axis=0, concat_axis=0...  7.56 us
    all_to_all x1, starting transfers between devices, body(): lax.all_to_all(mine, ('sample', 'space'), split_axis=0, concat_axis=0, ti...  7.4 us
    all_to_all x1, waiting for transfers between devices, body(): lax.all_to_all(mine, ('sample', 'space'), split_axis=0, concat_axis=0, ti...  6.54 us
    pallas_call x1, Pallas kernels, body(): pl.pallas_call(functools.partial(send_kernel, float(elements * slabs)), i...  2.66 us
    ppermute x1, waiting for transfers between devices, body(): other = lax.ppermute(own, 'sample', [(i, i ^ 1) for i in range(8)])  2.35 us
    unnamed x13, local copies, waits for them, and re-layouts  2.26 us
  transfers between devices with their start and end apart: 3, of which 3 were waited for; matrix products, arithmetic and copies ran while one was open for 3% of the time, Pallas kernels for 0%

profile of v10, /device:TPU:0, one launch (start us, length us, event | category | flops | bytes accessed | tf_op | source)
XLA Modules:
  0.0 88.2 jit_solution(3267908811712160)
XLA Ops:
  0.6 0.0 copy-start
  0.6 0.0 copy-start.5
  0.7 0.0 copy-start.1
  0.7 1.4 %pad_convert_fusion.own_ref = f32[24,18560]{1,0:T(8,128)S(1)} fusion(bf16[24,18513]{1,0:T(8,128)(2,1)} %bitcast.29), kind=kLoop, calls=%fused_computation.3 | loop fusion | flops 445440 | bytes 2670384 | tf_op jit(solution)/shard_map/jit(_pad)/pad | solution.py:219
  2.0 0.1 collective-permute-start
  2.1 0.0 copy-done.5
  2.1 0.1 copy.15
  2.3 0.1 stack.27.place_ref
  2.4 1.2 %fusion.weight_ref = bf16[512,512]{1,0:T(8,128)(2,1)S(1)} fusion(bf16[24,24]{1,0:T(8,128)(2,1)} %param.11, s32[512]{0:T(512)S(1)} %get-tuple-element.19, s32[512]{0:T(512)S(1)} %get-tuple-element.20), kind=kOutput, calls=%fused_computation.1 | convolution fusion | flops 13996032 | bytes 529536 | tf_op jit(solution)/shard_map/dot_general | solution.py:203
  3.6 2.3 %collective-permute-done.other_ref = f32[24,18560]{1,0:T(8,128)} collective-permute-done((f32[24,18560]{1,0:T(8,128)S(1)}, f32[24,18560]{1,0:T(8,128)}, u32[]{:S(2)}, u32[]{:S(2)}) %collective-permute-start) | collective-permute-done | bytes 1781792 | tf_op jit(solution)/shard_map/ppermute | solution.py:220
  5.9 0.0 copy-done.1
  5.9 44.5 %energy.1 = (f32[4,16,2048]{2,1,0:T(8,128)S(1)}, f32[32,64]{1,0:T(8,128)S(1)}) custom-call(s32[6]{0:T(128)S(1)} %stack.27.place_ref, s32[131072]{0:T(1024)S(1)} %bitcast.24, f32[24,18560]{1,0:T(8,128)S(1)} %pad_convert_fusion.own_ref, f32[24,18560]{1,0:T(8,128)} %collective-permute-done.other_ref, bf16[512,512]{1,0:T(8,128)(2,1)S(1)} %fusion.weight_ref, ...), custom_call_target="tpu_custom_call" | custom-call | tf_op jit(solution)/shard_map/energy/pallas_call | solution.py:228
  50.4 0.0 copy-start.2
  50.4 0.6 copy-done.2
  51.0 7.4 %all-to-all-start = ((f32[32,1,64]{2,1,0:T(1,128)}), f32[32,1,64]{2,1,0:T(1,128)S(1)}, u32[]{:S(2)}, u32[]{:S(2)}) async-start(f32[32,1,64]{2,1,0:T(1,128)} %bitcast.28), calls=%async_computation | async-start | bytes 32768 | tf_op jit(solution)/shard_map/all_to_all | solution.py:240
  58.4 0.0 copy-done
  58.5 0.8 reshape.107.count_ref
  59.2 6.5 %all-to-all-done = f32[32,1,64]{2,1,0:T(1,128)S(1)} async-done(((f32[32,1,64]{2,1,0:T(1,128)}), f32[32,1,64]{2,1,0:T(1,128)S(1)}, u32[]{:S(2)}, u32[]{:S(2)}) %all-to-all-start) | async-done | bytes 8224 | tf_op jit(solution)/shard_map/all_to_all | solution.py:240
  65.8 2.7 %send.1 = f32[64,8,128]{2,1,0:T(8,128)} custom-call(s32[6]{0:T(128)S(1)} %stack.27.place_ref, s32[128]{0:T(128)S(1)} %reshape.107.count_ref, f32[32,64]{1,0:T(8,128)S(1)} %bitcast.27, f32[4,16,2048]{2,1,0:T(8,128)S(1)} %get-tuple-element.12.energy_ref._, f32[8,1,2048]{2,1,0:T(1,128)S(1)} %bitcast.26, s32[4,16,256]{2,1,0:T(8,128)S(1)} %dynamic-slice_bitcast_fusion.picks_ref), custom_call_target="tpu_custom_call" | custom-call | tf_op jit(solution)/shard_map/send/pallas_call | solution.py:257
  68.4 7.6 %all-to-all-start.1 = ((f32[64,8,128]{2,1,0:T(8,128)}), f32[64,8,128]{2,1,0:T(8,128)S(1)}, u32[]{:S(2)}, u32[]{:S(2)}) async-start(f32[64,8,128]{2,1,0:T(8,128)} %send.1), calls=%async_computation.1 | async-start | bytes 524288 | tf_op jit(solution)/shard_map/all_to_all | solution.py:267
  76.0 0.0 copy-start.3
  76.0 0.8 copy-done.3
  76.9 0.0 copy-start.4
  76.9 0.7 copy-done.4
  77.6 0.2 prepare.1
  77.8 8.8 %all-to-all-done.1.got_ref = f32[64,8,128]{2,1,0:T(8,128)S(1)} async-done(((f32[64,8,128]{2,1,0:T(8,128)}), f32[64,8,128]{2,1,0:T(8,128)S(1)}, u32[]{:S(2)}, u32[]{:S(2)}) %all-to-all-start.1) | async-done | bytes 262176 | tf_op jit(solution)/shard_map/all_to_all | solution.py:267
  86.6 1.5 %owner.1 = (f32[1,64]{1,0:T(1,128)}, f32[1,1,2048]{2,1,0:T(1,128)}, f32[1,1,2048]{2,1,0:T(1,128)}) custom-call(f32[64,8,128]{2,1,0:T(8,128)S(1)} %all-to-all-done.1.got_ref, bf16[128,4096]{1,0:T(8,128)(2,1)S(1)} %get-tuple-element.13.hot_ref, f32[16,4096]{1,0:T(8,128)S(1)} %get-tuple-element.14.mine_ref, bf16[128,384]{1,0:T(8,128)(2,1)S(1)} %get-tuple-element.15.filter_ref), custom_call_target="tpu_custom_call" | custom-call | tf_op jit(solution)/shard_map/owner/pallas_call | solution.py:270
  (2 shorter events, 0.0 us)
Async XLA Ops:
  0.6 57.8 %copy-start = (s32[1,8,16,256]{3,2,1,0:T(8,128)S(1)}, s32[1,8,16,256]{3,2,1,0:T(8,128)}, u32[]{:S(2)}) copy-start(s32[1,8,16,256]{3,2,1,0:T(8,128)} %param.13) | copy-start | bytes 393220
  0.6 1.5 %copy-start.5 = (s32[8,16384]{1,0:T(8,128)S(1)}, s32[8,16384]{1,0:T(8,128)}, u32[]{:S(2)}) copy-start(s32[8,16384]{1,0:T(8,128)} %param.9) | copy-start | bytes 1572868
  0.7 5.3 %copy-start.1 = (f32[16384]{0:T(1024)S(1)}, f32[16384]{0:T(1024)}, u32[]{:S(2)}) copy-start(f32[16384]{0:T(1024)} %param.10) | copy-start | bytes 196612
  2.0 3.9 %collective-permute-start = (f32[24,18560]{1,0:T(8,128)S(1)}, f32[24,18560]{1,0:T(8,128)}, u32[]{:S(2)}, u32[]{:S(2)}) collective-permute-start(f32[24,18560]{1,0:T(8,128)S(1)} %pad_convert_fusion.own_ref), channel_id=1, source_target_pairs={{0,16},{16,0},{32,48},{48,32},{64,80},{80,64},{96,112},{112,96},{1... | collective-permute-start | bytes 5345288 | tf_op jit(solution)/shard_map/ppermute | solution.py:220
  50.4 0.6 copy-start.2
  51.0 14.8 %all-to-all-start = ((f32[32,1,64]{2,1,0:T(1,128)}), f32[32,1,64]{2,1,0:T(1,128)S(1)}, u32[]{:S(2)}, u32[]{:S(2)}) async-start(f32[32,1,64]{2,1,0:T(1,128)} %bitcast.28), calls=%async_computation | async-start | bytes 32768 | tf_op jit(solution)/shard_map/all_to_all | solution.py:240
  68.4 18.2 %all-to-all-start.1 = ((f32[64,8,128]{2,1,0:T(8,128)}), f32[64,8,128]{2,1,0:T(8,128)S(1)}, u32[]{:S(2)}, u32[]{:S(2)}) async-start(f32[64,8,128]{2,1,0:T(8,128)} %send.1), calls=%async_computation.1 | async-start | bytes 524288 | tf_op jit(solution)/shard_map/all_to_all | solution.py:267
  76.0 0.8 copy-start.3
  76.9 0.7 copy-start.4
